TPU v7x, 32 devices: a whole 2x2x4 slice. The times are simulated.
32 devices in a mesh: dp: 2 (over core), expert: 16 (over z, y, x).
Axes of the slice: x: 2, y: 2, z: 4, core: 2. Of those that a mesh axis runs over, the one named last changes fastest.
Arguments:
- tokens: bfloat16 [8192, 2048], P(('dp', 'expert')), may hold values from -6 to 6
- segments: int32 [32, 256], P(('dp', 'expert')), may hold values from 0 to 7, never falling along the last dimension, each value on 1 to 128 neighbouring positions
- expert_ids: int32 [8192, 8], P(('dp', 'expert')), may hold values from 0 to 15, all different within a row
- norm_gains: float32 [4, 2048], P(None, ('dp', 'expert')), may hold values from 0.1 to 1.9
- w_query: float32 [2048, 2048], P(('dp', 'expert')), may hold values from -0.125 to 0.125
- w_key: float32 [2048, 2048], P(('dp', 'expert')), may hold values from -0.125 to 0.125
- w_value: float32 [2048, 2048], P(('dp', 'expert')), may hold values from -0.125 to 0.125
- w_out: float32 [2048, 2048], P(('dp', 'expert')), may hold values from -1 to 1
- w_router: float32 [2048, 16], P(('dp', 'expert')), may hold values from -0.0625 to 0.0625
- expert_gate: bfloat16 [16, 2048, 1024], P('expert'), may hold values from -0.125 to 0.125
- expert_up: bfloat16 [16, 2048, 1024], P('expert'), may hold values from -0.125 to 0.125
- expert_down: bfloat16 [16, 1024, 2048], P('expert'), may hold values from -3 to 3
- cotangent: bfloat16 [8192, 2048], P(('dp', 'expert')), may hold values from -6 to 6
Outputs:
- mixed: bfloat16 [8192, 2048], P(('dp', 'expert'))
- grad_tokens: bfloat16 [8192, 2048], P(('dp', 'expert'))
- grad_norm_gains: float32 [4, 2048], P(None, ('dp', 'expert'))
- grad_w_query: float32 [2048, 2048], P(('dp', 'expert'))
- grad_w_key: float32 [2048, 2048], P(('dp', 'expert'))
- grad_w_value: float32 [2048, 2048], P(('dp', 'expert'))
- grad_w_out: float32 [2048, 2048], P(('dp', 'expert'))
- grad_w_router: float32 [2048, 16], P(('dp', 'expert'))
- grad_expert_gate: float32 [2, 16, 2048, 1024], P('dp', 'expert')
- grad_expert_up: float32 [2, 16, 2048, 1024], P('dp', 'expert')
- grad_expert_down: float32 [2, 16, 1024, 2048], P('dp', 'expert')
Inputs may be any that keep to these rules, and one draw needn't show every extreme that they name: `expert_ids`: each row names 8 different experts. `segments`: document numbers never fall along a sequence.
All inputs are finite; a program needn't handle non-finite values.
Results may differ from a plain program's by a relative error of at most 0.018.
The roundings to bfloat16 on the way count: a program that leaves them out, or rounds other values in their place, can miss the bound.
Values may be sent and summed in bfloat16 or wider, within the bound.
No kernel may reach another device: no remote copies, remote signals or barrier semaphores. Data moves between devices by JAX's collectives and lax.ppermute only.
A program may use at most 256 MiB of HBM per device.

v0:
```python
import jax
import jax.numpy as jnp
from jax import lax
from jax.sharding import PartitionSpec as P

HD = 128


EPS = 1e-05
THETA = 10000.0
MASKED = -1e30


def norm_rows(value, gain):
    inverse = lax.rsqrt(jnp.mean(value * value, axis=-1, keepdims=True) + EPS)
    normed = value * inverse
    return (normed * gain, normed, inverse)


def norm_back(grad_in, gain, normed, inverse):
    grad_normed = grad_in * gain
    grad_gain = jnp.sum(grad_in * normed, axis=0)
    inner = jnp.mean(grad_normed * normed, axis=-1, keepdims=True)
    return (inverse * (grad_normed - normed * inner), grad_gain)


def rope_tables(length, head):
    half = head // 2
    freq = THETA ** (-(jnp.arange(half, dtype=jnp.float32) * 2.0) / head)
    angle = jnp.arange(length, dtype=jnp.float32)[:, None] * freq[None, :]
    angle = jnp.concatenate([angle, angle], axis=-1)
    return (jnp.cos(angle)[:, None, :], jnp.sin(angle)[:, None, :])


def rotate(value, cosine, sine):
    half = value.shape[-1] // 2
    turned = jnp.concatenate([-value[..., half:], value[..., :half]], axis=-1)
    return value * cosine + turned * sine


def rotate_back(grad_in, cosine, sine):
    half = grad_in.shape[-1] // 2
    part = grad_in * sine
    turned = jnp.concatenate([part[..., half:], -part[..., :half]], axis=-1)
    return grad_in * cosine + turned


def contract_rows(left, right):
    return lax.dot_general(
        left, right, (((0,), (0,)), ((), ())), preferred_element_type=jnp.float32
    )


def contract_cols(left, right):
    return lax.dot_general(
        left, right, (((1,), (1,)), ((), ())), preferred_element_type=jnp.float32
    )


def slot_table(block_ids, experts, capacity):
    labels = jnp.arange(experts, dtype=jnp.int32)
    onehot = (block_ids[:, :, None] == labels[None, None, :]).astype(jnp.int32).reshape(-1, experts)
    before = jnp.cumsum(onehot, axis=0) - onehot
    position = jnp.sum(before * onehot, axis=1).reshape(block_ids.shape)
    return jnp.where(position < capacity, block_ids * capacity + position, -1)


def expert_pass(received, gate_w, up_w, down_w):
    local = gate_w.shape[0]
    grouped = received.reshape(-1, local, received.shape[1], received.shape[2])
    pre_gate = jnp.einsum("slkd,ldf->slkf", grouped, gate_w, preferred_element_type=jnp.float32)
    pre_up = jnp.einsum("slkd,ldf->slkf", grouped, up_w, preferred_element_type=jnp.float32)
    activated = (jax.nn.silu(pre_gate) * pre_up).astype(jnp.bfloat16)
    result = jnp.einsum("slkf,lfd->slkd", activated, down_w, preferred_element_type=jnp.float32)
    return (result.astype(jnp.bfloat16).reshape(received.shape), pre_gate, pre_up)


def on_device(
    tokens,
    segments,
    expert_ids,
    norm_gains,
    w_query,
    w_key,
    w_value,
    w_out,
    w_router,
    expert_gate,
    expert_up,
    expert_down,
    cotangent,
):
    bfloat = jnp.bfloat16
    length, width = tokens.shape
    topk = expert_ids.shape[1]
    local = expert_gate.shape[0]
    hidden = expert_gate.shape[2]
    experts = lax.axis_size("expert") * local
    capacity = length * topk // experts
    heads = width // HD
    gains, wq, wk, wv, wo, wr = (
        lax.all_gather(norm_gains.astype(bfloat), ("dp", "expert"), axis=1, tiled=True),
        lax.all_gather(w_query.astype(bfloat), ("dp", "expert"), axis=0, tiled=True),
        lax.all_gather(w_key.astype(bfloat), ("dp", "expert"), axis=0, tiled=True),
        lax.all_gather(w_value.astype(bfloat), ("dp", "expert"), axis=0, tiled=True),
        lax.all_gather(w_out.astype(bfloat), ("dp", "expert"), axis=0, tiled=True),
        lax.all_gather(w_router.astype(bfloat), ("dp", "expert"), axis=0, tiled=True),
    )
    gains_f = gains.astype(jnp.float32)
    inputs = tokens.astype(jnp.float32)
    normed_in_f, normed_one, inverse_one = norm_rows(inputs, gains_f[0])
    normed_in = normed_in_f.astype(bfloat)
    query_raw = jnp.dot(normed_in, wq, preferred_element_type=jnp.float32)
    key_raw = jnp.dot(normed_in, wk, preferred_element_type=jnp.float32)
    values = jnp.dot(normed_in, wv, preferred_element_type=jnp.float32).astype(bfloat)
    query_n, query_normed, query_inverse = norm_rows(query_raw, gains_f[1])
    key_n, key_normed, key_inverse = norm_rows(key_raw, gains_f[2])
    cosine, sine = rope_tables(length, HD)
    query_rot = rotate(query_n.reshape(length, heads, HD), cosine, sine).astype(bfloat)
    key_rot = rotate(key_n.reshape(length, heads, HD), cosine, sine).astype(bfloat)
    value_heads = values.reshape(length, heads, HD)
    doc_ids = segments[0]
    places = jnp.arange(length, dtype=jnp.int32)
    visible = (doc_ids[:, None] == doc_ids[None, :]) & (places[:, None] >= places[None, :])
    score_scale = HD ** (-0.5)
    scores = (
        jnp.einsum("qhd,khd->hqk", query_rot, key_rot, preferred_element_type=jnp.float32)
        * score_scale
    )
    scores = jnp.where(visible[None], scores, MASKED)
    row_max = jnp.max(scores, axis=-1, keepdims=True)
    expo = jnp.exp(scores - row_max)
    totals = jnp.sum(expo, axis=-1, keepdims=True)
    log_total = row_max + jnp.log(totals)
    weights = (expo / totals).astype(bfloat)
    attended = (
        jnp.einsum("hqk,khd->qhd", weights, value_heads, preferred_element_type=jnp.float32)
        .reshape(length, width)
        .astype(bfloat)
    )
    residual = inputs + jnp.dot(attended, wo, preferred_element_type=jnp.float32)
    normed_mid_f, normed_two, inverse_two = norm_rows(residual, gains_f[3])
    normed_mid = normed_mid_f.astype(bfloat)
    logits = jnp.dot(normed_mid, wr, preferred_element_type=jnp.float32)
    route = jax.nn.softmax(logits, axis=-1)
    expert_mask = expert_ids[:, :, None] == jnp.arange(experts, dtype=jnp.int32)[None, None, :]
    gate_vals = jnp.sum(jnp.where(expert_mask, route[:, None, :], 0.0), axis=-1).astype(bfloat)
    slot_index = slot_table(expert_ids, experts, capacity)
    slot_hit = (
        slot_index[:, :, None] == jnp.arange(experts * capacity, dtype=jnp.int32)[None, None, :]
    )
    combine = jnp.sum(
        jnp.where(slot_hit, gate_vals.astype(jnp.float32)[:, :, None], 0.0), axis=1
    ).astype(bfloat)
    spread = jnp.any(slot_hit, axis=1).astype(bfloat)
    sent = contract_rows(spread, normed_mid).astype(bfloat).reshape(experts, capacity, width)
    received = lax.all_to_all(sent, "expert", split_axis=0, concat_axis=0, tiled=True)
    result, pre_gate, pre_up = expert_pass(received, expert_gate, expert_up, expert_down)
    results = (
        result,
        received,
        pre_gate.reshape(-1, received.shape[1], hidden),
        pre_up.reshape(-1, received.shape[1], hidden),
    )
    returned = lax.all_to_all(results[0], "expert", split_axis=0, concat_axis=0, tiled=True)
    flat_back = returned.reshape(-1, width)
    moe = jnp.dot(combine, flat_back, preferred_element_type=jnp.float32)
    mixed = (residual + moe).astype(bfloat)
    grad_out = cotangent.astype(jnp.float32)
    grad_rows_y = contract_rows(combine, cotangent).astype(bfloat).reshape(experts, capacity, width)
    grad_comb = contract_cols(cotangent, flat_back)
    grad_gate = jnp.sum(jnp.where(slot_hit, grad_comb[:, None, :], 0.0), axis=-1)
    arrived_grad = lax.all_to_all(grad_rows_y, "expert", split_axis=0, concat_axis=0, tiled=True)
    arrived = results[1]
    grouped_in = arrived.reshape(-1, local, capacity, width)
    grouped_grad = arrived_grad.reshape(-1, local, capacity, width)
    pre_gate = results[2].reshape(-1, local, capacity, hidden)
    pre_up = results[3].reshape(-1, local, capacity, hidden)
    sigmoid_g = jax.nn.sigmoid(pre_gate)
    silu_g = pre_gate * sigmoid_g
    activated = (silu_g * pre_up).astype(bfloat)
    grad_act = jnp.einsum(
        "slkd,lfd->slkf", grouped_grad, expert_down, preferred_element_type=jnp.float32
    )
    grad_pre_gate = (grad_act * pre_up * (sigmoid_g * (1.0 + pre_gate * (1.0 - sigmoid_g)))).astype(
        bfloat
    )
    grad_pre_up = (grad_act * silu_g).astype(bfloat)
    grad_down = jnp.einsum(
        "slkf,slkd->lfd", activated, grouped_grad, preferred_element_type=jnp.float32
    )
    grad_gate_w = jnp.einsum(
        "slkd,slkf->ldf", grouped_in, grad_pre_gate, preferred_element_type=jnp.float32
    )
    grad_up_w = jnp.einsum(
        "slkd,slkf->ldf", grouped_in, grad_pre_up, preferred_element_type=jnp.float32
    )
    grad_sent = jnp.einsum(
        "slkf,ldf->slkd", grad_pre_gate, expert_gate, preferred_element_type=jnp.float32
    )
    grad_sent = grad_sent + jnp.einsum(
        "slkf,ldf->slkd", grad_pre_up, expert_up, preferred_element_type=jnp.float32
    )
    grad_sent = grad_sent.astype(bfloat).reshape(experts, capacity, width)
    grad_back = lax.all_to_all(grad_sent, "expert", split_axis=0, concat_axis=0, tiled=True)
    grad_mid = jnp.dot(spread, grad_back.reshape(-1, width), preferred_element_type=jnp.float32)
    grad_route = jnp.sum(jnp.where(expert_mask, grad_gate[:, :, None], 0.0), axis=1)
    grad_logits = (
        route * (grad_route - jnp.sum(route * grad_route, axis=-1, keepdims=True))
    ).astype(bfloat)
    grad_router = contract_rows(normed_mid, grad_logits)
    grad_mid = grad_mid + contract_cols(grad_logits, wr)
    grad_res_two, grad_gain_mid = norm_back(grad_mid, gains_f[3], normed_two, inverse_two)
    grad_residual = grad_out + grad_res_two
    grad_attn = grad_residual.astype(bfloat)
    grad_wo = contract_rows(attended, grad_attn)
    grad_attended = contract_cols(grad_attn, wo).astype(bfloat).reshape(length, heads, HD)
    scores_again = (
        jnp.einsum("qhd,khd->hqk", query_rot, key_rot, preferred_element_type=jnp.float32)
        * score_scale
    )
    scores_again = jnp.where(visible[None], scores_again, MASKED)
    probs_again = jnp.exp(scores_again - log_total)
    grad_probs = jnp.einsum(
        "qhd,khd->hqk", grad_attended, value_heads, preferred_element_type=jnp.float32
    )
    grad_values = jnp.einsum(
        "hqk,qhd->khd",
        probs_again.astype(bfloat),
        grad_attended,
        preferred_element_type=jnp.float32,
    )
    grad_values = grad_values.reshape(length, width).astype(bfloat)
    inner = jnp.sum(probs_again * grad_probs, axis=-1, keepdims=True)
    grad_scores = (probs_again * (grad_probs - inner)).astype(bfloat)
    grad_query_rot = (
        jnp.einsum("hqk,khd->qhd", grad_scores, key_rot, preferred_element_type=jnp.float32)
        * score_scale
    )
    grad_key_rot = (
        jnp.einsum("hqk,qhd->khd", grad_scores, query_rot, preferred_element_type=jnp.float32)
        * score_scale
    )
    grad_query_n = rotate_back(grad_query_rot, cosine, sine).reshape(length, width)
    grad_key_n = rotate_back(grad_key_rot, cosine, sine).reshape(length, width)
    grad_query_f, grad_gain_query = norm_back(grad_query_n, gains_f[1], query_normed, query_inverse)
    grad_key_f, grad_gain_key = norm_back(grad_key_n, gains_f[2], key_normed, key_inverse)
    grad_query = grad_query_f.astype(bfloat)
    grad_key = grad_key_f.astype(bfloat)
    grad_wq = contract_rows(normed_in, grad_query)
    grad_wk = contract_rows(normed_in, grad_key)
    grad_wv = contract_rows(normed_in, grad_values)
    grad_in_norm = (
        contract_cols(grad_query, wq) + contract_cols(grad_key, wk) + contract_cols(grad_values, wv)
    )
    grad_res_one, grad_gain_in = norm_back(grad_in_norm, gains_f[0], normed_one, inverse_one)
    grad_tokens = (grad_residual + grad_res_one).astype(bfloat)
    grad_gains = jnp.stack([grad_gain_in, grad_gain_query, grad_gain_key, grad_gain_mid], axis=0)
    shares = (
        lax.psum_scatter(grad_gains, ("dp", "expert"), scatter_dimension=1, tiled=True),
        lax.psum_scatter(grad_wq, ("dp", "expert"), scatter_dimension=0, tiled=True),
        lax.psum_scatter(grad_wk, ("dp", "expert"), scatter_dimension=0, tiled=True),
        lax.psum_scatter(grad_wv, ("dp", "expert"), scatter_dimension=0, tiled=True),
        lax.psum_scatter(grad_wo, ("dp", "expert"), scatter_dimension=0, tiled=True),
        lax.psum_scatter(grad_router, ("dp", "expert"), scatter_dimension=0, tiled=True),
    )
    return (
        mixed,
        grad_tokens,
        shares[0],
        shares[1],
        shares[2],
        shares[3],
        shares[4],
        shares[5],
        grad_gate_w[None],
        grad_up_w[None],
        grad_down[None],
    )


def solution(mesh):
    return jax.shard_map(
        on_device,
        mesh=mesh,
        in_specs=(
            P(("dp", "expert"), None),
            P(("dp", "expert"), None),
            P(("dp", "expert"), None),
            P(None, ("dp", "expert")),
            P(("dp", "expert"), None),
            P(("dp", "expert"), None),
            P(("dp", "expert"), None),
            P(("dp", "expert"), None),
            P(("dp", "expert"), None),
            P("expert", None, None),
            P("expert", None, None),
            P("expert", None, None),
            P(("dp", "expert"), None),
        ),
        out_specs=(
            P(("dp", "expert"), None),
            P(("dp", "expert"), None),
            P(None, ("dp", "expert")),
            P(("dp", "expert"), None),
            P(("dp", "expert"), None),
            P(("dp", "expert"), None),
            P(("dp", "expert"), None),
            P(("dp", "expert"), None),
            P("dp", "expert", None, None),
            P("dp", "expert", None, None),
            P("dp", "expert", None, None),
        ),
        check_vma=False,
    )
```

profile of v0, /device:TPU:9, one launch (start us, length us, event | category | flops | bytes accessed | tf_op | source)
XLA Modules:
  0.0 2921.4 jit_solution(10196357463042990690)
XLA Ops:
  13.0 62.3 %all-gather = bf16[32,64,4]{1,2,0:T(4,128)(2,1)S(1)} all-gather(bf16[1,64,4]{1,2,0:T(4,128)(2,1)S(1)} %convert_bitcast_fusion.1), channel_id=1, replica_groups=mesh['dp'=2,'expert'=16] {'dp','expert'}, dimensions={0}, use_global_device_ids=true | all-gather | bytes 16896 | tf_op jit(solution)/shard_map/all_gather | solution.py:102
  83.3 10.6 fusion
  105.4 65.2 %all-gather.9.cloned.1.call-done = bf16[2048,2048]{1,0:T(8,128)(2,1)} async-done(((bf16[64,2048]{1,0:T(8,128)(2,1)}), bf16[2048,2048]{1,0:T(8,128)(2,1)}) %all-gather.9.cloned.1.call-update) | async-done | bytes 8388624 | tf_op jit(solution)/shard_map/all_gather | solution.py:103
  189.5 60.7 %all-gather.7.cloned.1.call-done = bf16[2048,2048]{1,0:T(8,128)(2,1)} async-done(((bf16[64,2048]{1,0:T(8,128)(2,1)}), bf16[2048,2048]{1,0:T(8,128)(2,1)}) %all-gather.7.cloned.1.call-update) | async-done | bytes 8388624 | tf_op jit(solution)/shard_map/all_gather | solution.py:105
  257.2 72.5 %all-gather.13.cloned.1.call-done = bf16[2048,2048]{1,0:T(8,128)(2,1)} async-done(((bf16[64,2048]{1,0:T(8,128)(2,1)}), bf16[2048,2048]{1,0:T(8,128)(2,1)}) %all-gather.13.cloned.1.call-update) | async-done | bytes 8388624 | tf_op jit(solution)/shard_map/all_gather | solution.py:106
  339.6 186.8 %all_to_all.20 = bf16[16,128,2048]{2,1,0:T(8,128)(2,1)S(1)} all-to-all(bf16[16,128,2048]{2,1,0:T(8,128)(2,1)S(1)} %bitcast.222), channel_id=1, replica_groups=mesh['dp'=2,'expert'=16] {'expert'}, dimensions={0} | all-to-all | bytes 16777216 | tf_op jit(solution)/shard_map/all_to_all | solution.py:157
  526.4 9.3 fusion.19
  535.7 11.1 fusion.22
  554.1 11.3 convolution_convert_fusion.2
  570.2 228.9 %all-gather.1 = bf16[32,64,16]{1,2,0:T(8,128)(2,1)S(1)} all-gather(bf16[1,64,16]{1,2,0:T(8,128)(2,1)S(1)} %convert_bitcast_fusion), channel_id=1, replica_groups=mesh['dp'=2,'expert'=16] {'dp','expert'}, dimensions={0}, use_global_device_ids=true | all-gather | bytes 67584 | tf_op jit(solution)/shard_map/all_gather | solution.py:107
  800.6 7.1 convolution_bitcast_fusion.3
  809.6 8.2 select_reduce_fusion
  820.2 193.8 %all_to_all.21 = bf16[16,128,2048]{2,1,0:T(8,128)(2,1)} all-to-all(bf16[16,128,2048]{2,1,0:T(8,128)(2,1)S(1)} %bitcast.223), channel_id=1, replica_groups=mesh['dp'=2,'expert'=16] {'expert'}, dimensions={0} | all-to-all | bytes 16777216 | tf_op jit(solution)/shard_map/all_to_all | solution.py:173
  1014.0 20.7 fusion.11
  1034.7 15.3 fusion.13
  1050.1 16.0 add_convert_fusion
  1072.8 182.8 %all-to-all-done.3 = bf16[16,128,2048]{2,1,0:T(8,128)(2,1)} async-done(((bf16[16,128,2048]{2,1,0:T(8,128)(2,1)}), bf16[16,128,2048]{2,1,0:T(8,128)(2,1)}, u32[]{:S(2)}, u32[]{:S(2)}) %all-to-all-start.3) | async-done | bytes 8388640 | tf_op jit(solution)/shard_map/all_to_all | solution.py:205
  1264.7 6.7 convolution_convert_fusion.3
  1298.6 7.8 fusion.91
  1316.4 10.0 fusion.57
  1326.7 9.5 fusion.71
  1336.2 9.5 fusion.73
  1345.8 9.5 fusion.75
  1355.3 7.0 fusion.30
  1363.7 15.0 convolution_bitcast_fusion.1
  1378.7 13.7 convolution_bitcast_fusion.2
  1392.5 11.8 convolution_bitcast_fusion
  1405.9 55.4 %reduce-scatter.19.cloned.1.call-done = f32[64,4]{1,0:T(8,128)} async-done(((f32[2048,4]{1,0:T(8,128)}), f32[64,4]{1,0:T(8,128)}) %reduce-scatter.19.cloned.1.call-update) | async-done | bytes 1040
  1462.7 362.9 %reduce-scatter.17.cloned.1.call-done = f32[64,2048]{1,0:T(8,128)} async-done(((f32[2048,2048]{1,0:T(8,128)}), f32[64,2048]{1,0:T(8,128)}) %reduce-scatter.17.cloned.1.call-update) | async-done | bytes 524304 | tf_op jit(solution)/shard_map/reduce_scatter | solution.py:264
  1825.7 362.9 %reduce-scatter.15.cloned.1.call-done = f32[64,2048]{1,0:T(8,128)} async-done(((f32[2048,2048]{1,0:T(8,128)}), f32[64,2048]{1,0:T(8,128)}) %reduce-scatter.15.cloned.1.call-update) | async-done | bytes 524304 | tf_op jit(solution)/shard_map/reduce_scatter | solution.py:263
  2188.6 362.9 %reduce-scatter.13.cloned.1.call-done = f32[64,2048]{1,0:T(8,128)} async-done(((f32[2048,2048]{1,0:T(8,128)}), f32[64,2048]{1,0:T(8,128)}) %reduce-scatter.13.cloned.1.call-update) | async-done | bytes 524304 | tf_op jit(solution)/shard_map/reduce_scatter | solution.py:262
  2551.5 362.8 %reduce-scatter.11.cloned.1.call-done = f32[64,2048]{1,0:T(8,128)} async-done(((f32[2048,2048]{1,0:T(8,128)}), f32[64,2048]{1,0:T(8,128)}) %reduce-scatter.11.cloned.1.call-update) | async-done | bytes 524304 | tf_op jit(solution)/shard_map/reduce_scatter | solution.py:261
  (279 shorter events, 135.9 us)
Async XLA Ops:
  7.2 87.3 %all-gather.11.cloned.1.call-start = ((), (), s32[]{:S(2)}) async-start(), calls=%async_computation.12 | async-start | bytes 8650752 | tf_op jit(solution)/shard_map/all_gather | solution.py:104
  9.1 161.5 %all-gather.9.cloned.1.call-start = ((), (), s32[]{:S(2)}) async-start(), calls=%async_computation.11 | async-start | bytes 8650752 | tf_op jit(solution)/shard_map/all_gather | solution.py:103
  11.0 239.3 %all-gather.7.cloned.1.call-start = ((), (), s32[]{:S(2)}) async-start(), calls=%async_computation.10 | async-start | bytes 8650752 | tf_op jit(solution)/shard_map/all_gather | solution.py:105
  11.8 70.5 %copy-start.3 = (bf16[256,2048]{1,0:T(8,128)(2,1)S(1)}, bf16[256,2048]{1,0:T(8,128)(2,1)}, u32[]{:S(2)}) copy-start(bf16[256,2048]{1,0:T(8,128)(2,1)} %param.13) | copy-start | bytes 3145732
  11.8 317.9 %all-gather.13.cloned.1.call-start = ((), (), s32[]{:S(2)}) async-start(), calls=%async_computation.13 | async-start | bytes 8650752 | tf_op jit(solution)/shard_map/all_gather | solution.py:106
  12.6 69.9 %copy-start.66 = (s32[1,256]{1,0:T(1,128)S(1)}, s32[1,256]{1,0:T(1,128)}, u32[]{:S(2)}) copy-start(s32[1,256]{1,0:T(1,128)} %param.14) | copy-start | bytes 3076
  82.5 18.0 copy-start.54
  94.5 82.0 %copy-start.48 = (f32[1,2048]{1,0:T(1,128)}, f32[1,2048]{1,0:T(1,128)S(1)}, u32[]{:S(2)}) copy-start(f32[1,2048]{1,0:T(1,128)S(1)} %get-tuple-element.43) | copy-start | bytes 24580
  94.5 155.8 %copy-start.41 = (f32[1,2048]{1,0:T(1,128)}, f32[1,2048]{1,0:T(1,128)S(1)}, u32[]{:S(2)}) copy-start(f32[1,2048]{1,0:T(1,128)S(1)} %get-tuple-element.44) | copy-start | bytes 24580
  186.9 69.3 %copy-start.44 = (f32[16,256]{1,0:T(8,128)}, f32[16,256]{1,0:T(8,128)S(1)}, u32[]{:S(2)}) copy-start(f32[16,256]{1,0:T(8,128)S(1)} %get-tuple-element.49) | copy-start | bytes 49156
  188.9 61.3 %copy-start.55 = (f32[256]{0:T(256)S(1)}, f32[256]{0:T(256)}, u32[]{:S(2)}) copy-start(f32[256]{0:T(256)} %copy-done.54) | copy-start | bytes 3076
  189.5 66.7 %copy-start.57 = (f32[16,256]{1,0:T(8,128)}, f32[16,256]{1,0:T(8,128)S(1)}, u32[]{:S(2)}) copy-start(f32[16,256]{1,0:T(8,128)S(1)} %fusion.24) | copy-start | bytes 49156
  257.2 78.3 %copy-start.22 = (bf16[16,128,256]{2,1,0:T(8,128)(2,1)}, bf16[16,128,256]{2,1,0:T(8,128)(2,1)S(1)}, u32[]{:S(2)}) copy-start(bf16[16,128,256]{2,1,0:T(8,128)(2,1)S(1)} %fusion.47) | copy-start | bytes 3145732
  339.6 186.8 %copy-start.71 = (bf16[1,2048,1024]{2,1,0:T(8,128)(2,1)S(1)}, bf16[1,2048,1024]{2,1,0:T(8,128)(2,1)}, u32[]{:S(2)}) copy-start(bf16[1,2048,1024]{2,1,0:T(8,128)(2,1)} %param.23) | copy-start | bytes 12582916
  565.3 234.4 %copy-start.53 = (s32[256,8]{0,1:T(8,128)S(1)}, s32[256,8]{0,1:T(8,128)}, u32[]{:S(2)}) copy-start(s32[256,8]{0,1:T(8,128)} %param.15) | copy-start | bytes 24580
  565.3 235.2 %copy-start.26 = (bf16[256,2048]{1,0:T(8,128)(2,1)S(1)}, bf16[256,2048]{1,0:T(8,128)(2,1)}, u32[]{:S(2)}) copy-start(bf16[256,2048]{1,0:T(8,128)(2,1)} %param.25) | copy-start | bytes 3145732
  565.3 235.2 %all-to-all-start.1 = ((bf16[16,128,2048]{2,1,0:T(8,128)(2,1)}), bf16[16,128,2048]{2,1,0:T(8,128)(2,1)}, u32[]{:S(2)}, u32[]{:S(2)}) async-start(bf16[16,128,2048]{2,1,0:T(8,128)(2,1)} %convolution_convert_fusion.2), calls=%async_computation.1 | async-start | bytes 16777216 | tf_op jit(solution)/shard_map/all_to_all | solution.py:165
  820.2 193.8 %copy-start.69 = (bf16[1,1024,2048]{2,1,0:T(8,128)(2,1)S(1)}, bf16[1,1024,2048]{2,1,0:T(8,128)(2,1)}, u32[]{:S(2)}) copy-start(bf16[1,1024,2048]{2,1,0:T(8,128)(2,1)} %param.24) | copy-start | bytes 12582916
  1034.7 15.3 copy-start.72
  1066.1 189.5 %all-to-all-start.3 = ((bf16[16,128,2048]{2,1,0:T(8,128)(2,1)}), bf16[16,128,2048]{2,1,0:T(8,128)(2,1)}, u32[]{:S(2)}, u32[]{:S(2)}) async-start(bf16[16,128,2048]{2,1,0:T(8,128)(2,1)} %add_convert_fusion), calls=%async_computation.3 | async-start | bytes 16777216 | tf_op jit(solution)/shard_map/all_to_all | solution.py:205
  1070.9 184.7 %copy-start.33 = (pred[256,2048]{1,0:T(8,128)(4,1)S(1)}, pred[256,2048]{1,0:T(8,128)(4,1)}, u32[]{:S(2)}) copy-start(pred[256,2048]{1,0:T(8,128)(4,1)} %fusion) | copy-start | bytes 1572868
  1070.9 291.4 %reduce-scatter.21.cloned.1.call-start = ((), (), s32[]{:S(2)}) async-start(), calls=%async_computation.19 | async-start | bytes 1081344
  1072.7 388.6 %reduce-scatter.19.cloned.1.call-start = ((), (), s32[]{:S(2)}) async-start(), calls=%async_computation.18 | async-start | bytes 1081344
  1298.6 12.1 slice-start.4
  1316.3 509.3 %reduce-scatter.17.cloned.1.call-start = ((), (), s32[]{:S(2)}) async-start(), calls=%async_computation.17 | async-start | bytes 17301504 | tf_op jit(solution)/shard_map/reduce_scatter | solution.py:264
  1326.5 862.1 %reduce-scatter.15.cloned.1.call-start = ((), (), s32[]{:S(2)}) async-start(), calls=%async_computation.16 | async-start | bytes 17301504 | tf_op jit(solution)/shard_map/reduce_scatter | solution.py:263
  1336.2 1215.3 %reduce-scatter.13.cloned.1.call-start = ((), (), s32[]{:S(2)}) async-start(), calls=%async_computation.15 | async-start | bytes 17301504 | tf_op jit(solution)/shard_map/reduce_scatter | solution.py:262
  1345.7 1568.5 %reduce-scatter.11.cloned.1.call-start = ((), (), s32[]{:S(2)}) async-start(), calls=%async_computation.14 | async-start | bytes 17301504 | tf_op jit(solution)/shard_map/reduce_scatter | solution.py:261
  1363.7 15.0 copy-start.73
  1363.7 28.7 slice-start
  1378.7 13.7 slice-start.1
  1378.7 13.7 copy-start.25
  (60 other events, 247.1 us)
Sparse Core Ops, SparseCore 0:
  11.5 79.4 all-gather.10
  94.4 76.1 all-gather.8
  174.1 76.1 all-gather.6
  253.5 76.1 all-gather.12
  1073.7 250.1 reduce-scatter.20
  1326.1 135.1 reduce-scatter.18
  1464.2 361.4 reduce-scatter.16
  1828.5 359.9 reduce-scatter.14
  2191.4 360.0 reduce-scatter.12
  2554.2 360.0 reduce-scatter.10
where the time goes:
time: 2930 us; the launch traced here: 2920 us
  waiting for transfers between devices  1890 us (65%)
  blocking collectives  672 us (23%)
  matrix products  245 us (8%)
  other arithmetic  54.5 us (2%)
  local copies, waits for them, and re-layouts  35.8 us (1%)
    reduce_scatter x1, waiting for transfers between devices, on_device(): lax.psum_scatter(grad_wo, ('dp', 'expert'), scatter_dimension=0, tiled=True)  363 us
    reduce_scatter x1, waiting for transfers between devices, on_device(): lax.psum_scatter(grad_wk, ('dp', 'expert'), scatter_dimension=0, tiled=True)  363 us
    reduce_scatter x1, waiting for transfers between devices, on_device(): lax.psum_scatter(grad_wv, ('dp', 'expert'), scatter_dimension=0, tiled=True)  363 us
    reduce_scatter x1, waiting for transfers between devices, on_device(): lax.psum_scatter(grad_wq, ('dp', 'expert'), scatter_dimension=0, tiled=True)  363 us
    all_gather x1, blocking collectives, on_device(): lax.all_gather(w_router.astype(bfloat), ('dp', 'expert'), axis=0, tiled=T...  229 us
    all_to_all x1, blocking collectives, on_device(): lax.all_to_all(grad_rows_y, 'expert', split_axis=0, concat_axis=0, tiled=...  194 us
    all_to_all x1, blocking collectives, on_device(): lax.all_to_all(sent, 'expert', split_axis=0, concat_axis=0, tiled=True)  187 us
    all_to_all x1, waiting for transfers between devices, on_device(): lax.all_to_all(grad_sent, 'expert', split_axis=0, concat_axis=0, tiled=True)  183 us
  transfers between devices with their start and end apart: 12, of which 9 were waited for; matrix products, arithmetic and copies ran while one was open for 7% of the time, Pallas kernels for 0%

commit v1 on v0

v1 whole, which is shorter than its diff:
```python
import jax
import jax.numpy as jnp
from jax import lax
from jax.experimental import pallas as pl
from jax.experimental.pallas import tpu as pltpu
from jax.sharding import PartitionSpec as P

HD = 128


EPS = 1e-05
THETA = 10000.0
MASKED = -1e30
LANES = 128


def norm_rows(value, gain):
    inverse = lax.rsqrt(jnp.mean(value * value, axis=-1, keepdims=True) + EPS)
    normed = value * inverse
    return (normed * gain, normed, inverse)


def norm_back(grad_in, gain, normed, inverse):
    grad_normed = grad_in * gain
    grad_gain = jnp.sum(grad_in * normed, axis=0)
    inner = jnp.mean(grad_normed * normed, axis=-1, keepdims=True)
    return (inverse * (grad_normed - normed * inner), grad_gain)


def rope_tables(length, head):
    half = head // 2
    freq = THETA ** (-(jnp.arange(half, dtype=jnp.float32) * 2.0) / head)
    angle = jnp.arange(length, dtype=jnp.float32)[:, None] * freq[None, :]
    angle = jnp.concatenate([angle, angle], axis=-1)
    return (jnp.cos(angle)[:, None, :], jnp.sin(angle)[:, None, :])


def rotate(value, cosine, sine):
    half = value.shape[-1] // 2
    turned = jnp.concatenate([-value[..., half:], value[..., :half]], axis=-1)
    return value * cosine + turned * sine


def rotate_back(grad_in, cosine, sine):
    half = grad_in.shape[-1] // 2
    part = grad_in * sine
    turned = jnp.concatenate([part[..., half:], -part[..., :half]], axis=-1)
    return grad_in * cosine + turned


def contract_rows(left, right):
    return lax.dot_general(
        left, right, (((0,), (0,)), ((), ())), preferred_element_type=jnp.float32
    )


def contract_cols(left, right):
    return lax.dot_general(
        left, right, (((1,), (1,)), ((), ())), preferred_element_type=jnp.float32
    )


def product(left, right):
    return jnp.dot(left, right, preferred_element_type=jnp.float32)


def tie(*values):
    return lax.optimization_barrier(values)


class Spread:
    def __init__(self, here, own):
        self.here, self.queue, self.done = here, [own], 0

    def step(self):
        here, own = self.here, self.queue[0]
        self.done += 1
        if self.done >= here.nz:
            return []
        if here.nz != 4:
            moves = [(a, (a + self.done) % here.nz) for a in range(here.nz)]
            return [here.along_line(own, moves)]
        if self.done == 1:
            return [
                here.along_line(own, [(0, 1), (1, 0), (2, 3), (3, 2)]),
                here.along_line(own, [(1, 2), (2, 1)]),
            ]
        if self.done == 2:
            return [
                here.along_line(self.middle, [(1, 0), (2, 3)]),
                here.along_line(self.queue[1], [(1, 2), (2, 1)]),
            ]
        return [here.along_line(self.across, [(1, 0), (2, 3)])]

    def land(self, arrays):
        here = self.here
        if not arrays:
            return
        if here.nz != 4:
            self.queue += arrays
            return
        inner = (here.z == 1) | (here.z == 2)
        if self.done == 1:
            one, self.middle = arrays
            self.queue.append(one)
        elif self.done == 2:
            edge, self.across = arrays
            self.queue.append(jnp.where(inner, self.middle, edge))
        else:
            self.queue.append(jnp.where(inner, self.across, arrays[0]))

    def finish(self):
        while len(self.queue) < self.here.nz:
            self.land(self.step())
        return self.queue


class Collect:
    def __init__(self, here):
        self.here, self.came, self.moves = here, [], []

    def add(self, k, part):
        here = self.here
        if k == 0:
            self.total = part
            for value in self.came:
                self.total = self.total + value
            return []
        if here.nz != 4:
            out = [(part, [(a, (a - k) % here.nz) for a in range(here.nz)])]
        elif k == 3:
            self.three = part
            out = [(part, [(0, 1), (3, 2)])]
        elif k == 2:
            self.two = part
            (edge,) = self.came
            out = [(self.three + edge, [(1, 2), (2, 1)]), (part, [(0, 1), (3, 2)])]
        else:
            across, edge = self.came
            out = [
                (part + across, [(0, 1), (1, 0), (2, 3), (3, 2)]),
                (self.two + edge, [(1, 2), (2, 1)]),
            ]
        self.moves = [moves for _, moves in out]
        return [value.astype(jnp.bfloat16) for value, _ in out]

    def send(self, values):
        return [self.here.along_line(v, m) for v, m in zip(values, self.moves, strict=True)]

    def land(self, arrays):
        came = [value.astype(jnp.float32) for value in arrays]
        self.came = came if self.here.nz == 4 else self.came + came
        self.moves = []


def grid_of(count):
    if count % 32 == 0:
        return (count // 16, 4, 4)
    if count % 4 == 0:
        return (count // 4, 2, 2)
    return (count, 1, 1)


class Places:
    def __init__(self):
        self.count = lax.axis_size("expert")
        self.cores = lax.axis_size("dp")
        self.nz, self.ny, self.nx = grid_of(self.count)
        self.plane = self.ny * self.nx
        self.me = lax.axis_index("expert")
        self.core = lax.axis_index("dp")
        self.z = self.me // self.plane
        self.y = (self.me // self.nx) % self.ny
        self.x = self.me % self.nx
        self.steps = [(dy, dx) for dy in range(self.ny) for dx in range(self.nx)]
        self.square = (self.ny, self.nx) == (2, 2)
        if self.nz == 4:
            self.queue = [[0, 1, 2, 3], [1, 0, 2, 3], [2, 3, 1, 0], [3, 2, 1, 0]]
        else:
            self.queue = [[(z - k) % self.nz for k in range(self.nz)] for z in range(self.nz)]

    def at(self, z, y, x):
        return (z * self.ny + y) * self.nx + x

    def shift_plane(self, value, dy, dx):
        pairs = [
            (self.at(z, y, x), self.at(z, (y + dy) % self.ny, (x + dx) % self.nx))
            for z in range(self.nz)
            for y in range(self.ny)
            for x in range(self.nx)
        ]
        return lax.ppermute(value, "expert", pairs)

    def along_line(self, value, moves):
        pairs = [
            (self.at(a, y, x), self.at(b, y, x))
            for a, b in moves
            for y in range(self.ny)
            for x in range(self.nx)
        ]
        return lax.ppermute(value, "expert", pairs)

    def other_core(self, value, step):
        pairs = [(c, (c + step) % self.cores) for c in range(self.cores)]
        return lax.ppermute(value, "dp", pairs)

    def arrival(self, rows):
        shard = rows // (self.cores * self.count)
        order = jnp.arange(rows, dtype=jnp.int32)
        inside, rest = order % shard, order // shard
        step, rest = rest % self.plane, rest // self.plane
        core, k = rest % self.cores, rest // self.cores
        zed = self.queue_of(k)
        y = (self.y - step // self.nx) % self.ny
        x = (self.x - step % self.nx) % self.nx
        core = (self.core - core) % self.cores
        source = (core * self.count + self.at(zed, y, x)) * shard + inside
        return (order[:, None] == source[None, :]).astype(jnp.bfloat16)

    def queue_of(self, k):
        table = jnp.asarray(self.queue, jnp.int32)[self.z]
        zed = jnp.zeros_like(k)
        for q in range(self.nz):
            zed = jnp.where(k == q, table[q], zed)
        return zed

    def deal(self, rows):
        return [
            rows[i] if s == (0, 0) else self.shift_plane(rows[i], *s)
            for i, s in enumerate(self.steps)
        ]

    def deal_back(self, rows):
        return [
            rows[i] if s == (0, 0) else self.shift_plane(rows[i], -s[0], -s[1])
            for i, s in enumerate(self.steps)
        ]

    def along_plane(self, values):
        return [
            v if s == (0, 0) else self.shift_plane(v, *s)
            for v, s in zip(values, self.steps, strict=True)
        ]

    def along_whole_line(self, parts):
        return [
            part
            if k == 0
            else self.along_line(part, [(a, (a + k) % self.nz) for a in range(self.nz)])
            for k, part in enumerate(parts)
        ]

    def target_order(self, width, lead):
        shard = width // self.count
        order = jnp.arange(width, dtype=jnp.int32)
        inside, rest = order % shard, order // shard
        k, rest = rest % self.nz, rest // self.nz
        if lead == "x":
            dy, dx = rest % self.ny, rest // self.ny
        else:
            dx, dy = rest % self.nx, rest // self.nx
        y, x = (self.y + dy) % self.ny, (self.x + dx) % self.nx
        source = self.at((self.z + k) % self.nz, y, x) * shard + inside
        return (order[:, None] == source[None, :]).astype(jnp.bfloat16)

    def scatter_terms(self, by_x, by_y, right):
        wire = jnp.bfloat16
        if not self.square:
            line = by_x.shape[1] // self.plane
            starts = [(dx * self.ny + dy) * line for dy, dx in self.steps]
            parts = [contract_rows(by_x[:, start : start + line], right) for start in starts]
            return parts[:1] + [part.astype(wire) for part in parts[1:]]
        half, far = right.shape[1] // 2, by_x.shape[1] // 2
        return [
            contract_rows(by_x[:, far:], right[:, :half]).astype(wire),
            contract_rows(by_y[:, far:], right[:, half:]).astype(wire),
            contract_rows(by_x[:, :far], right[:, :half]),
            contract_rows(by_y[:, :far], right[:, half:]),
        ]

    def scatter_sums(self, terms):
        wire, full = jnp.bfloat16, jnp.float32
        from_x, from_y, near_x, near_y = terms
        line = near_x.shape[0] // 2
        return [
            (near_x[line:] + from_x[line:].astype(full)).astype(wire),
            (near_y[line:] + from_y[line:].astype(full)).astype(wire),
            near_x[:line] + from_x[:line].astype(full),
            near_y[:line] + from_y[:line].astype(full),
        ]

    def line_parts(self, terms):
        full = jnp.float32
        if not self.square:
            total = sum(t.astype(full) for t in terms)
        else:
            from_y, from_x, near_x, near_y = terms
            total = jnp.concatenate(
                [near_x + from_y.astype(full), near_y + from_x.astype(full)], axis=1
            )
        shard = total.shape[0] // self.nz
        parts = [total[k * shard : (k + 1) * shard] for k in range(self.nz)]
        return parts[:1] + [part.astype(jnp.bfloat16) for part in parts[1:]]

    def all_tokens(self, value):
        return jnp.concatenate(
            [value] + [self.other_core(value, step) for step in range(1, self.cores)], axis=0
        )

    def own_columns(self, value):
        width = value.shape[1] // self.cores
        pieces = []
        for step in range(self.cores):
            start = ((self.core + step) % self.cores) * width
            piece = lax.dynamic_slice(value, (0, start), (value.shape[0], width))
            pieces.append(piece if step == 0 else self.other_core(piece, step))
        return jnp.concatenate(pieces, axis=0)


COLUMNS = 1024


def times_gathered(left, pieces, start, stop, so_far=None):
    plane, _, shard, width = pieces[0].shape
    rows, tiles = plane * shard, width // COLUMNS

    def body(left_ref, *refs):
        *piece_refs, out_ref = refs
        total = None if so_far is None else piece_refs.pop()[...]
        for i, piece_ref in enumerate(piece_refs):
            part = left_ref[:, i * rows : (i + 1) * rows]
            term = jnp.dot(
                part, piece_ref[...].reshape(rows, COLUMNS), preferred_element_type=jnp.float32
            )
            total = term if total is None else total + term
        out_ref[...] = total

    depth = (stop - start) * width
    out_spec = pl.BlockSpec((left.shape[0], COLUMNS), lambda w, j: (0, w * tiles + j))
    piece_spec = pl.BlockSpec((plane, 1, shard, COLUMNS), lambda w, j: (0, w + start, 0, j))
    return pl.pallas_call(
        body,
        grid=(stop - start, tiles),
        in_specs=[pl.BlockSpec(left.shape, lambda w, j: (0, 0))]
        + [piece_spec] * len(pieces)
        + [out_spec] * (so_far is not None),
        out_specs=out_spec,
        out_shape=jax.ShapeDtypeStruct((left.shape[0], depth), jnp.float32),
        compiler_params=pltpu.CompilerParams(vmem_limit_bytes=40 << 20),
        cost_estimate=pl.CostEstimate(
            flops=2 * left.shape[0] * left.shape[1] * depth,
            bytes_accessed=2 * left.shape[1] * depth + 8 * left.shape[0] * depth,
            transcendentals=0,
        ),
    )(left, *pieces, *([] if so_far is None else [so_far]))


def times_transposed(left, pieces, start, stop):
    plane, _, shard, width = pieces[0].shape
    rows, tiles = plane * shard, width // COLUMNS
    out_shape = (left.shape[0], rows * len(pieces))

    def body(left_ref, *refs):
        *piece_refs, out_ref = refs

        @pl.when((pl.program_id(0) == 0) & (pl.program_id(1) == 0))
        def _():
            out_ref[...] = jnp.zeros_like(out_ref)

        for i, piece_ref in enumerate(piece_refs):
            out_ref[:, i * rows : (i + 1) * rows] += lax.dot_general(
                left_ref[...],
                piece_ref[...].reshape(rows, COLUMNS),
                (((1,), (1,)), ((), ())),
                preferred_element_type=jnp.float32,
            )

    piece_spec = pl.BlockSpec((plane, 1, shard, COLUMNS), lambda w, j: (0, w + start, 0, j))
    return pl.pallas_call(
        body,
        grid=(stop - start, tiles),
        in_specs=[pl.BlockSpec((left.shape[0], COLUMNS), lambda w, j: (0, w * tiles + j))]
        + [piece_spec] * len(pieces),
        out_specs=pl.BlockSpec(out_shape, lambda w, j: (0, 0)),
        out_shape=jax.ShapeDtypeStruct(out_shape, jnp.float32),
        compiler_params=pltpu.CompilerParams(vmem_limit_bytes=40 << 20),
        cost_estimate=pl.CostEstimate(
            flops=2 * left.size * out_shape[1],
            bytes_accessed=2 * left.shape[1] * out_shape[1] + 4 * left.shape[0] * out_shape[1],
            transcendentals=0,
        ),
    )(left, *pieces)


def on_device(
    tokens,
    segments,
    expert_ids,
    norm_gains,
    w_query,
    w_key,
    w_value,
    w_out,
    w_router,
    expert_gate,
    expert_up,
    expert_down,
    cotangent,
):
    bfloat = jnp.bfloat16
    here = Places()
    length, width = tokens.shape
    topk = expert_ids.shape[1]
    experts = here.count
    capacity = length * topk // experts
    heads = width // HD
    shard = w_query.shape[0]
    plane = here.plane
    gate_w, up_w, down_w = expert_gate[0], expert_up[0], expert_down[0]

    labels = jnp.arange(experts, dtype=jnp.int32)
    named = jnp.any(expert_ids[:, :, None] == labels[None, None, :], axis=1)
    places = jnp.arange(length, dtype=jnp.int32)
    earlier = (places[:, None] < places[None, :]).astype(bfloat)
    slots = contract_rows(named.astype(bfloat), earlier)
    slots = jnp.where(named.T & (slots < capacity), slots, -1.0).astype(bfloat)

    order = range(here.nz)
    arrival = here.arrival(width)
    extra = norm_gains.shape[0] + w_router.shape[1]
    smalls = jnp.concatenate(
        [norm_gains.T, w_router, jnp.zeros((shard, -extra % LANES), jnp.float32)], axis=1
    ).astype(bfloat)
    smalls = jnp.concatenate([smalls, slots.reshape(-1, LANES)], axis=0)
    smalls = here.along_whole_line([smalls] * here.nz)
    plane_expert = jnp.stack(
        [
            here.at(here.z, (here.y + dy) % here.ny, (here.x + dx) % here.nx)
            for dy, dx in here.steps
        ]
    )
    chosen = plane_expert[:, None] == labels[None, :]
    slot_ids = jnp.arange(capacity, dtype=jnp.int32)
    spreads = []

    def spread_of(part):
        picked = jnp.sum(
            jnp.where(chosen[:, :, None], part[None].astype(jnp.float32), 0.0), axis=1
        ).astype(jnp.int32)
        hit = picked[:, None, :] == slot_ids[None, :, None]
        return hit.astype(bfloat).reshape(plane * capacity, length)

    def rows_of(spread, part):
        return list(product(spread, part).astype(bfloat).reshape(plane, capacity, -1))

    def parted(rows):
        return list(rows.reshape(plane, capacity, -1))

    def joined(rows):
        return jnp.concatenate(rows, axis=0)

    inputs = tokens.astype(jnp.float32)
    weights = jnp.stack([w_query, w_key, w_value, w_out]).astype(bfloat)
    line, cot_line = Spread(here, weights), Spread(here, cotangent)
    half = weights.shape[0] // 2
    got, pieces = [], []
    projected = None
    depth = width // here.nz
    cot_rows, rows_cot = [None] * here.nz, [None] * here.nz

    def stacked(rows):
        return rows.reshape(-1, shard, width)

    def share(blocks):
        chunk = jnp.concatenate(blocks, axis=0).reshape(plane, *weights.shape)
        return [chunk] + [here.other_core(chunk, s) for s in range(1, here.cores)]

    def project(k):
        return times_gathered(
            in_order[:, k * depth : (k + 1) * depth], pieces[k], 0, 3, projected
        )

    for k in range(here.nz + 2):
        outs = []
        if here.square:
            by_x, by_y = [], []
            if k < here.nz:
                by_x.append(line.queue[k])
                by_y.append(line.queue[k])
            if 0 < k <= here.nz:
                by_x.append(got[k - 1][2][:half])
                by_y.append(got[k - 1][1][half:])
            if k >= here.nz:
                by_x.append(stacked(cot_rows[k - here.nz][1]))
                by_y.append(stacked(cot_rows[k - here.nz][2]))
            outs = [jnp.concatenate(by_x, axis=0), jnp.concatenate(by_y, axis=0)]
            if k > here.nz:
                outs.append(jnp.concatenate([cot_rows[0][3], cot_rows[1][3]], axis=0))
        elif k < here.nz:
            outs = [line.queue[k]] * plane
        else:
            outs = cot_rows[k - here.nz]
        if k == 1:
            turned = jnp.stack(smalls).reshape(here.nz, -1)
            near = (here.z - here.queue_of(jnp.arange(here.nz))) % here.nz
            pick = (near[:, None] == jnp.arange(here.nz)[None, :]).astype(bfloat)
            turned = product(pick, turned).astype(bfloat).reshape(here.nz, -1, LANES)
            smalls, slots = turned[:, :shard], turned[:, shard:]
        outs, smalls, got, pieces, line.queue, cot_line.queue, cot_rows, cotangent = tie(
            outs, smalls, got, pieces, line.queue, cot_line.queue, cot_rows, cotangent
        )
        if here.square:
            ins = [here.shift_plane(outs[0], 0, 1), here.shift_plane(outs[1], 1, 0)]
            if k > here.nz:
                ins.append(here.shift_plane(outs[2], 1, 1))
        else:
            ins = here.along_plane(outs)
        moving = line.step() if k < here.nz else []
        moving_cot = cot_line.step() if k >= here.nz - 1 else []
        if k == 1:
            spreads = [spread_of(part.reshape(experts, length)) for part in slots]
            smalls = here.along_plane([smalls] * plane)
        if k > 1:
            pieces.append(share(got[k - 2]))
        if k == 2:
            smalls = jnp.stack(smalls, axis=1)
            smalls = [smalls] + [here.other_core(smalls, s) for s in range(1, here.cores)]
            smalls = jnp.stack(smalls, axis=1).reshape(width, -1)
        if k == 3:
            smalls = product(arrival, smalls).astype(bfloat)
            gains_f = smalls[:, : norm_gains.shape[0]].T.astype(jnp.float32)
            wr = smalls[:, norm_gains.shape[0] : extra]
            normed_in_f, normed_one, inverse_one = norm_rows(inputs, gains_f[0])
            normed_in = normed_in_f.astype(bfloat)
            in_order = product(normed_in, arrival).astype(bfloat)
        if k > 2:
            projected = project(k - 3)
        if k >= here.nz - 1 and k - here.nz + 1 < here.nz:
            at = k - here.nz + 1
            cot_rows[at] = rows_of(spreads[at], cot_line.queue[at])
        ins, moving, moving_cot, smalls, projected, cot_rows, spreads = tie(
            ins, moving, moving_cot, smalls, projected, cot_rows, spreads
        )
        line.land(moving)
        cot_line.land(moving_cot)
        if here.square:
            by_x, by_y = ins[:2]
            if k < here.nz:
                got.append([line.queue[k], by_x[: 2 * half], by_y[: 2 * half]])
                by_x, by_y = by_x[2 * half :], by_y[2 * half :]
            if 0 < k <= here.nz:
                got[k - 1] += [by_x[:half], by_y[:half]]
                by_x, by_y = by_x[half:], by_y[half:]
            if k >= here.nz:
                own = cot_rows[k - here.nz][0]
                rows_cot[k - here.nz] = [own, by_x.reshape(own.shape), by_y.reshape(own.shape)]
            if k > here.nz:
                for i in (0, 1):
                    rows_cot[i].append(ins[2][i * capacity : (i + 1) * capacity])
        elif k < here.nz:
            got.append(ins)
        else:
            rows_cot[k - here.nz] = ins

    order_x = here.target_order(width // here.cores, "x")
    order_y = here.target_order(width // here.cores, "y")

    def targeted(value):
        columns = here.own_columns(value)
        return [product(columns, o).astype(bfloat) for o in (order_x, order_y)]

    if here.nz > 2:
        cot_rows[2:], pieces, projected = tie(cot_rows[2:], pieces, projected)
        rows_cot[2] = here.along_plane(cot_rows[2])
        cot_rows[3] = rows_of(spreads[3], cot_line.queue[3])
    projected = project(here.nz - 1)
    pieces = [piece for chunk in pieces for piece in chunk]
    query_raw = projected[:, :width]
    key_raw = projected[:, width : 2 * width]
    values = projected[:, 2 * width :].astype(bfloat)
    query_n, query_normed, query_inverse = norm_rows(query_raw, gains_f[1])
    key_n, key_normed, key_inverse = norm_rows(key_raw, gains_f[2])
    cosine, sine = rope_tables(length, HD)
    query_rot = rotate(query_n.reshape(length, heads, HD), cosine, sine).astype(bfloat)
    key_rot = rotate(key_n.reshape(length, heads, HD), cosine, sine).astype(bfloat)
    if here.nz > 2:
        targets = targeted(normed_in)
        query_rot, key_rot, values, cot_rows[3], rows_cot[2], targets = tie(
            query_rot, key_rot, values, cot_rows[3], rows_cot[2], targets
        )
        rows_cot[3] = here.along_plane(cot_rows[3])
    else:
        targets = targeted(normed_in)
    value_heads = values.reshape(length, heads, HD)
    doc_ids = segments[0]
    visible = (doc_ids[:, None] == doc_ids[None, :]) & (places[:, None] >= places[None, :])
    score_scale = HD ** (-0.5)
    scores = (
        jnp.einsum("qhd,khd->hqk", query_rot, key_rot, preferred_element_type=jnp.float32)
        * score_scale
    )
    scores = jnp.where(visible[None], scores, MASKED)
    row_max = jnp.max(scores, axis=-1, keepdims=True)
    expo = jnp.exp(scores - row_max)
    probs = expo / jnp.sum(expo, axis=-1, keepdims=True)
    probs_low = probs.astype(bfloat)
    attended = (
        jnp.einsum("hqk,khd->qhd", probs_low, value_heads, preferred_element_type=jnp.float32)
        .reshape(length, width)
        .astype(bfloat)
    )
    residual = inputs + times_gathered(
        product(attended, arrival).astype(bfloat), pieces, 3, 4
    )
    normed_mid_f, normed_two, inverse_two = norm_rows(residual, gains_f[3])
    normed_mid = normed_mid_f.astype(bfloat)

    own_label = labels[None, :] == here.me

    def expert_forward(arrived):
        route_here = jax.nn.softmax(product(arrived, wr), axis=-1)
        gate = jnp.sum(jnp.where(own_label, route_here, 0.0), axis=-1)
        gate = gate.astype(bfloat).astype(jnp.float32)[:, None]
        pre_gate = product(arrived, gate_w)
        pre_up = product(arrived, up_w)
        activated = (jax.nn.silu(pre_gate) * pre_up).astype(bfloat)
        result = product(activated, down_w).astype(bfloat)
        gated = (gate * result.astype(jnp.float32)).astype(bfloat)
        return (gate, pre_gate, pre_up, activated, result, gated)

    def expert_backward(kept, cot):
        gate, pre_gate, pre_up, activated, result, _ = kept
        cot_f, result_f = cot.astype(jnp.float32), result.astype(jnp.float32)
        grad_y = (gate * cot_f).astype(bfloat)
        grad_g = jnp.sum(cot_f * result_f, axis=-1, keepdims=True)
        grad_act = contract_cols(grad_y, down_w)
        sigmoid_g = jax.nn.sigmoid(pre_gate)
        slope = sigmoid_g * (1.0 + pre_gate * (1.0 - sigmoid_g))
        grad_a = (grad_act * pre_up * slope).astype(bfloat)
        grad_b = (grad_act * (pre_gate * sigmoid_g)).astype(bfloat)
        grad_e = contract_cols(grad_a, gate_w) + contract_cols(grad_b, up_w)
        high = grad_g.astype(bfloat)
        low = (grad_g - high.astype(jnp.float32)).astype(bfloat)
        lanes = jnp.arange(LANES, dtype=jnp.int32)[None, :]
        tail = jnp.where(lanes == here.me, high, jnp.zeros((), bfloat))
        tail = jnp.where(lanes == here.me + LANES // 2, low, tail)
        back = jnp.concatenate([grad_e.astype(bfloat), tail], axis=1)
        return (back, grad_y, grad_a, grad_b)

    rows_next = rows_of(spreads[0], normed_mid)
    normed_mid, rows_next, rows_cot[-1] = tie(normed_mid, rows_next, rows_cot[-1])
    line = Spread(here, normed_mid)
    rows_in, forward = [], []
    for k in order:
        if k > 0:
            rows_next = rows_of(spreads[k], line.queue[k])
        rows_next, rows_in, line.queue = tie(rows_next, rows_in, line.queue)
        moving = line.step()
        rows = here.along_plane(rows_next)
        if k > 0:
            rows_in[-1] = joined(rows_in[-1])
            forward.append(expert_forward(rows_in[-1]))
        if k == here.nz // 2:
            targets_out = targeted(attended)
            rows, targets_out = tie(rows, targets_out)
        moving, rows, forward = tie(moving, rows, forward)
        rows_in.append(rows)
        line.land(moving)

    half = here.nz // 2
    back_y = [None] * here.nz
    backward = [None] * here.nz
    todo = ["forward", *reversed(order)]

    def work():
        k = todo.pop(0) if todo else None
        if k == "forward":
            rows_in[-1] = joined(rows_in[-1])
            forward.append(expert_forward(rows_in[-1]))
        elif k is not None:
            backward[k] = expert_backward(forward[k], joined(rows_cot[k]))

    for k in order[:half]:
        rows_next = parted(forward[k][5])
        rows_next, forward, backward, rows_in, rows_cot = tie(
            rows_next, forward, backward, rows_in, rows_cot
        )
        rows = here.deal_back(rows_next)
        work()
        rows, forward, backward = tie(rows, forward, backward)
        back_y[k] = rows
    collect = Collect(here)
    moving, back = [], None
    for k in reversed(order):
        if backward[k] is None:
            work()
        rows_next = parted(backward[k][0])
        rows_next, forward, backward, moving, back = tie(
            rows_next, forward, backward, moving, back
        )
        rows = here.deal_back(rows_next)
        if back is not None:
            collect.land(moving)
            moving = collect.add(k + 1, contract_rows(spreads[k + 1], joined(back)))
            if k == 0:
                arrived, activated = joined(rows_in), joined([kept[3] for kept in forward])
                grad_y, grad_a, grad_b = [
                    joined([kept[i] for kept in backward]) for i in (1, 2, 3)
                ]
                moving, activated, grad_y, arrived, grad_a, grad_b = tie(
                    moving, activated, grad_y, arrived, grad_a, grad_b
                )
            moving = collect.send(moving)
        if k > 0:
            work()
            moving, rows, forward, backward = tie(moving, rows, forward, backward)
        else:
            grad_down = contract_rows(activated, grad_y)
            moving, rows, grad_down = tie(moving, rows, grad_down)
        back = rows
    collect.land(moving)
    rows_next = parted(forward[-1][5])
    back, rows_next = tie(back, rows_next)
    collect.add(0, contract_rows(spreads[0], joined(back)))
    returned = collect.total
    rows_y = here.deal_back(rows_next)

    grad_mid = returned[:, :width]
    grad_route = (
        returned[:, width : width + experts]
        + returned[:, width + LANES // 2 : width + LANES // 2 + experts]
    )
    route = jax.nn.softmax(product(normed_mid, wr), axis=-1)
    grad_logits = (
        route * (grad_route - jnp.sum(route * grad_route, axis=-1, keepdims=True))
    ).astype(bfloat)
    grad_router = contract_rows(normed_mid, grad_logits)
    grad_mid = grad_mid + contract_cols(grad_logits, wr)
    grad_res_two, grad_gain_mid = norm_back(grad_mid, gains_f[3], normed_two, inverse_two)
    grad_residual = cotangent.astype(jnp.float32) + grad_res_two
    grad_attn = grad_residual.astype(bfloat)
    out_tokens = here.all_tokens(grad_attn)
    grad_attended = times_transposed(grad_attn, pieces, 3, 4).astype(bfloat)
    grad_attended = contract_cols(grad_attended, arrival).astype(bfloat)
    terms = here.scatter_terms(*targets_out, out_tokens)
    rows_next = [parted(forward[k][5]) for k in order[half : here.nz - 1]]
    grad_attended, terms, rows_y, rows_next = tie(grad_attended, terms, rows_y, rows_next)
    back_y[-1] = rows_y

    collect_y, adds_y = Collect(here), list(reversed(order))

    def next_y():
        if not adds_y:
            return []
        k = adds_y.pop(0)
        return collect_y.add(k, contract_rows(spreads[k], joined(back_y[k])))

    sending_y = next_y()
    sending_y, rows_next, grad_attended = tie(sending_y, rows_next, grad_attended)
    for k in reversed(order[half : here.nz - 1]):
        back_y[k] = here.deal_back(rows_next[k - half])
    moving = collect_y.send(sending_y)
    grad_attended = grad_attended.reshape(length, heads, HD)
    grad_probs = jnp.einsum(
        "qhd,khd->hqk", grad_attended, value_heads, preferred_element_type=jnp.float32
    )
    grad_values = jnp.einsum(
        "hqk,qhd->khd", probs_low, grad_attended, preferred_element_type=jnp.float32
    )
    grad_values = grad_values.reshape(length, width).astype(bfloat)
    inner = jnp.sum(probs * grad_probs, axis=-1, keepdims=True)
    grad_scores = (probs * (grad_probs - inner)).astype(bfloat)
    right = here.all_tokens(grad_values)
    grad_scores, grad_values, right, moving, back_y = tie(
        grad_scores, grad_values, right, moving, back_y
    )
    collect_y.land(moving)

    def leave(terms, sums, more_x, more_y):
        if not here.square:
            return list(terms)
        by_x, by_y = list(terms[:1]), list(terms[1:2])
        if sums:
            by_x.append(sums[1])
            by_y.append(sums[0])
        return [jnp.concatenate(by_x + more_x, axis=0), jnp.concatenate(by_y + more_y, axis=0)]

    def arrive(outs):
        if not here.square:
            return here.along_plane(outs) if outs else []
        return [here.shift_plane(outs[0], 0, 1), here.shift_plane(outs[1], 1, 0)]

    sending_y = next_y()
    outs = leave(terms, [], [], [])
    near, near_last = terms[2:], []
    outs, sending_y, grad_scores, right = tie(outs, sending_y, grad_scores, right)
    ins = arrive(outs)
    moving = collect_y.send(sending_y)
    terms = here.scatter_terms(*targets, right)
    grad_query_rot = (
        jnp.einsum("hqk,khd->qhd", grad_scores, key_rot, preferred_element_type=jnp.float32)
        * score_scale
    )
    grad_key_rot = (
        jnp.einsum("hqk,qhd->khd", grad_scores, query_rot, preferred_element_type=jnp.float32)
        * score_scale
    )
    grad_query_n = rotate_back(grad_query_rot, cosine, sine).reshape(length, width)
    grad_key_n = rotate_back(grad_key_rot, cosine, sine).reshape(length, width)
    grad_query_f, grad_gain_query = norm_back(grad_query_n, gains_f[1], query_normed, query_inverse)
    grad_key_f, grad_gain_key = norm_back(grad_key_n, gains_f[2], key_normed, key_inverse)
    grad_query = grad_query_f.astype(bfloat)
    grad_key = grad_key_f.astype(bfloat)

    grad_query, grad_key, terms, ins, moving = tie(grad_query, grad_key, terms, ins, moving)
    expert_sums = [(arrived, grad_a), (arrived, grad_b)]
    firsts, lasts, shares = [], [], []
    small_rows = 4 + experts
    jobs, small = 4, [None]
    for i in range(1, jobs + 2):
        collect_y.land(moving)
        if here.square:
            by_x, by_y = ins
            if i <= jobs:
                rows = near[0].shape[0]
                firsts.append([by_x[:rows], by_y[:rows], *near])
                by_x, by_y = by_x[rows:], by_y[rows:]
            if i > 1:
                rows = near_last[0].shape[0]
                lasts.append([by_y[:rows], by_x[:rows], *near_last])
                by_x, by_y = by_x[rows:], by_y[rows:]
        elif i <= jobs:
            lasts.append(ins)
        sums, parts, more_x, more_y, outs = [], [], [], [], []
        if here.square:
            sums = here.scatter_sums(firsts[i - 1]) if i <= jobs else []
            columns = small[0].shape[1] // 2 if small[0] is not None else 0
            if i == 3:
                more_x = [small[0][:, columns:].astype(bfloat).reshape(-1, width // 2)]
                small = [small[0][:, :columns]]
            elif i == 4:
                got_small = by_x.reshape(small[0].shape).astype(jnp.float32)
                small = [small[0] + got_small]
                more_y = [small[0][:, columns:].astype(bfloat).reshape(-1, width // 2)]
                small = [small[0][:, :columns]]
            elif i == 5:
                small = [small[0] + by_y.reshape(small[0].shape).astype(jnp.float32)]
            if i < jobs:
                near = terms[2:]
                outs = leave(terms, sums, more_x, more_y)
            elif i == jobs:
                outs = [
                    jnp.concatenate([sums[1], *more_x], axis=0),
                    jnp.concatenate([sums[0], *more_y], axis=0),
                ]
            near_last = sums[2:]
        elif i < jobs:
            outs = leave(terms, [], [], [])
        at = i - 2 if here.square else i - 1
        if 0 <= at < jobs:
            parts = here.line_parts(lasts[at])
            if here.square and at == jobs - 1:
                flat = [
                    piece.reshape(-1, width)
                    for piece in jnp.split(small[0], here.nz, axis=1)
                ]
                parts = [
                    jnp.concatenate([part, piece.astype(part.dtype)], axis=0)
                    for part, piece in zip(parts, flat, strict=True)
                ]
        sending_y = next_y()
        outs, parts, sending_y, terms, expert_sums, near, near_last, small = tie(
            outs, parts, sending_y, terms, expert_sums, near, near_last, small
        )
        ins = arrive(outs) if outs else []
        if parts:
            parts = here.along_whole_line(parts)
        moving = collect_y.send(sending_y)
        if i == 1:
            both = jnp.stack([grad_key, grad_query])
            others = [here.other_core(both, step) for step in range(1, here.cores)]
            rights = [jnp.concatenate([v[j] for v in [both, *others]], axis=0) for j in (0, 1)]
            grad_in_norm = times_transposed(
                jnp.concatenate([grad_query, grad_key, grad_values], axis=1), pieces, 0, 3
            )
            high = grad_in_norm.astype(bfloat)
            low = (grad_in_norm - high.astype(jnp.float32)).astype(bfloat)
            grad_in_norm = contract_cols(high, arrival) + contract_cols(low, arrival)
            grad_res_one, grad_gain_in = norm_back(
                grad_in_norm, gains_f[0], normed_one, inverse_one
            )
            grad_tokens = (grad_residual + grad_res_one).astype(bfloat)
            smalls = jnp.concatenate(
                [
                    jnp.stack(
                        [grad_gain_in, grad_gain_query, grad_gain_key, grad_gain_mid], axis=0
                    ),
                    grad_router.T,
                    jnp.zeros((-small_rows % 32, width), jnp.float32),
                ],
                axis=0,
            )
            if here.square:
                rows = smalls.shape[0]
                smalls = here.own_columns(smalls)
                smalls = sum(smalls[c * rows : (c + 1) * rows] for c in range(here.cores))
                small = [product(smalls.astype(bfloat), order_x)]
            else:
                smalls = lax.psum(smalls, ("dp", "expert"))
                smalls = lax.dynamic_slice(
                    smalls,
                    (0, (here.core * here.count + here.me) * shard),
                    (smalls.shape[0], shard),
                )
            ins, grad_tokens, small, rights = tie(ins, grad_tokens, small, rights)
        if i < jobs - 1:
            terms = here.scatter_terms(*targets, rights[i - 1])
        if 1 < i < 4:
            grad = contract_rows(*expert_sums[i - 2])
            ins, expert_sums[i - 2] = tie(ins, grad)
        ins, parts, moving, terms = tie(ins, parts, moving, terms)
        if parts:
            shares.append(sum(part.astype(jnp.float32) for part in parts))
    if here.square:
        smalls = shares[-1][shard:].reshape(-1, shard)
        shares[-1] = shares[-1][:shard]
    mixed = (residual + collect_y.total).astype(bfloat)
    grad_wo, grad_wv, grad_wk, grad_wq = shares
    grad_gate_w, grad_up_w = expert_sums
    return (
        mixed,
        grad_tokens,
        smalls[:4],
        grad_wq,
        grad_wk,
        grad_wv,
        grad_wo,
        smalls[4:small_rows].T,
        grad_gate_w[None, None],
        grad_up_w[None, None],
        grad_down[None, None],
    )


def solution(mesh):
    return jax.shard_map(
        on_device,
        mesh=mesh,
        in_specs=(
            P(("dp", "expert"), None),
            P(("dp", "expert"), None),
            P(("dp", "expert"), None),
            P(None, ("dp", "expert")),
            P(("dp", "expert"), None),
            P(("dp", "expert"), None),
            P(("dp", "expert"), None),
            P(("dp", "expert"), None),
            P(("dp", "expert"), None),
            P("expert", None, None),
            P("expert", None, None),
            P("expert", None, None),
            P(("dp", "expert"), None),
        ),
        out_specs=(
            P(("dp", "expert"), None),
            P(("dp", "expert"), None),
            P(None, ("dp", "expert")),
            P(("dp", "expert"), None),
            P(("dp", "expert"), None),
            P(("dp", "expert"), None),
            P(("dp", "expert"), None),
            P(("dp", "expert"), None),
            P("dp", "expert", None, None),
            P("dp", "expert", None, None),
            P("dp", "expert", None, None),
        ),
        check_vma=False,
    )
```

time: 2930 us -> 1050 us (0.36)
  waiting for transfers between devices: 1890 us -> 337 us
  blocking collectives: 672 us -> 0 us
  starting transfers between devices: 10.2 us -> 164 us
  local copies, waits for them, and re-layouts: 35.8 us -> 109 us
  other arithmetic: 54.5 us -> 119 us
  Pallas kernels: 0 us -> 56.6 us
    reduce_scatter x4 -> x0, waiting for transfers between devices: 1450 us -> none  [the longest x1 363 us: on_device(): lax.psum_scatter(grad_wo, ('dp', 'expert'), scatter_dimension=0, tiled=True)]
    all_to_all x2 -> x0, blocking collectives: 381 us -> none  [the longest x1 194 us: on_device(): lax.all_to_all(grad_rows_y, 'expert', split_axis=0, concat_axis=0, tiled=...]
    ppermute x0 -> x119, waiting for transfers between devices: none -> 337 us  [the longest x68 237 us: shift_plane(): return lax.ppermute(value, 'expert', pairs)]
    all_gather x2 -> x0, blocking collectives: 291 us -> none  [the longest x1 229 us: on_device(): lax.all_gather(w_router.astype(bfloat), ('dp', 'expert'), axis=0, tiled=T...]
    all_gather x4 -> x0, waiting for transfers between devices: 198 us -> none  [the longest x1 72.5 us: on_device(): lax.all_gather(w_out.astype(bfloat), ('dp', 'expert'), axis=0, tiled=True)]
    all_to_all x2 -> x0, waiting for transfers between devices: 183 us -> none  [the longest x1 183 us: on_device(): lax.all_to_all(grad_sent, 'expert', split_axis=0, concat_axis=0, tiled=True)]
    ppermute x0 -> x119, starting transfers between devices: none -> 164 us  [the longest x40 65.1 us: along_line(): return lax.ppermute(value, 'expert', pairs)]
    dot_general x19 -> x36, matrix products: 167 us -> 76.7 us  [the longest x34 73 us: product(): return jnp.dot(left, right, preferred_element_type=jnp.float32)]
  transfers between devices with their start and end apart: 12 -> 119, of which waited for: 9 -> 60; matrix products, arithmetic and copies ran while one was open for 7% -> 29% of each run, Pallas kernels for 0% -> 4%
where the time goes in v1:
time: 1050 us
  waiting for transfers between devices  337 us (32%)
  matrix products  257 us (24%)
  starting transfers between devices  164 us (16%)
  other arithmetic  119 us (11%)
  local copies, waits for them, and re-layouts  109 us (10%)
  Pallas kernels  56.6 us (5%)
    ppermute x68, waiting for transfers between devices, shift_plane(): return lax.ppermute(value, 'expert', pairs)  237 us
    ppermute x40, waiting for transfers between devices, along_line(): return lax.ppermute(value, 'expert', pairs)  96.8 us
    dot_general x16, matrix products, contract_cols(): lax.dot_general(left, right, (((1,), (1,)), ((), ())), preferred_element_...  88.2 us
    dot_general x29, matrix products, contract_rows(): lax.dot_general(left, right, (((0,), (0,)), ((), ())), preferred_element_...  82.5 us
    dot_general x34, matrix products, product(): return jnp.dot(left, right, preferred_element_type=jnp.float32)  73 us
    ppermute x40, starting transfers between devices, along_line(): return lax.ppermute(value, 'expert', pairs)  65.1 us
    ppermute x68, starting transfers between devices, shift_plane(): return lax.ppermute(value, 'expert', pairs)  59.1 us
    ppermute x11, starting transfers between devices, other_core(): return lax.ppermute(value, 'dp', pairs)  39.7 us
  transfers between devices with their start and end apart: 119, of which 60 were waited for; matrix products, arithmetic and copies ran while one was open for 29% of the time, Pallas kernels for 4%

profile of v1, /device:TPU:9, one launch (start us, length us, event | category | flops | bytes accessed | tf_op | source)
XLA Modules:
  0.0 1046.5 jit_solution(9690275098857090339)
XLA Ops:
  20.2 11.4 %collective-permute-done.3 = bf16[4,64,2048]{2,1,0:T(8,128)(2,1)} collective-permute-done((bf16[4,64,2048]{2,1,0:T(8,128)(2,1)S(1)}, bf16[4,64,2048]{2,1,0:T(8,128)(2,1)}, u32[]{:S(2)}, u32[]{:S(2)}) %collective-permute-start.3) | collective-permute-done | bytes 1048608 | tf_op jit(solution)/shard_map/ppermute | solution.py:192
  48.3 26.6 %collective-permute-done.11 = bf16[4,64,128]{2,1,0:T(8,128)(2,1)S(1)} collective-permute-done((bf16[4,64,128]{2,1,0:T(8,128)(2,1)S(1)}, bf16[4,64,128]{2,1,0:T(8,128)(2,1)S(1)}, u32[]{:S(2)}, u32[]{:S(2)}) %collective-permute-start.11) | collective-permute-done | bytes 65568 | tf_op jit(solution)/shard_map/ppermute | solution.py:192
  114.5 17.5 %collective-permute-done.16 = bf16[4,64,2048]{2,1,0:T(8,128)(2,1)} collective-permute-done((bf16[4,64,2048]{2,1,0:T(8,128)(2,1)}, bf16[4,64,2048]{2,1,0:T(8,128)(2,1)}, u32[]{:S(2)}, u32[]{:S(2)}) %collective-permute-start.16) | collective-permute-done | bytes 1048608 | tf_op jit(solution)/shard_map/ppermute | solution.py:201
  132.0 11.6 %collective-permute-done.14 = bf16[6,64,2048]{2,1,0:T(8,128)(2,1)} collective-permute-done((bf16[6,64,2048]{2,1,0:T(8,128)(2,1)}, bf16[6,64,2048]{2,1,0:T(8,128)(2,1)}, u32[]{:S(2)}, u32[]{:S(2)}) %collective-permute-start.14) | collective-permute-done | bytes 1572896 | tf_op jit(solution)/shard_map/ppermute | solution.py:192
  169.3 8.0 shard_map.230.refs_2_
  180.3 19.5 %collective-permute-done.19 = bf16[6,64,2048]{2,1,0:T(8,128)(2,1)} collective-permute-done((bf16[6,64,2048]{2,1,0:T(8,128)(2,1)}, bf16[6,64,2048]{2,1,0:T(8,128)(2,1)}, u32[]{:S(2)}, u32[]{:S(2)}) %collective-permute-start.19) | collective-permute-done | bytes 1572896 | tf_op jit(solution)/shard_map/ppermute | solution.py:192
  219.1 8.1 shard_map.231.refs_2_
  230.4 6.6 collective-permute-done.26
  273.0 8.5 shard_map.232.refs_2_
  282.9 7.0 collective-permute-done.32
  289.9 14.0 %collective-permute-done.29 = bf16[2,64,2048]{2,1,0:T(8,128)(2,1)S(1)} collective-permute-done((bf16[2,64,2048]{2,1,0:T(8,128)(2,1)S(1)}, bf16[2,64,2048]{2,1,0:T(8,128)(2,1)S(1)}, u32[]{:S(2)}, u32[]{:S(2)}) %collective-permute-start.29) | collective-permute-done | bytes 524320 | tf_op jit(solution)/shard_map/ppermute | solution.py:192
  308.4 9.2 shard_map.233
  344.6 12.0 %collective-permute-done.36 = bf16[128,2048]{1,0:T(8,128)(2,1)S(1)} collective-permute-done((bf16[128,2048]{1,0:T(8,128)(2,1)}, bf16[128,2048]{1,0:T(8,128)(2,1)S(1)}, u32[]{:S(2)}, u32[]{:S(2)}) %collective-permute-start.36) | collective-permute-done | bytes 524320 | tf_op jit(solution)/shard_map/ppermute | solution.py:192
  390.7 7.1 collective-permute-done.40
  417.9 8.1 collective-permute-done.45
  498.2 6.8 collective-permute-done.57
  541.3 6.6 fusion.45
  596.4 6.6 fusion.41
  628.4 7.3 fusion.39
  661.9 11.7 %fusion.426 = f32[1024,2048]{1,0:T(8,128)} fusion(bf16[2048,1024]{1,0:T(8,128)(2,1)S(1)} %pad_maximum_fusion.2, bf16[2048,2048]{1,0:T(8,128)(2,1)S(1)} %pad_maximum_fusion), kind=kOutput, calls=%fused_computation.785 | convolution fusion | flops 8589934592 | bytes 20971520 | tf_op jit(solution)/shard_map/dot_general | solution.py:52
  680.2 19.8 %collective-permute-start.82 = (bf16[256,2048]{1,0:T(8,128)(2,1)S(1)}, bf16[256,2048]{1,0:T(8,128)(2,1)S(1)}, u32[]{:S(2)}, u32[]{:S(2)}) collective-permute-start(bf16[256,2048]{1,0:T(8,128)(2,1)S(1)} %fusion.378.left_ref), channel_id=1, source_target_pairs={{0,16},{16,0},{1,17},{17,1},{2,18},{18,2},{3,19},{19,3},{4,20},{20... | collective-permute-start | bytes 3145736 | tf_op jit(solution)/shard_map/ppermute | solution.py:205
  740.3 6.9 multiply_convert_fusion
  752.0 11.2 %collective-permute-done.90 = bf16[128,2048]{1,0:T(8,128)(2,1)S(1)} collective-permute-done((bf16[128,2048]{1,0:T(8,128)(2,1)S(1)}, bf16[128,2048]{1,0:T(8,128)(2,1)S(1)}, u32[]{:S(2)}, u32[]{:S(2)}) %collective-permute-start.90) | collective-permute-done | bytes 524320 | tf_op jit(solution)/shard_map/ppermute | solution.py:192
  795.8 14.8 %collective-permute-done.91 = bf16[512,1024]{1,0:T(8,128)(2,1)S(1)} collective-permute-done((bf16[512,1024]{1,0:T(8,128)(2,1)S(1)}, bf16[512,1024]{1,0:T(8,128)(2,1)S(1)}, u32[]{:S(2)}, u32[]{:S(2)}) %collective-permute-start.91) | collective-permute-done | bytes 1048608 | tf_op jit(solution)/shard_map/ppermute | solution.py:192
  830.0 12.4 %shard_map.236 = f32[256,2048]{1,0:T(8,128)S(1)} custom-call(bf16[256,6144]{1,0:T(8,128)(2,1)S(1)} %pad_maximum_fusion.5.left_ref, bf16[4,4,64,2048]{3,2,1,0:T(8,128)(2,1)} %bitcast.30.refs_0_, bf16[4,4,64,2048]{3,2,1,0:T(8,128)(2,1)} %collective-permute-done.18.refs_1_, bf16[4,4,64,2048]{3,2,1,0:T(8,128)(2,1)} %bitcast.323, ...), custom_call_target="tpu_custom_call" | custom-call | flops 6442450944 | bytes 27262976 | tf_op jit(solution)/shard_map/pallas_call | solution.py:379
  884.0 7.1 collective-permute-done.100
  915.5 13.7 %fusion.428 = f32[2048,1024]{1,0:T(8,128)} fusion(bf16[2048,2048]{1,0:T(8,128)(2,1)} %pad_maximum_fusion.1, bf16[2048,1024]{1,0:T(8,128)(2,1)S(1)} %copy-done.39), kind=kOutput, calls=%fused_computation.787 | convolution fusion | flops 8589934592 | bytes 20971520 | tf_op jit(solution)/shard_map/dot_general | solution.py:52
  930.0 12.8 %collective-permute-done.101 = bf16[768,1024]{1,0:T(8,128)(2,1)S(1)} collective-permute-done((bf16[768,1024]{1,0:T(8,128)(2,1)}, bf16[768,1024]{1,0:T(8,128)(2,1)S(1)}, u32[]{:S(2)}, u32[]{:S(2)}) %collective-permute-start.101) | collective-permute-done | bytes 1572896 | tf_op jit(solution)/shard_map/ppermute | solution.py:192
  951.7 11.6 %fusion.429 = f32[2048,1024]{1,0:T(8,128)} fusion(bf16[2048,2048]{1,0:T(8,128)(2,1)S(1)} %bitcast.340, bf16[2048,1024]{1,0:T(8,128)(2,1)S(1)} %copy-done.38), kind=kOutput, calls=%fused_computation.788 | convolution fusion | flops 8589934592 | bytes 20971520 | tf_op jit(solution)/shard_map/dot_general | solution.py:52
  963.3 19.1 %collective-permute-done.107 = bf16[768,1024]{1,0:T(8,128)(2,1)S(1)} collective-permute-done((bf16[768,1024]{1,0:T(8,128)(2,1)S(1)}, bf16[768,1024]{1,0:T(8,128)(2,1)S(1)}, u32[]{:S(2)}, u32[]{:S(2)}) %collective-permute-start.107) | collective-permute-done | bytes 1572896 | tf_op jit(solution)/shard_map/ppermute | solution.py:192
  998.9 14.1 %collective-permute-done.114 = bf16[64,2048]{1,0:T(8,128)(2,1)S(1)} collective-permute-done((bf16[64,2048]{1,0:T(8,128)(2,1)S(1)}, bf16[64,2048]{1,0:T(8,128)(2,1)S(1)}, u32[]{:S(2)}, u32[]{:S(2)}) %collective-permute-start.114) | collective-permute-done | bytes 262176 | tf_op jit(solution)/shard_map/ppermute | solution.py:201
  1023.0 16.1 %collective-permute-done.117 = bf16[65,2048]{1,0:T(8,128)(2,1)S(1)} collective-permute-done((bf16[65,2048]{1,0:T(8,128)(2,1)S(1)}, bf16[65,2048]{1,0:T(8,128)(2,1)S(1)}, u32[]{:S(2)}, u32[]{:S(2)}) %collective-permute-start.117) | collective-permute-done | bytes 266272 | tf_op jit(solution)/shard_map/ppermute | solution.py:201
  (1026 shorter events, 668.0 us)
Async XLA Ops:
  41.1 41.6 %collective-permute-start.7 = (bf16[6,64,2048]{2,1,0:T(8,128)(2,1)}, bf16[6,64,2048]{2,1,0:T(8,128)(2,1)}, u32[]{:S(2)}, u32[]{:S(2)}) collective-permute-start(bf16[6,64,2048]{2,1,0:T(8,128)(2,1)} %get-tuple-element.818), channel_id=1, source_target_pairs={{0,1},{1,0},{2,3},{3,2},{4,5},{5,4},{6,7},{7,6},{8,9},{9,8},{10,11... | collective-permute-start | bytes 4718600 | tf_op jit(solution)/shard_map/ppermute | solution.py:192
  41.4 41.4 %collective-permute-start.8 = (bf16[6,64,2048]{2,1,0:T(8,128)(2,1)}, bf16[6,64,2048]{2,1,0:T(8,128)(2,1)}, u32[]{:S(2)}, u32[]{:S(2)}) collective-permute-start(bf16[6,64,2048]{2,1,0:T(8,128)(2,1)} %get-tuple-element.819), channel_id=1, source_target_pairs={{0,2},{1,3},{2,0},{3,1},{4,6},{5,7},{6,4},{7,5},{8,10},{9,11},{10,... | collective-permute-start | bytes 4718600 | tf_op jit(solution)/shard_map/ppermute | solution.py:192
  41.6 41.2 %collective-permute-start.9 = (bf16[4,64,2048]{2,1,0:T(8,128)(2,1)}, bf16[4,64,2048]{2,1,0:T(8,128)(2,1)}, u32[]{:S(2)}, u32[]{:S(2)}) collective-permute-start(bf16[4,64,2048]{2,1,0:T(8,128)(2,1)} %collective-permute-done.6), channel_id=1, source_target_pairs={{4,0},{5,1},{6,2},{7,3},{8,12},{9,13},{10,14},{11,15},{20,16},{21,... | collective-permute-start | bytes 3145736 | tf_op jit(solution)/shard_map/ppermute | solution.py:201
  43.9 38.9 %collective-permute-start.10 = (bf16[4,64,2048]{2,1,0:T(8,128)(2,1)S(1)}, bf16[4,64,2048]{2,1,0:T(8,128)(2,1)}, u32[]{:S(2)}, u32[]{:S(2)}) collective-permute-start(bf16[4,64,2048]{2,1,0:T(8,128)(2,1)S(1)} %collective-permute-done.5), channel_id=1, source_target_pairs={{4,8},{5,9},{6,10},{7,11},{8,4},{9,5},{10,6},{11,7},{20,24},{21,25... | collective-permute-start | bytes 3145736 | tf_op jit(solution)/shard_map/ppermute | solution.py:201
  100.7 53.7 %collective-permute-start.18 = (bf16[4,4,64,2048]{3,2,1,0:T(8,128)(2,1)}, bf16[4,4,64,2048]{3,2,1,0:T(8,128)(2,1)}, u32[]{:S(2)}, u32[]{:S(2)}) collective-permute-start(bf16[4,4,64,2048]{3,2,1,0:T(8,128)(2,1)} %bitcast.30.refs_0_), channel_id=1, source_target_pairs={{0,16},{16,0},{1,17},{17,1},{2,18},{18,2},{3,19},{19,3},{4,20},{20... | collective-permute-start | bytes 12582920 | tf_op jit(solution)/shard_map/ppermute | solution.py:205
  107.3 36.3 %collective-permute-start.14 = (bf16[6,64,2048]{2,1,0:T(8,128)(2,1)}, bf16[6,64,2048]{2,1,0:T(8,128)(2,1)}, u32[]{:S(2)}, u32[]{:S(2)}) collective-permute-start(bf16[6,64,2048]{2,1,0:T(8,128)(2,1)} %get-tuple-element.836), channel_id=1, source_target_pairs={{0,1},{1,0},{2,3},{3,2},{4,5},{5,4},{6,7},{7,6},{8,9},{9,8},{10,11... | collective-permute-start | bytes 4718600 | tf_op jit(solution)/shard_map/ppermute | solution.py:192
  107.9 36.0 %collective-permute-start.15 = (bf16[6,64,2048]{2,1,0:T(8,128)(2,1)}, bf16[6,64,2048]{2,1,0:T(8,128)(2,1)}, u32[]{:S(2)}, u32[]{:S(2)}) collective-permute-start(bf16[6,64,2048]{2,1,0:T(8,128)(2,1)} %get-tuple-element.837), channel_id=1, source_target_pairs={{0,2},{1,3},{2,0},{3,1},{4,6},{5,7},{6,4},{7,5},{8,10},{9,11},{10,... | collective-permute-start | bytes 4718600 | tf_op jit(solution)/shard_map/ppermute | solution.py:192
  158.2 50.7 %collective-permute-start.23 = (bf16[4,4,64,2048]{3,2,1,0:T(8,128)(2,1)S(1)}, bf16[4,4,64,2048]{3,2,1,0:T(8,128)(2,1)S(1)}, u32[]{:S(2)}, u32[]{:S(2)}) collective-permute-start(bf16[4,4,64,2048]{3,2,1,0:T(8,128)(2,1)S(1)} %bitcast.319), channel_id=1, source_target_pairs={{0,16},{16,0},{1,17},{17,1},{2,18},{18,2},{3,19},{19,3},{4,20},{20... | collective-permute-start | bytes 12582920 | tf_op jit(solution)/shard_map/ppermute | solution.py:205
  163.4 36.4 %collective-permute-start.19 = (bf16[6,64,2048]{2,1,0:T(8,128)(2,1)}, bf16[6,64,2048]{2,1,0:T(8,128)(2,1)}, u32[]{:S(2)}, u32[]{:S(2)}) collective-permute-start(bf16[6,64,2048]{2,1,0:T(8,128)(2,1)} %get-tuple-element.862), channel_id=1, source_target_pairs={{0,1},{1,0},{2,3},{3,2},{4,5},{5,4},{6,7},{7,6},{8,9},{9,8},{10,11... | collective-permute-start | bytes 4718600 | tf_op jit(solution)/shard_map/ppermute | solution.py:192
  164.6 36.0 %collective-permute-start.20 = (bf16[6,64,2048]{2,1,0:T(8,128)(2,1)}, bf16[6,64,2048]{2,1,0:T(8,128)(2,1)}, u32[]{:S(2)}, u32[]{:S(2)}) collective-permute-start(bf16[6,64,2048]{2,1,0:T(8,128)(2,1)} %get-tuple-element.863), channel_id=1, source_target_pairs={{0,2},{1,3},{2,0},{3,1},{4,6},{5,7},{6,4},{7,5},{8,10},{9,11},{10,... | collective-permute-start | bytes 4718600 | tf_op jit(solution)/shard_map/ppermute | solution.py:192
  211.2 37.5 %collective-permute-start.28 = (bf16[4,4,64,2048]{3,2,1,0:T(8,128)(2,1)S(1)}, bf16[4,4,64,2048]{3,2,1,0:T(8,128)(2,1)S(1)}, u32[]{:S(2)}, u32[]{:S(2)}) collective-permute-start(bf16[4,4,64,2048]{3,2,1,0:T(8,128)(2,1)S(1)} %bitcast.324), channel_id=1, source_target_pairs={{0,16},{16,0},{1,17},{17,1},{2,18},{18,2},{3,19},{19,3},{4,20},{20... | collective-permute-start | bytes 12582920 | tf_op jit(solution)/shard_map/ppermute | solution.py:205
  254.3 54.2 %collective-permute-start.33 = (bf16[4,4,64,2048]{3,2,1,0:T(8,128)(2,1)}, bf16[4,4,64,2048]{3,2,1,0:T(8,128)(2,1)}, u32[]{:S(2)}, u32[]{:S(2)}) collective-permute-start(bf16[4,4,64,2048]{3,2,1,0:T(8,128)(2,1)} %bitcast.39.refs_0_.refs_6_), channel_id=1, source_target_pairs={{0,16},{16,0},{1,17},{17,1},{2,18},{18,2},{3,19},{19,3},{4,20},{20... | collective-permute-start | bytes 12582920 | tf_op jit(solution)/shard_map/ppermute | solution.py:205
  267.2 37.3 %collective-permute-start.31 = (bf16[256,2048]{1,0:T(8,128)(2,1)S(1)}, bf16[256,2048]{1,0:T(8,128)(2,1)S(1)}, u32[]{:S(2)}, u32[]{:S(2)}) collective-permute-start(bf16[256,2048]{1,0:T(8,128)(2,1)S(1)} %copy-done.91), channel_id=1, source_target_pairs={{0,3},{1,2},{2,1},{3,0},{4,7},{5,6},{6,5},{7,4},{8,11},{9,10},{10,... | collective-permute-start | bytes 3145736 | tf_op jit(solution)/shard_map/ppermute | solution.py:192
  271.4 32.5 %collective-permute-start.29 = (bf16[2,64,2048]{2,1,0:T(8,128)(2,1)S(1)}, bf16[2,64,2048]{2,1,0:T(8,128)(2,1)S(1)}, u32[]{:S(2)}, u32[]{:S(2)}) collective-permute-start(bf16[2,64,2048]{2,1,0:T(8,128)(2,1)S(1)} %bitcast.354), channel_id=1, source_target_pairs={{0,1},{1,0},{2,3},{3,2},{4,5},{5,4},{6,7},{7,6},{8,9},{9,8},{10,11... | collective-permute-start | bytes 1572872 | tf_op jit(solution)/shard_map/ppermute | solution.py:192
  272.0 32.5 %collective-permute-start.30 = (bf16[2,64,2048]{2,1,0:T(8,128)(2,1)S(1)}, bf16[2,64,2048]{2,1,0:T(8,128)(2,1)S(1)}, u32[]{:S(2)}, u32[]{:S(2)}) collective-permute-start(bf16[2,64,2048]{2,1,0:T(8,128)(2,1)S(1)} %bitcast.353), channel_id=1, source_target_pairs={{0,2},{1,3},{2,0},{3,1},{4,6},{5,7},{6,4},{7,5},{8,10},{9,11},{10,... | collective-permute-start | bytes 1572872 | tf_op jit(solution)/shard_map/ppermute | solution.py:192
  378.6 29.1 %collective-permute-start.55 = (bf16[256,1024]{0,1:T(8,128)(2,1)}, bf16[256,1024]{0,1:T(8,128)(2,1)}, u32[]{:S(2)}, u32[]{:S(2)}) collective-permute-start(bf16[256,1024]{0,1:T(8,128)(2,1)} %get-tuple-element.1768), channel_id=1, source_target_pairs={{0,16},{16,0},{1,17},{17,1},{2,18},{18,2},{3,19},{19,3},{4,20},{20... | collective-permute-start | bytes 1572872 | tf_op jit(solution)/shard_map/ppermute | solution.py:205
  529.8 28.3 %collective-permute-start.62 = (bf16[128,2048]{1,0:T(8,128)(2,1)}, bf16[128,2048]{1,0:T(8,128)(2,1)S(1)}, u32[]{:S(2)}, u32[]{:S(2)}) collective-permute-start(bf16[128,2048]{1,0:T(8,128)(2,1)} %get-tuple-element.1153), channel_id=1, source_target_pairs={{0,1},{1,0},{2,3},{3,2},{4,5},{5,4},{6,7},{7,6},{8,9},{9,8},{10,11... | collective-permute-start | bytes 1572872 | tf_op jit(solution)/shard_map/ppermute | solution.py:192
  531.5 28.3 %collective-permute-start.64 = (bf16[128,2048]{1,0:T(8,128)(2,1)S(1)}, bf16[128,2048]{1,0:T(8,128)(2,1)}, u32[]{:S(2)}, u32[]{:S(2)}) collective-permute-start(bf16[128,2048]{1,0:T(8,128)(2,1)S(1)} %get-tuple-element.1155), channel_id=1, source_target_pairs={{0,3},{1,2},{2,1},{3,0},{4,7},{5,6},{6,5},{7,4},{8,11},{9,10},{10,... | collective-permute-start | bytes 1572872 | tf_op jit(solution)/shard_map/ppermute | solution.py:192
  610.9 31.1 %collective-permute-start.72 = (bf16[256,2176]{1,0:T(8,128)(2,1)S(1)}, bf16[256,2176]{1,0:T(8,128)(2,1)S(1)}, u32[]{:S(2)}, u32[]{:S(2)}) collective-permute-start(bf16[256,2176]{1,0:T(8,128)(2,1)S(1)} %add_convert_fusion.5), channel_id=1, source_target_pairs={{4,8},{5,9},{6,10},{7,11},{8,4},{9,5},{10,6},{11,7},{20,24},{21,25... | collective-permute-start | bytes 3342344 | tf_op jit(solution)/shard_map/ppermute | solution.py:201
  680.2 33.2 %collective-permute-start.82 = (bf16[256,2048]{1,0:T(8,128)(2,1)S(1)}, bf16[256,2048]{1,0:T(8,128)(2,1)S(1)}, u32[]{:S(2)}, u32[]{:S(2)}) collective-permute-start(bf16[256,2048]{1,0:T(8,128)(2,1)S(1)} %fusion.378.left_ref), channel_id=1, source_target_pairs={{0,16},{16,0},{1,17},{17,1},{2,18},{18,2},{3,19},{19,3},{4,20},{20... | collective-permute-start | bytes 3145736 | tf_op jit(solution)/shard_map/ppermute | solution.py:205
  828.0 43.9 %collective-permute-start.95 = (bf16[768,1024]{1,0:T(8,128)(2,1)}, bf16[768,1024]{1,0:T(8,128)(2,1)}, u32[]{:S(2)}, u32[]{:S(2)}) collective-permute-start(bf16[768,1024]{1,0:T(8,128)(2,1)} %pad_maximum_fusion.29), channel_id=1, source_target_pairs={{0,1},{1,0},{2,3},{3,2},{4,5},{5,4},{6,7},{7,6},{8,9},{9,8},{10,11... | collective-permute-start | bytes 4718600 | tf_op jit(solution)/shard_map/ppermute | solution.py:192
  828.9 43.0 %collective-permute-start.96 = (bf16[768,1024]{1,0:T(8,128)(2,1)}, bf16[768,1024]{1,0:T(8,128)(2,1)}, u32[]{:S(2)}, u32[]{:S(2)}) collective-permute-start(bf16[768,1024]{1,0:T(8,128)(2,1)} %pad_maximum_fusion.30), channel_id=1, source_target_pairs={{0,2},{1,3},{2,0},{3,1},{4,6},{5,7},{6,4},{7,5},{8,10},{9,11},{10,... | collective-permute-start | bytes 4718600 | tf_op jit(solution)/shard_map/ppermute | solution.py:192
  907.9 34.9 %collective-permute-start.101 = (bf16[768,1024]{1,0:T(8,128)(2,1)}, bf16[768,1024]{1,0:T(8,128)(2,1)S(1)}, u32[]{:S(2)}, u32[]{:S(2)}) collective-permute-start(bf16[768,1024]{1,0:T(8,128)(2,1)} %pad_maximum_fusion.31), channel_id=1, source_target_pairs={{0,1},{1,0},{2,3},{3,2},{4,5},{5,4},{6,7},{7,6},{8,9},{9,8},{10,11... | collective-permute-start | bytes 4718600 | tf_op jit(solution)/shard_map/ppermute | solution.py:192
  908.6 34.6 %collective-permute-start.102 = (bf16[768,1024]{1,0:T(8,128)(2,1)}, bf16[768,1024]{1,0:T(8,128)(2,1)S(1)}, u32[]{:S(2)}, u32[]{:S(2)}) collective-permute-start(bf16[768,1024]{1,0:T(8,128)(2,1)} %pad_maximum_fusion.32), channel_id=1, source_target_pairs={{0,2},{1,3},{2,0},{3,1},{4,6},{5,7},{6,4},{7,5},{8,10},{9,11},{10,... | collective-permute-start | bytes 4718600 | tf_op jit(solution)/shard_map/ppermute | solution.py:192
  909.4 33.7 %collective-permute-start.103 = (bf16[64,2048]{1,0:T(8,128)(2,1)}, bf16[64,2048]{1,0:T(8,128)(2,1)S(1)}, u32[]{:S(2)}, u32[]{:S(2)}) collective-permute-start(bf16[64,2048]{1,0:T(8,128)(2,1)} %get-tuple-element.1520), channel_id=1, source_target_pairs={{0,4},{1,5},{2,6},{3,7},{4,8},{5,9},{6,10},{7,11},{8,12},{9,13},{1... | collective-permute-start | bytes 786440 | tf_op jit(solution)/shard_map/ppermute | solution.py:201
  910.1 33.0 %collective-permute-start.104 = (bf16[64,2048]{1,0:T(8,128)(2,1)}, bf16[64,2048]{1,0:T(8,128)(2,1)S(1)}, u32[]{:S(2)}, u32[]{:S(2)}) collective-permute-start(bf16[64,2048]{1,0:T(8,128)(2,1)} %get-tuple-element.1521), channel_id=1, source_target_pairs={{0,8},{1,9},{2,10},{3,11},{4,12},{5,13},{6,14},{7,15},{8,0},{9,1},... | collective-permute-start | bytes 786440 | tf_op jit(solution)/shard_map/ppermute | solution.py:201
  910.1 34.4 %collective-permute-start.105 = (bf16[64,2048]{1,0:T(8,128)(2,1)}, bf16[64,2048]{1,0:T(8,128)(2,1)}, u32[]{:S(2)}, u32[]{:S(2)}) collective-permute-start(bf16[64,2048]{1,0:T(8,128)(2,1)} %get-tuple-element.1522), channel_id=1, source_target_pairs={{0,12},{1,13},{2,14},{3,15},{4,0},{5,1},{6,2},{7,3},{8,4},{9,5},{1... | collective-permute-start | bytes 786440 | tf_op jit(solution)/shard_map/ppermute | solution.py:201
  948.3 34.2 %collective-permute-start.106 = (bf16[784,1024]{1,0:T(8,128)(2,1)S(1)}, bf16[784,1024]{1,0:T(8,128)(2,1)S(1)}, u32[]{:S(2)}, u32[]{:S(2)}) collective-permute-start(bf16[784,1024]{1,0:T(8,128)(2,1)S(1)} %pad_maximum_fusion.28), channel_id=1, source_target_pairs={{0,1},{1,0},{2,3},{3,2},{4,5},{5,4},{6,7},{7,6},{8,9},{9,8},{10,11... | collective-permute-start | bytes 4816904 | tf_op jit(solution)/shard_map/ppermute | solution.py:192
  949.2 33.2 %collective-permute-start.107 = (bf16[768,1024]{1,0:T(8,128)(2,1)S(1)}, bf16[768,1024]{1,0:T(8,128)(2,1)S(1)}, u32[]{:S(2)}, u32[]{:S(2)}) collective-permute-start(bf16[768,1024]{1,0:T(8,128)(2,1)S(1)} %pad_maximum_fusion.33), channel_id=1, source_target_pairs={{0,2},{1,3},{2,0},{3,1},{4,6},{5,7},{6,4},{7,5},{8,10},{9,11},{10,... | collective-permute-start | bytes 4718600 | tf_op jit(solution)/shard_map/ppermute | solution.py:192
  950.1 32.5 %collective-permute-start.108 = (bf16[64,2048]{1,0:T(8,128)(2,1)S(1)}, bf16[64,2048]{1,0:T(8,128)(2,1)S(1)}, u32[]{:S(2)}, u32[]{:S(2)}) collective-permute-start(bf16[64,2048]{1,0:T(8,128)(2,1)S(1)} %get-tuple-element.1546), channel_id=1, source_target_pairs={{0,4},{1,5},{2,6},{3,7},{4,8},{5,9},{6,10},{7,11},{8,12},{9,13},{1... | collective-permute-start | bytes 786440 | tf_op jit(solution)/shard_map/ppermute | solution.py:201
  950.4 32.2 %collective-permute-start.109 = (bf16[64,2048]{1,0:T(8,128)(2,1)S(1)}, bf16[64,2048]{1,0:T(8,128)(2,1)S(1)}, u32[]{:S(2)}, u32[]{:S(2)}) collective-permute-start(bf16[64,2048]{1,0:T(8,128)(2,1)S(1)} %get-tuple-element.1547), channel_id=1, source_target_pairs={{0,8},{1,9},{2,10},{3,11},{4,12},{5,13},{6,14},{7,15},{8,0},{9,1},... | collective-permute-start | bytes 786440 | tf_op jit(solution)/shard_map/ppermute | solution.py:201
  950.4 32.2 %collective-permute-start.110 = (bf16[64,2048]{1,0:T(8,128)(2,1)S(1)}, bf16[64,2048]{1,0:T(8,128)(2,1)S(1)}, u32[]{:S(2)}, u32[]{:S(2)}) collective-permute-start(bf16[64,2048]{1,0:T(8,128)(2,1)S(1)} %get-tuple-element.1548), channel_id=1, source_target_pairs={{0,12},{1,13},{2,14},{3,15},{4,0},{5,1},{6,2},{7,3},{8,4},{9,5},{1... | collective-permute-start | bytes 786440 | tf_op jit(solution)/shard_map/ppermute | solution.py:201
  (316 other events, 3594.9 us)

commit v2 on v1

--- a/solution.py
+++ b/solution.py
@@ -25,27 +25,6 @@
     grad_gain = jnp.sum(grad_in * normed, axis=0)
     inner = jnp.mean(grad_normed * normed, axis=-1, keepdims=True)
     return (inverse * (grad_normed - normed * inner), grad_gain)
-
-
-def rope_tables(length, head):
-    half = head // 2
-    freq = THETA ** (-(jnp.arange(half, dtype=jnp.float32) * 2.0) / head)
-    angle = jnp.arange(length, dtype=jnp.float32)[:, None] * freq[None, :]
-    angle = jnp.concatenate([angle, angle], axis=-1)
-    return (jnp.cos(angle)[:, None, :], jnp.sin(angle)[:, None, :])
-
-
-def rotate(value, cosine, sine):
-    half = value.shape[-1] // 2
-    turned = jnp.concatenate([-value[..., half:], value[..., :half]], axis=-1)
-    return value * cosine + turned * sine
-
-
-def rotate_back(grad_in, cosine, sine):
-    half = grad_in.shape[-1] // 2
-    part = grad_in * sine
-    turned = jnp.concatenate([part[..., half:], -part[..., :half]], axis=-1)
-    return grad_in * cosine + turned
 
 
 def contract_rows(left, right):
@@ -263,7 +242,7 @@
         source = self.at((self.z + k) % self.nz, y, x) * shard + inside
         return (order[:, None] == source[None, :]).astype(jnp.bfloat16)
 
-    def scatter_terms(self, by_x, by_y, right):
+    def scatter_far(self, by_x, by_y, right):
         wire = jnp.bfloat16
         if not self.square:
             line = by_x.shape[1] // self.plane
@@ -274,6 +253,13 @@
         return [
             contract_rows(by_x[:, far:], right[:, :half]).astype(wire),
             contract_rows(by_y[:, far:], right[:, half:]).astype(wire),
+        ]
+
+    def scatter_near(self, by_x, by_y, right):
+        if not self.square:
+            return []
+        half, far = right.shape[1] // 2, by_x.shape[1] // 2
+        return [
             contract_rows(by_x[:, :far], right[:, :half]),
             contract_rows(by_y[:, :far], right[:, half:]),
         ]
@@ -307,14 +293,16 @@
             [value] + [self.other_core(value, step) for step in range(1, self.cores)], axis=0
         )
 
-    def own_columns(self, value):
+    def core_columns(self, value):
         width = value.shape[1] // self.cores
-        pieces = []
-        for step in range(self.cores):
-            start = ((self.core + step) % self.cores) * width
-            piece = lax.dynamic_slice(value, (0, start), (value.shape[0], width))
-            pieces.append(piece if step == 0 else self.other_core(piece, step))
-        return jnp.concatenate(pieces, axis=0)
+        starts = [((self.core + step) % self.cores) * width for step in range(self.cores)]
+        return [lax.dynamic_slice(value, (0, start), (value.shape[0], width)) for start in starts]
+
+    def to_cores(self, pieces):
+        return [
+            piece if step == 0 else self.other_core(piece, step)
+            for step, piece in enumerate(pieces)
+        ]
 
 
 COLUMNS = 1024
@@ -390,6 +378,260 @@
             transcendentals=0,
         ),
     )(left, *pieces)
+
+
+def attention(projected, gains, tables, doc_ids, heads):
+    length, width = projected.shape[0], projected.shape[1] // 3
+    low, full = jnp.bfloat16, jnp.float32
+    scale = HD ** (-0.5)
+
+    def body(raw_ref, gain_ref, cos_ref, sin_ref, row_ref, col_ref,
+             query_ref, key_ref, value_ref, out_ref, prob_ref, inv_ref, seen_ref):
+        head = pl.program_id(0)
+
+        @pl.when(head == 0)
+        def _():
+            for i in (0, 1):
+                raw = raw_ref[:, i * width : (i + 1) * width]
+                mean = jnp.mean(raw * raw, axis=-1, keepdims=True)
+                inv_ref[:, i : i + 1] = lax.rsqrt(mean + EPS)
+            at = lax.broadcasted_iota(jnp.int32, (length, length), 0)
+            to = lax.broadcasted_iota(jnp.int32, (length, length), 1)
+            seen = (row_ref[...] == col_ref[...]) & (at >= to)
+            seen_ref[...] = jnp.where(seen, 1.0, 0.0)
+
+        here = pl.multiple_of(head * HD, HD)
+
+        def turned(i):
+            raw = raw_ref[:, pl.ds(pl.multiple_of(i * width + head * HD, HD), HD)]
+            value = raw * inv_ref[:, i : i + 1] * gain_ref[i + 1 : i + 2, pl.ds(here, HD)]
+            return (value * cos_ref[...] + pltpu.roll(value, HD // 2, 1) * sin_ref[...]).astype(low)
+
+        query, key = turned(0), turned(1)
+        value = raw_ref[:, pl.ds(pl.multiple_of(2 * width + head * HD, HD), HD)].astype(low)
+        scores = lax.dot_general(
+            query, key, (((1,), (1,)), ((), ())), preferred_element_type=full
+        ) * scale
+        scores = jnp.where(seen_ref[...] > 0.0, scores, MASKED)
+        expo = jnp.exp(scores - jnp.max(scores, axis=-1, keepdims=True))
+        probs = expo / jnp.sum(expo, axis=-1, keepdims=True)
+        prob_ref[0] = probs
+        out_ref[...] = jnp.dot(probs.astype(low), value, preferred_element_type=full).astype(low)
+        query_ref[...], key_ref[...], value_ref[...] = query, key, value
+
+    def whole(shape):
+        return pl.BlockSpec(shape, lambda h: (0,) * len(shape))
+
+    part = pl.BlockSpec((length, HD), lambda h: (0, h))
+    flat = jax.ShapeDtypeStruct((length, width), low)
+    return pl.pallas_call(
+        body,
+        grid=(heads,),
+        in_specs=[
+            whole(projected.shape), whole(gains.shape), whole((length, HD)), whole((length, HD)),
+            whole((length, 1)), whole((1, length)),
+        ],
+        out_specs=[part, part, part, part,
+                   pl.BlockSpec((1, length, length), lambda h: (h, 0, 0)), whole((length, LANES))],
+        out_shape=[flat, flat, flat, flat,
+                   jax.ShapeDtypeStruct((heads, length, length), full),
+                   jax.ShapeDtypeStruct((length, LANES), full)],
+        scratch_shapes=[pltpu.VMEM((length, length), full)],
+        compiler_params=pltpu.CompilerParams(vmem_limit_bytes=40 << 20),
+        cost_estimate=pl.CostEstimate(
+            flops=4 * heads * length * length * HD,
+            bytes_accessed=4 * projected.size + 8 * length * width + 4 * heads * length * length,
+            transcendentals=heads * length * length,
+        ),
+    )(projected, gains, *tables, doc_ids.reshape(length, 1), doc_ids.reshape(1, length))
+
+
+def attention_back(grad_out, query, key, value, probs, projected, inverses, gains, tables, heads):
+    length, width = grad_out.shape
+    low, full = jnp.bfloat16, jnp.float32
+    scale = HD ** (-0.5)
+
+    def body(grad_ref, query_ref, key_ref, value_ref, prob_ref, raw_ref, inv_ref, gain_ref,
+             cos_ref, sin_ref, dq_ref, dk_ref, dv_ref, dgain_ref, turned_ref, inner_ref):
+        head = pl.program_id(0)
+        here = pl.multiple_of(head * HD, HD)
+        grad, probs = grad_ref[...], prob_ref[0]
+        grad_probs = lax.dot_general(
+            grad, value_ref[...], (((1,), (1,)), ((), ())), preferred_element_type=full
+        )
+        dv_ref[...] = lax.dot_general(
+            probs.astype(low), grad, (((0,), (0,)), ((), ())), preferred_element_type=full
+        ).astype(low)
+        inner = jnp.sum(probs * grad_probs, axis=-1, keepdims=True)
+        grad_scores = (probs * (grad_probs - inner)).astype(low)
+        rotated = (
+            jnp.dot(grad_scores, key_ref[...], preferred_element_type=full) * scale,
+            lax.dot_general(
+                grad_scores, query_ref[...], (((0,), (0,)), ((), ())), preferred_element_type=full
+            ) * scale,
+        )
+
+        @pl.when(head == 0)
+        def _():
+            inner_ref[...] = jnp.zeros_like(inner_ref)
+
+        for i in (0, 1):
+            back = rotated[i] * cos_ref[...] - pltpu.roll(rotated[i], HD // 2, 1) * sin_ref[...]
+            at = pl.ds(pl.multiple_of(i * width + head * HD, HD), HD)
+            turned_ref[:, at] = back
+            normed = raw_ref[:, at] * inv_ref[:, i : i + 1]
+            dgain_ref[i : i + 1, pl.ds(here, HD)] = jnp.sum(back * normed, axis=0, keepdims=True)
+            weighed = back * gain_ref[i + 1 : i + 2, pl.ds(here, HD)]
+            inner_ref[:, i : i + 1] += jnp.sum(weighed * normed, axis=-1, keepdims=True)
+
+        @pl.when(head == heads - 1)
+        def _():
+            for i, out_ref in ((0, dq_ref), (1, dk_ref)):
+                inverse = inv_ref[:, i : i + 1]
+                inner = inner_ref[:, i : i + 1] * (1.0 / width)
+
+                @pl.loop(0, heads)
+                def _(j):
+                    at = pl.ds(pl.multiple_of(i * width + j * HD, HD), HD)
+                    there = pl.ds(pl.multiple_of(j * HD, HD), HD)
+                    weighed = turned_ref[:, at] * gain_ref[i + 1 : i + 2, there]
+                    normed = raw_ref[:, at] * inverse
+                    out_ref[:, there] = (inverse * (weighed - normed * inner)).astype(low)
+
+    def whole(shape):
+        return pl.BlockSpec(shape, lambda h: (0,) * len(shape))
+
+    part = pl.BlockSpec((length, HD), lambda h: (0, h))
+    flat = jax.ShapeDtypeStruct((length, width), low)
+    return pl.pallas_call(
+        body,
+        grid=(heads,),
+        in_specs=[
+            part, part, part, part,
+            pl.BlockSpec((1, length, length), lambda h: (h, 0, 0)),
+            whole((length, 2 * width)), whole(inverses.shape), whole(gains.shape),
+            whole((length, HD)), whole((length, HD)),
+        ],
+        out_specs=[whole((length, width)), whole((length, width)), part, whole((8, width))],
+        out_shape=[flat, flat, flat, jax.ShapeDtypeStruct((8, width), full)],
+        scratch_shapes=[pltpu.VMEM((length, 2 * width), full), pltpu.VMEM((length, LANES), full)],
+        compiler_params=pltpu.CompilerParams(vmem_limit_bytes=40 << 20),
+        cost_estimate=pl.CostEstimate(
+            flops=8 * heads * length * length * HD,
+            bytes_accessed=8 * length * width + 14 * length * width + 4 * heads * length * length,
+            transcendentals=0,
+        ),
+    )(grad_out, query, key, value, probs, projected, inverses, gains, *tables)
+
+
+BESIDE = pl.CostEstimate(flops=1, bytes_accessed=1, transcendentals=0)
+
+
+def expert_back(cot, gate, result, pre_gate, pre_up, gate_w, up_w, down_w, own):
+    total, width = cot.shape
+    rows = min(512, total)
+    hidden = pre_gate.shape[1]
+    low, full = jnp.bfloat16, jnp.float32
+    tile = min(512, hidden)
+
+    def body(own_ref, cot_ref, gate_ref, result_ref, a_ref, b_ref, gate_w_ref, up_w_ref, down_w_ref,
+             back_ref, grad_y_ref, grad_a_ref, grad_b_ref, sum_ref):
+        step = pl.program_id(1)
+
+        @pl.when(step == 0)
+        def _():
+            cot_f = cot_ref[...].astype(full)
+            grad_y_ref[...] = (gate_ref[...] * cot_f).astype(low)
+            grad_g = jnp.sum(cot_f * result_ref[...].astype(full), axis=-1, keepdims=True)
+            high = grad_g.astype(low).astype(full)
+            lanes = lax.broadcasted_iota(jnp.int32, (rows, LANES), 1)
+            tail = jnp.where(lanes == own_ref[0], high, 0.0)
+            tail = jnp.where(lanes == own_ref[0] + LANES // 2, grad_g - high, tail)
+            back_ref[:, width:] = tail.astype(low)
+            sum_ref[...] = jnp.zeros_like(sum_ref)
+
+        grad_act = lax.dot_general(
+            grad_y_ref[...], down_w_ref[...], (((1,), (1,)), ((), ())), preferred_element_type=full
+        )
+        pre_gate, pre_up = a_ref[...], b_ref[...]
+        sigmoid_g = jax.nn.sigmoid(pre_gate)
+        slope = sigmoid_g * (1.0 + pre_gate * (1.0 - sigmoid_g))
+        grad_a = (grad_act * pre_up * slope).astype(low)
+        grad_b = (grad_act * (pre_gate * sigmoid_g)).astype(low)
+        grad_a_ref[...], grad_b_ref[...] = grad_a, grad_b
+        contract = (((1,), (1,)), ((), ()))
+        sum_ref[...] += lax.dot_general(
+            grad_a, gate_w_ref[...], contract, preferred_element_type=full
+        ) + lax.dot_general(grad_b, up_w_ref[...], contract, preferred_element_type=full)
+
+        @pl.when(step == hidden // tile - 1)
+        def _():
+            back_ref[:, :width] = sum_ref[...].astype(low)
+
+    def whole(columns):
+        return pl.BlockSpec((rows, columns), lambda r, f: (r, 0))
+
+    inner = pl.BlockSpec((rows, tile), lambda r, f: (r, f))
+    into = pl.BlockSpec((width, tile), lambda r, f: (0, f))
+    return pl.pallas_call(
+        body,
+        grid=(total // rows, hidden // tile),
+        in_specs=[
+            pl.BlockSpec(memory_space=pltpu.SMEM),
+            whole(width), whole(1), whole(width), inner, inner, into, into,
+            pl.BlockSpec((tile, width), lambda r, f: (f, 0)),
+        ],
+        out_specs=[whole(width + LANES), whole(width), inner, inner],
+        out_shape=[
+            jax.ShapeDtypeStruct((total, width + LANES), low),
+            jax.ShapeDtypeStruct(cot.shape, low),
+            jax.ShapeDtypeStruct(pre_gate.shape, low),
+            jax.ShapeDtypeStruct(pre_gate.shape, low),
+        ],
+        scratch_shapes=[pltpu.VMEM((rows, width), full)],
+        compiler_params=pltpu.CompilerParams(vmem_limit_bytes=52 << 20),
+        cost_estimate=BESIDE,
+    )(own.reshape(1), cot, gate, result, pre_gate, pre_up, gate_w, up_w, down_w)
+
+
+def rows_product(lefts, rights):
+    rows, height = lefts[0].shape
+    width = rights[0].shape[1]
+    tile = min(512, height)
+
+    def body(*refs):
+        out_ref = refs[-1]
+        total = None
+        for left_ref, right_ref in zip(refs[: len(lefts)], refs[len(lefts) : -1], strict=True):
+            term = lax.dot_general(
+                left_ref[...], right_ref[...], (((0,), (0,)), ((), ())),
+                preferred_element_type=jnp.float32,
+            )
+            total = term if total is None else total + term
+        out_ref[...] = total
+
+    return pl.pallas_call(
+        body,
+        grid=(height // tile,),
+        in_specs=[pl.BlockSpec((rows, tile), lambda i: (0, i))] * len(lefts)
+        + [pl.BlockSpec((rows, width), lambda i: (0, 0))] * len(rights),
+        out_specs=pl.BlockSpec((tile, width), lambda i: (i, 0)),
+        out_shape=jax.ShapeDtypeStruct((height, width), jnp.float32),
+        compiler_params=pltpu.CompilerParams(vmem_limit_bytes=52 << 20),
+        cost_estimate=BESIDE,
+    )(*lefts, *rights)
+
+
+def rope_tables(length):
+    half = HD // 2
+    freq = THETA ** (-(jnp.arange(half, dtype=jnp.float32) * 2.0) / HD)
+    angle = jnp.arange(length, dtype=jnp.float32)[:, None] * freq[None, :]
+    sine = jnp.sin(angle)
+    cosine = jnp.cos(angle)
+    return (
+        jnp.concatenate([cosine, cosine], axis=-1),
+        jnp.concatenate([-sine, sine], axis=-1),
+    )
 
 
 def on_device(
@@ -463,7 +705,7 @@
     weights = jnp.stack([w_query, w_key, w_value, w_out]).astype(bfloat)
     line, cot_line = Spread(here, weights), Spread(here, cotangent)
     half = weights.shape[0] // 2
-    got, pieces = [], []
+    raw, chunks, pieces = [], [], []
     projected = None
     depth = width // here.nz
     cot_rows, rows_cot = [None] * here.nz, [None] * here.nz
@@ -471,8 +713,16 @@
     def stacked(rows):
         return rows.reshape(-1, shard, width)
 
-    def share(blocks):
-        chunk = jnp.concatenate(blocks, axis=0).reshape(plane, *weights.shape)
+    def chunk_of(k):
+        if here.square:
+            at = 2 * half if k + 1 < here.nz else 0
+            blocks = [line.queue[k]] + [by[: 2 * half] for by in raw[k][:2]]
+            blocks += [by[at : at + half] for by in raw[k + 1][:2]]
+        else:
+            blocks = raw[k]
+        return jnp.concatenate(blocks, axis=0).reshape(plane, *weights.shape)
+
+    def share(chunk):
         return [chunk] + [here.other_core(chunk, s) for s in range(1, here.cores)]
 
     def project(k):
@@ -488,8 +738,8 @@
                 by_x.append(line.queue[k])
                 by_y.append(line.queue[k])
             if 0 < k <= here.nz:
-                by_x.append(got[k - 1][2][:half])
-                by_y.append(got[k - 1][1][half:])
+                by_x.append(raw[k - 1][1][:half])
+                by_y.append(raw[k - 1][0][half : 2 * half])
             if k >= here.nz:
                 by_x.append(stacked(cot_rows[k - here.nz][1]))
                 by_y.append(stacked(cot_rows[k - here.nz][2]))
@@ -501,13 +751,15 @@
         else:
             outs = cot_rows[k - here.nz]
         if k == 1:
+            outs, smalls, raw, line.queue = tie(outs, smalls, raw, line.queue)
             turned = jnp.stack(smalls).reshape(here.nz, -1)
             near = (here.z - here.queue_of(jnp.arange(here.nz))) % here.nz
             pick = (near[:, None] == jnp.arange(here.nz)[None, :]).astype(bfloat)
             turned = product(pick, turned).astype(bfloat).reshape(here.nz, -1, LANES)
             smalls, slots = turned[:, :shard], turned[:, shard:]
-        outs, smalls, got, pieces, line.queue, cot_line.queue, cot_rows, cotangent = tie(
-            outs, smalls, got, pieces, line.queue, cot_line.queue, cot_rows, cotangent
+            smalls = here.along_plane([smalls] * plane)
+        outs, smalls, slots, raw, chunks, line.queue, cot_line.queue, cot_rows, cotangent = tie(
+            outs, smalls, slots, raw, chunks, line.queue, cot_line.queue, cot_rows, cotangent
         )
         if here.square:
             ins = [here.shift_plane(outs[0], 0, 1), here.shift_plane(outs[1], 1, 0)]
@@ -519,9 +771,10 @@
         moving_cot = cot_line.step() if k >= here.nz - 1 else []
         if k == 1:
             spreads = [spread_of(part.reshape(experts, length)) for part in slots]
-            smalls = here.along_plane([smalls] * plane)
+        if k > 2:
+            pieces.append(share(chunks[k - 3]))
         if k > 1:
-            pieces.append(share(got[k - 2]))
+            chunks.append(chunk_of(k - 2))
         if k == 2:
             smalls = jnp.stack(smalls, axis=1)
             smalls = [smalls] + [here.other_core(smalls, s) for s in range(1, here.cores)]
@@ -535,83 +788,53 @@
             in_order = product(normed_in, arrival).astype(bfloat)
         if k > 2:
             projected = project(k - 3)
+        if k == 1:
+            both_w = jnp.concatenate([gate_w, up_w], axis=1)
+            spreads, both_w = tie(spreads, both_w)
         if k >= here.nz - 1 and k - here.nz + 1 < here.nz:
             at = k - here.nz + 1
             cot_rows[at] = rows_of(spreads[at], cot_line.queue[at])
-        ins, moving, moving_cot, smalls, projected, cot_rows, spreads = tie(
-            ins, moving, moving_cot, smalls, projected, cot_rows, spreads
+        ins, moving, moving_cot, smalls, projected, cot_rows, spreads, chunks = tie(
+            ins, moving, moving_cot, smalls, projected, cot_rows, spreads, chunks
         )
         line.land(moving)
         cot_line.land(moving_cot)
-        if here.square:
-            by_x, by_y = ins[:2]
-            if k < here.nz:
-                got.append([line.queue[k], by_x[: 2 * half], by_y[: 2 * half]])
-                by_x, by_y = by_x[2 * half :], by_y[2 * half :]
-            if 0 < k <= here.nz:
-                got[k - 1] += [by_x[:half], by_y[:half]]
-                by_x, by_y = by_x[half:], by_y[half:]
-            if k >= here.nz:
+        raw.append(ins)
+        if k >= here.nz:
+            rows_cot[k - here.nz] = ins
+            if here.square:
                 own = cot_rows[k - here.nz][0]
-                rows_cot[k - here.nz] = [own, by_x.reshape(own.shape), by_y.reshape(own.shape)]
-            if k > here.nz:
+                skip = half if k == here.nz else 0
+                rows_cot[k - here.nz] = [own] + [by[skip:].reshape(own.shape) for by in ins[:2]]
+            if here.square and k > here.nz:
                 for i in (0, 1):
                     rows_cot[i].append(ins[2][i * capacity : (i + 1) * capacity])
-        elif k < here.nz:
-            got.append(ins)
-        else:
-            rows_cot[k - here.nz] = ins
 
     order_x = here.target_order(width // here.cores, "x")
     order_y = here.target_order(width // here.cores, "y")
 
-    def targeted(value):
-        columns = here.own_columns(value)
+    def targeted(columns):
+        columns = jnp.concatenate(columns, axis=0)
         return [product(columns, o).astype(bfloat) for o in (order_x, order_y)]
 
+    merged = []
     if here.nz > 2:
-        cot_rows[2:], pieces, projected = tie(cot_rows[2:], pieces, projected)
-        rows_cot[2] = here.along_plane(cot_rows[2])
         cot_rows[3] = rows_of(spreads[3], cot_line.queue[3])
+        merged = [joined(pair) for pair in zip(*cot_rows[2:], strict=True)]
+    in_columns = here.core_columns(normed_in)
+    merged, chunks, projected, pieces, in_columns = tie(
+        merged, chunks, projected, pieces, in_columns
+    )
+    ins = here.along_plane(merged) if merged else []
+    pieces.append(share(chunks[-1]))
+    in_columns = here.to_cores(in_columns)
     projected = project(here.nz - 1)
     pieces = [piece for chunk in pieces for piece in chunk]
-    query_raw = projected[:, :width]
-    key_raw = projected[:, width : 2 * width]
-    values = projected[:, 2 * width :].astype(bfloat)
-    query_n, query_normed, query_inverse = norm_rows(query_raw, gains_f[1])
-    key_n, key_normed, key_inverse = norm_rows(key_raw, gains_f[2])
-    cosine, sine = rope_tables(length, HD)
-    query_rot = rotate(query_n.reshape(length, heads, HD), cosine, sine).astype(bfloat)
-    key_rot = rotate(key_n.reshape(length, heads, HD), cosine, sine).astype(bfloat)
-    if here.nz > 2:
-        targets = targeted(normed_in)
-        query_rot, key_rot, values, cot_rows[3], rows_cot[2], targets = tie(
-            query_rot, key_rot, values, cot_rows[3], rows_cot[2], targets
-        )
-        rows_cot[3] = here.along_plane(cot_rows[3])
-    else:
-        targets = targeted(normed_in)
-    value_heads = values.reshape(length, heads, HD)
-    doc_ids = segments[0]
-    visible = (doc_ids[:, None] == doc_ids[None, :]) & (places[:, None] >= places[None, :])
-    score_scale = HD ** (-0.5)
-    scores = (
-        jnp.einsum("qhd,khd->hqk", query_rot, key_rot, preferred_element_type=jnp.float32)
-        * score_scale
-    )
-    scores = jnp.where(visible[None], scores, MASKED)
-    row_max = jnp.max(scores, axis=-1, keepdims=True)
-    expo = jnp.exp(scores - row_max)
-    probs = expo / jnp.sum(expo, axis=-1, keepdims=True)
-    probs_low = probs.astype(bfloat)
-    attended = (
-        jnp.einsum("hqk,khd->qhd", probs_low, value_heads, preferred_element_type=jnp.float32)
-        .reshape(length, width)
-        .astype(bfloat)
-    )
-    residual = inputs + times_gathered(
-        product(attended, arrival).astype(bfloat), pieces, 3, 4
-    )
+    tables = rope_tables(length)
+    query_rot, key_rot, values, attended, probs, inverses = attention(
+        projected, gains_f, tables, segments[0], heads
+    )
+    residual = inputs + times_gathered(product(attended, arrival).astype(bfloat), pieces, 3, 4)
     normed_mid_f, normed_two, inverse_two = norm_rows(residual, gains_f[3])
     normed_mid = normed_mid_f.astype(bfloat)
 
@@ -629,44 +852,39 @@
         return (gate, pre_gate, pre_up, activated, result, gated)
 
     def expert_backward(kept, cot):
-        gate, pre_gate, pre_up, activated, result, _ = kept
-        cot_f, result_f = cot.astype(jnp.float32), result.astype(jnp.float32)
-        grad_y = (gate * cot_f).astype(bfloat)
-        grad_g = jnp.sum(cot_f * result_f, axis=-1, keepdims=True)
-        grad_act = contract_cols(grad_y, down_w)
-        sigmoid_g = jax.nn.sigmoid(pre_gate)
-        slope = sigmoid_g * (1.0 + pre_gate * (1.0 - sigmoid_g))
-        grad_a = (grad_act * pre_up * slope).astype(bfloat)
-        grad_b = (grad_act * (pre_gate * sigmoid_g)).astype(bfloat)
-        grad_e = contract_cols(grad_a, gate_w) + contract_cols(grad_b, up_w)
-        high = grad_g.astype(bfloat)
-        low = (grad_g - high.astype(jnp.float32)).astype(bfloat)
-        lanes = jnp.arange(LANES, dtype=jnp.int32)[None, :]
-        tail = jnp.where(lanes == here.me, high, jnp.zeros((), bfloat))
-        tail = jnp.where(lanes == here.me + LANES // 2, low, tail)
-        back = jnp.concatenate([grad_e.astype(bfloat), tail], axis=1)
-        return (back, grad_y, grad_a, grad_b)
+        gate, pre_gate, pre_up, _, result, _ = kept
+        return expert_back(cot, gate, result, pre_gate, pre_up, gate_w, up_w, down_w, here.me)
 
     rows_next = rows_of(spreads[0], normed_mid)
-    normed_mid, rows_next, rows_cot[-1] = tie(normed_mid, rows_next, rows_cot[-1])
+    out_columns = here.core_columns(attended)
+    normed_mid, rows_next, ins, in_columns, out_columns = tie(
+        normed_mid, rows_next, ins, in_columns, out_columns
+    )
+    if here.nz > 2:
+        rows_cot[2:] = [[row[i : i + capacity] for row in ins] for i in (0, capacity)]
     line = Spread(here, normed_mid)
     rows_in, forward = [], []
     for k in order:
         if k > 0:
             rows_next = rows_of(spreads[k], line.queue[k])
-        rows_next, rows_in, line.queue = tie(rows_next, rows_in, line.queue)
+        rows_next, rows_in, line.queue, out_columns = tie(
+            rows_next, rows_in, line.queue, out_columns
+        )
         moving = line.step()
         rows = here.along_plane(rows_next)
         if k > 0:
             rows_in[-1] = joined(rows_in[-1])
             forward.append(expert_forward(rows_in[-1]))
+        if k == 0:
+            targets = targeted(in_columns)
+            rows, targets = tie(rows, targets)
         if k == here.nz // 2:
-            targets_out = targeted(attended)
-            rows, targets_out = tie(rows, targets_out)
-        moving, rows, forward = tie(moving, rows, forward)
+            out_columns = here.to_cores(out_columns)
+        moving, rows, forward, out_columns = tie(moving, rows, forward, out_columns)
         rows_in.append(rows)
         line.land(moving)
 
+    targets_out = targeted(out_columns)
     half = here.nz // 2
     back_y = [None] * here.nz
     backward = [None] * here.nz
@@ -680,50 +898,60 @@
         elif k is not None:
             backward[k] = expert_backward(forward[k], joined(rows_cot[k]))
 
-    for k in order[:half]:
-        rows_next = parted(forward[k][5])
-        rows_next, forward, backward, rows_in, rows_cot = tie(
-            rows_next, forward, backward, rows_in, rows_cot
+    rows_next = parted(forward[0][5])
+    rows_next, forward, rows_in, rows_cot, out_columns = tie(
+        rows_next, forward, rows_in, rows_cot, out_columns
+    )
+    rows = here.deal_back(rows_next)
+    work()
+    work()
+    rows, forward, backward = tie(rows, forward, backward)
+    back_y[0] = rows
+    collect, parts = Collect(here), [None] * here.nz
+    moving, sending, back = [], [], None
+    for k in reversed(order):
+        rows_next = parted(backward[k][0])
+        if k + 2 < here.nz:
+            collect.land(moving)
+            sending = collect.add(k + 2, parts[k + 2])
+        rows_next, sending, forward, backward, back = tie(
+            rows_next, sending, forward, backward, back
         )
         rows = here.deal_back(rows_next)
-        work()
-        rows, forward, backward = tie(rows, forward, backward)
-        back_y[k] = rows
-    collect = Collect(here)
-    moving, back = [], None
-    for k in reversed(order):
-        if backward[k] is None:
-            work()
-        rows_next = parted(backward[k][0])
-        rows_next, forward, backward, moving, back = tie(
-            rows_next, forward, backward, moving, back
-        )
-        rows = here.deal_back(rows_next)
-        if back is not None:
-            collect.land(moving)
-            moving = collect.add(k + 1, contract_rows(spreads[k + 1], joined(back)))
-            if k == 0:
-                arrived, activated = joined(rows_in), joined([kept[3] for kept in forward])
-                grad_y, grad_a, grad_b = [
-                    joined([kept[i] for kept in backward]) for i in (1, 2, 3)
-                ]
-                moving, activated, grad_y, arrived, grad_a, grad_b = tie(
-                    moving, activated, grad_y, arrived, grad_a, grad_b
-                )
-            moving = collect.send(moving)
+        moving = collect.send(sending)
         if k > 0:
             work()
-            moving, rows, forward, backward = tie(moving, rows, forward, backward)
         else:
-            grad_down = contract_rows(activated, grad_y)
-            moving, rows, grad_down = tie(moving, rows, grad_down)
+            grad_down = rows_product(
+                [kept[3] for kept in forward], [kept[1] for kept in backward]
+            )
+            rows, grad_down = tie(rows, grad_down)
+        if back is not None:
+            parts[k + 1] = contract_rows(spreads[k + 1], joined(back))
+        moving, rows, forward, backward, parts = tie(moving, rows, forward, backward, parts)
         back = rows
+    late = list(order[:0:-1])
     collect.land(moving)
-    rows_next = parted(forward[-1][5])
-    back, rows_next = tie(back, rows_next)
-    collect.add(0, contract_rows(spreads[0], joined(back)))
+    sending = collect.add(1, parts[1])
+    rows_next = parted(forward[late[0]][5])
+    rows_next, sending, back = tie(rows_next, sending, back)
+    rows = here.deal_back(rows_next)
+    moving = collect.send(sending)
+    parts[0] = contract_rows(spreads[0], joined(back))
+    rows_next = [parted(forward[k][5]) for k in late[1:]]
+    moving, rows, parts, rows_next = tie(moving, rows, parts, rows_next)
+    collect.land(moving)
+    collect.add(0, parts[0])
     returned = collect.total
-    rows_y = here.deal_back(rows_next)
+    back_y[late[0]] = rows
+    parts_y = [None] * here.nz
+    if rows_next:
+        back_y[late[1]] = here.deal_back(rows_next[0])
+
+    def add_up_y(k):
+        parts_y[k] = contract_rows(spreads[k], joined(back_y[k]))
+
+    add_up_y(late[0])
 
     grad_mid = returned[:, :width]
     grad_route = (
@@ -739,47 +967,33 @@
     grad_res_two, grad_gain_mid = norm_back(grad_mid, gains_f[3], normed_two, inverse_two)
     grad_residual = cotangent.astype(jnp.float32) + grad_res_two
     grad_attn = grad_residual.astype(bfloat)
-    out_tokens = here.all_tokens(grad_attn)
     grad_attended = times_transposed(grad_attn, pieces, 3, 4).astype(bfloat)
     grad_attended = contract_cols(grad_attended, arrival).astype(bfloat)
-    terms = here.scatter_terms(*targets_out, out_tokens)
-    rows_next = [parted(forward[k][5]) for k in order[half : here.nz - 1]]
-    grad_attended, terms, rows_y, rows_next = tie(grad_attended, terms, rows_y, rows_next)
-    back_y[-1] = rows_y
-
     collect_y, adds_y = Collect(here), list(reversed(order))
-
-    def next_y():
-        if not adds_y:
-            return []
-        k = adds_y.pop(0)
-        return collect_y.add(k, contract_rows(spreads[k], joined(back_y[k])))
-
-    sending_y = next_y()
-    sending_y, rows_next, grad_attended = tie(sending_y, rows_next, grad_attended)
-    for k in reversed(order[half : here.nz - 1]):
-        back_y[k] = here.deal_back(rows_next[k - half])
+    grad_attended, grad_attn, back_y, parts_y = tie(grad_attended, grad_attn, back_y, parts_y)
+    sending_y = collect_y.add(adds_y[0], parts_y[adds_y.pop(0)])
+    sending_y, grad_attended, grad_attn, back_y, rows_next = tie(
+        sending_y, grad_attended, grad_attn, back_y, rows_next
+    )
+    if rows_next:
+        back_y[late[2]] = here.deal_back(rows_next[1])
     moving = collect_y.send(sending_y)
-    grad_attended = grad_attended.reshape(length, heads, HD)
-    grad_probs = jnp.einsum(
-        "qhd,khd->hqk", grad_attended, value_heads, preferred_element_type=jnp.float32
-    )
-    grad_values = jnp.einsum(
-        "hqk,qhd->khd", probs_low, grad_attended, preferred_element_type=jnp.float32
-    )
-    grad_values = grad_values.reshape(length, width).astype(bfloat)
-    inner = jnp.sum(probs * grad_probs, axis=-1, keepdims=True)
-    grad_scores = (probs * (grad_probs - inner)).astype(bfloat)
-    right = here.all_tokens(grad_values)
-    grad_scores, grad_values, right, moving, back_y = tie(
-        grad_scores, grad_values, right, moving, back_y
-    )
-    collect_y.land(moving)
-
-    def leave(terms, sums, more_x, more_y):
+    out_tokens = here.all_tokens(grad_attn)
+    grad_query, grad_key, grad_values, grad_gain_heads = attention_back(
+        grad_attended, query_rot, key_rot, values, probs, projected, inverses, gains_f, tables, heads
+    )
+    far = here.scatter_far(*targets_out, out_tokens)
+    grads = jnp.stack([grad_values, grad_key, grad_query])
+    for k in [0, *late[1:2]]:
+        add_up_y(k)
+    grads, far, back_y, parts_y, moving, out_tokens = tie(
+        grads, far, back_y, parts_y, moving, out_tokens
+    )
+
+    def leave(far, sums, more_x, more_y):
         if not here.square:
-            return list(terms)
-        by_x, by_y = list(terms[:1]), list(terms[1:2])
+            return list(far)
+        by_x, by_y = list(far[:1]), list(far[1:])
         if sums:
             by_x.append(sums[1])
             by_y.append(sums[0])
@@ -790,36 +1004,12 @@
             return here.along_plane(outs) if outs else []
         return [here.shift_plane(outs[0], 0, 1), here.shift_plane(outs[1], 1, 0)]
 
-    sending_y = next_y()
-    outs = leave(terms, [], [], [])
-    near, near_last = terms[2:], []
-    outs, sending_y, grad_scores, right = tie(outs, sending_y, grad_scores, right)
-    ins = arrive(outs)
-    moving = collect_y.send(sending_y)
-    terms = here.scatter_terms(*targets, right)
-    grad_query_rot = (
-        jnp.einsum("hqk,khd->qhd", grad_scores, key_rot, preferred_element_type=jnp.float32)
-        * score_scale
-    )
-    grad_key_rot = (
-        jnp.einsum("hqk,qhd->khd", grad_scores, query_rot, preferred_element_type=jnp.float32)
-        * score_scale
-    )
-    grad_query_n = rotate_back(grad_query_rot, cosine, sine).reshape(length, width)
-    grad_key_n = rotate_back(grad_key_rot, cosine, sine).reshape(length, width)
-    grad_query_f, grad_gain_query = norm_back(grad_query_n, gains_f[1], query_normed, query_inverse)
-    grad_key_f, grad_gain_key = norm_back(grad_key_n, gains_f[2], key_normed, key_inverse)
-    grad_query = grad_query_f.astype(bfloat)
-    grad_key = grad_key_f.astype(bfloat)
-
-    grad_query, grad_key, terms, ins, moving = tie(grad_query, grad_key, terms, ins, moving)
-    expert_sums = [(arrived, grad_a), (arrived, grad_b)]
+    jobs = 4
+    lefts, rights = [targets_out, targets, targets, targets], [out_tokens]
     firsts, lasts, shares = [], [], []
-    small_rows = 4 + experts
-    jobs, small = 4, [None]
-    for i in range(1, jobs + 2):
-        collect_y.land(moving)
-        if here.square:
+    near, near_last, ins, small, smalls, expert_grads = [], [], [], [None], [], []
+    for i in range(jobs + 2):
+        if here.square and i > 0:
             by_x, by_y = ins
             if i <= jobs:
                 rows = near[0].shape[0]
@@ -829,104 +1019,110 @@
                 rows = near_last[0].shape[0]
                 lasts.append([by_y[:rows], by_x[:rows], *near_last])
                 by_x, by_y = by_x[rows:], by_y[rows:]
-        elif i <= jobs:
+        elif 0 < i <= jobs:
             lasts.append(ins)
         sums, parts, more_x, more_y, outs = [], [], [], [], []
         if here.square:
-            sums = here.scatter_sums(firsts[i - 1]) if i <= jobs else []
+            sums = here.scatter_sums(firsts[i - 1]) if 0 < i <= jobs else []
+            near_last = sums[2:]
             columns = small[0].shape[1] // 2 if small[0] is not None else 0
-            if i == 3:
+            if i == 2:
                 more_x = [small[0][:, columns:].astype(bfloat).reshape(-1, width // 2)]
                 small = [small[0][:, :columns]]
-            elif i == 4:
-                got_small = by_x.reshape(small[0].shape).astype(jnp.float32)
-                small = [small[0] + got_small]
+            elif i == 3:
+                small = [small[0] + by_x.reshape(small[0].shape).astype(jnp.float32)]
                 more_y = [small[0][:, columns:].astype(bfloat).reshape(-1, width // 2)]
                 small = [small[0][:, :columns]]
-            elif i == 5:
+            elif i == 4:
                 small = [small[0] + by_y.reshape(small[0].shape).astype(jnp.float32)]
             if i < jobs:
-                near = terms[2:]
-                outs = leave(terms, sums, more_x, more_y)
+                outs = leave(far, sums, more_x, more_y)
             elif i == jobs:
-                outs = [
-                    jnp.concatenate([sums[1], *more_x], axis=0),
-                    jnp.concatenate([sums[0], *more_y], axis=0),
-                ]
-            near_last = sums[2:]
+                outs = [sums[1], sums[0]]
         elif i < jobs:
-            outs = leave(terms, [], [], [])
+            outs = leave(far, [], [], [])
         at = i - 2 if here.square else i - 1
         if 0 <= at < jobs:
             parts = here.line_parts(lasts[at])
-            if here.square and at == jobs - 1:
-                flat = [
-                    piece.reshape(-1, width)
-                    for piece in jnp.split(small[0], here.nz, axis=1)
+            if here.square and i == 4:
+                parts = [
+                    jnp.concatenate([part, piece.reshape(-1, width).astype(part.dtype)], axis=0)
+                    for part, piece in zip(
+                        parts, jnp.split(small[0], here.nz, axis=1), strict=True
+                    )
                 ]
-                parts = [
-                    jnp.concatenate([part, piece.astype(part.dtype)], axis=0)
-                    for part, piece in zip(parts, flat, strict=True)
-                ]
-        sending_y = next_y()
-        outs, parts, sending_y, terms, expert_sums, near, near_last, small = tie(
-            outs, parts, sending_y, terms, expert_sums, near, near_last, small
+        sending_y = []
+        if adds_y:
+            collect_y.land(moving)
+            sending_y = collect_y.add(adds_y[0], parts_y[adds_y.pop(0)])
+        outs, parts, sending_y, near_last, small, rights, smalls, grads, back_y, rows_in = tie(
+            outs, parts, sending_y, near_last, small, rights, smalls, grads, back_y, rows_in
         )
         ins = arrive(outs) if outs else []
         if parts:
             parts = here.along_whole_line(parts)
-        moving = collect_y.send(sending_y)
-        if i == 1:
-            both = jnp.stack([grad_key, grad_query])
-            others = [here.other_core(both, step) for step in range(1, here.cores)]
-            rights = [jnp.concatenate([v[j] for v in [both, *others]], axis=0) for j in (0, 1)]
+        moving = collect_y.send(sending_y) if sending_y else []
+        if here.square and i == 5:
+            smalls = here.to_cores(smalls)
+        if i < jobs:
+            near = here.scatter_near(*lefts[i], rights[i])
+        if i == 0:
+            others = [here.other_core(grads, step) for step in range(1, here.cores)]
+            rights += [jnp.concatenate([v[j] for v in [grads, *others]], axis=0) for j in range(3)]
+        if i + 1 < jobs:
+            far = here.scatter_far(*lefts[i + 1], rights[i + 1])
+        if i == 0:
             grad_in_norm = times_transposed(
-                jnp.concatenate([grad_query, grad_key, grad_values], axis=1), pieces, 0, 3
+                jnp.concatenate([grads[2], grads[1], grads[0]], axis=1), pieces, 0, 3
             )
             high = grad_in_norm.astype(bfloat)
             low = (grad_in_norm - high.astype(jnp.float32)).astype(bfloat)
+            high, low, ins = tie(high, low, ins)
+        if i == 1:
             grad_in_norm = contract_cols(high, arrival) + contract_cols(low, arrival)
             grad_res_one, grad_gain_in = norm_back(
                 grad_in_norm, gains_f[0], normed_one, inverse_one
             )
             grad_tokens = (grad_residual + grad_res_one).astype(bfloat)
+            small_rows = 4 + experts
             smalls = jnp.concatenate(
                 [
-                    jnp.stack(
-                        [grad_gain_in, grad_gain_query, grad_gain_key, grad_gain_mid], axis=0
-                    ),
+                    grad_gain_in[None],
+                    grad_gain_heads[:2],
+                    grad_gain_mid[None],
                     grad_router.T,
                     jnp.zeros((-small_rows % 32, width), jnp.float32),
                 ],
                 axis=0,
             )
             if here.square:
-                rows = smalls.shape[0]
-                smalls = here.own_columns(smalls)
-                smalls = sum(smalls[c * rows : (c + 1) * rows] for c in range(here.cores))
+                smalls = jnp.concatenate(here.core_columns(smalls), axis=0)
                 small = [product(smalls.astype(bfloat), order_x)]
-            else:
-                smalls = lax.psum(smalls, ("dp", "expert"))
-                smalls = lax.dynamic_slice(
-                    smalls,
-                    (0, (here.core * here.count + here.me) * shard),
-                    (smalls.shape[0], shard),
-                )
-            ins, grad_tokens, small, rights = tie(ins, grad_tokens, small, rights)
-        if i < jobs - 1:
-            terms = here.scatter_terms(*targets, rights[i - 1])
-        if 1 < i < 4:
-            grad = contract_rows(*expert_sums[i - 2])
-            ins, expert_sums[i - 2] = tie(ins, grad)
-        ins, parts, moving, terms = tie(ins, parts, moving, terms)
+            grad_tokens, small, smalls, ins = tie(grad_tokens, small, smalls, ins)
+        if i == 0 and len(late) > 2:
+            add_up_y(late[2])
+        if 2 <= i <= 3:
+            grad = rows_product(rows_in, [kept[i] for kept in backward])
+            expert_grads.append(grad)
+            ins, expert_grads = tie(ins, expert_grads)
+        ins, parts, moving, far, near, rights, smalls, parts_y = tie(
+            ins, parts, moving, far, near, rights, smalls, parts_y
+        )
         if parts:
-            shares.append(sum(part.astype(jnp.float32) for part in parts))
+            share = sum(part.astype(jnp.float32) for part in parts)
+            if here.square and i == 4:
+                smalls = jnp.split(share[shard:].reshape(-1, shard), here.cores, axis=0)
+            shares.append(share[:shard])
     if here.square:
-        smalls = shares[-1][shard:].reshape(-1, shard)
-        shares[-1] = shares[-1][:shard]
+        smalls = sum(smalls)
+    else:
+        smalls = lax.psum(smalls, ("dp", "expert"))
+        smalls = lax.dynamic_slice(
+            smalls, (0, (here.core * here.count + here.me) * shard), (smalls.shape[0], shard)
+        )
     mixed = (residual + collect_y.total).astype(bfloat)
     grad_wo, grad_wv, grad_wk, grad_wq = shares
-    grad_gate_w, grad_up_w = expert_sums
+    grad_gate_w, grad_up_w = expert_grads
     return (
         mixed,
         grad_tokens,

time: 1050 us -> 932 us (0.89); the launches traced: 1050 us -> 916 us
  Pallas kernels: 56.6 us -> 204 us
  waiting for transfers between devices: 337 us -> 201 us
  matrix products: 257 us -> 128 us
  starting transfers between devices: 164 us -> 188 us
  local copies, waits for them, and re-layouts: 109 us -> 88.6 us
  other arithmetic: 119 us -> 101 us
    pallas_call x0 -> x9, Pallas kernels: none -> 149 us  [the longest x4 68.1 us: expert_back(): pl.pallas_call(body, grid=(total // rows, hidden // tile), in_specs=[pl.B...]
    ppermute x68 -> x65, waiting for transfers between devices: 237 us -> 147 us  [shift_plane(): return lax.ppermute(value, 'expert', pairs)]
    dot_general x16 -> x4, matrix products: 88.2 us -> 12.7 us  [contract_cols(): lax.dot_general(left, right, (((1,), (1,)), ((), ())), preferred_element_...]
    ppermute x40, waiting for transfers between devices: 96.8 us -> 53.9 us  [along_line(): return lax.ppermute(value, 'expert', pairs)]
    dot_general x29 -> x26, matrix products: 82.5 us -> 40.5 us  [contract_rows(): lax.dot_general(left, right, (((0,), (0,)), ((), ())), preferred_element_...]
    slice x20 -> x16, local copies, waits for them, and re-layouts: 31.4 us -> 10.3 us  [the longest x4 4.34 us: on_device(): rows_cot[2:] = [[row[i:i + capacity] for row in ins] for i in (0, capacity)]]
    ppermute x11 -> x10, starting transfers between devices: 39.7 us -> 58.8 us  [other_core(): return lax.ppermute(value, 'dp', pairs)]
    ppermute x68 -> x65, starting transfers between devices: 59.1 us -> 55.2 us  [shift_plane(): return lax.ppermute(value, 'expert', pairs)]
  transfers between devices with their start and end apart: 119 -> 115, of which waited for: 60 -> 41; matrix products, arithmetic and copies ran while one was open for 29% -> 21% of each run, Pallas kernels for 4% -> 22%
where the time goes in v2:
time: 932 us; the launch traced here: 916 us
  Pallas kernels  204 us (22%)
  waiting for transfers between devices  201 us (22%)
  starting transfers between devices  188 us (20%)
  matrix products  128 us (14%)
  other arithmetic  101 us (11%)
  local copies, waits for them, and re-layouts  88.6 us (10%)
    ppermute x65, waiting for transfers between devices, shift_plane(): return lax.ppermute(value, 'expert', pairs)  147 us
    dot_general x34, matrix products, product(): return jnp.dot(left, right, preferred_element_type=jnp.float32)  75 us
    ppermute x40, starting transfers between devices, along_line(): return lax.ppermute(value, 'expert', pairs)  74.4 us
    pallas_call x4, Pallas kernels, expert_back(): pl.pallas_call(body, grid=(total // rows, hidden // tile), in_specs=[pl.B...  68.1 us
    ppermute x10, starting transfers between devices, other_core(): return lax.ppermute(value, 'dp', pairs)  58.8 us
    ppermute x65, starting transfers between devices, shift_plane(): return lax.ppermute(value, 'expert', pairs)  55.2 us
    ppermute x40, waiting for transfers between devices, along_line(): return lax.ppermute(value, 'expert', pairs)  53.9 us
    pallas_call x3, Pallas kernels, rows_product(): pl.pallas_call(body, grid=(height // tile,), in_specs=[pl.BlockSpec((rows...  42.4 us
  transfers between devices with their start and end apart: 115, of which 41 were waited for; matrix products, arithmetic and copies ran while one was open for 21% of the time, Pallas kernels for 22%

profile of v2, /device:TPU:9, one launch (start us, length us, event | category | flops | bytes accessed | tf_op | source)
XLA Modules:
  0.0 916.0 jit_solution(8391704091252816414)
XLA Ops:
  20.2 11.4 %collective-permute-done.3 = bf16[4,64,2048]{2,1,0:T(8,128)(2,1)S(1)} collective-permute-done((bf16[4,64,2048]{2,1,0:T(8,128)(2,1)S(1)}, bf16[4,64,2048]{2,1,0:T(8,128)(2,1)S(1)}, u32[]{:S(2)}, u32[]{:S(2)}) %collective-permute-start.3) | collective-permute-done | bytes 1048608 | tf_op jit(solution)/shard_map/ppermute | solution.py:171
  56.9 10.3 %collective-permute-done.12 = bf16[4,64,2048]{2,1,0:T(8,128)(2,1)} collective-permute-done((bf16[4,64,2048]{2,1,0:T(8,128)(2,1)}, bf16[4,64,2048]{2,1,0:T(8,128)(2,1)}, u32[]{:S(2)}, u32[]{:S(2)}) %collective-permute-start.12) | collective-permute-done | bytes 1048608 | tf_op jit(solution)/shard_map/ppermute | solution.py:180
  83.8 7.4 collective-permute-start.17
  99.3 10.7 %collective-permute-done.14 = bf16[6,64,2048]{2,1,0:T(8,128)(2,1)S(1)} collective-permute-done((bf16[6,64,2048]{2,1,0:T(8,128)(2,1)S(1)}, bf16[6,64,2048]{2,1,0:T(8,128)(2,1)S(1)}, u32[]{:S(2)}, u32[]{:S(2)}) %collective-permute-start.14) | collective-permute-done | bytes 1572896 | tf_op jit(solution)/shard_map/ppermute | solution.py:171
  122.8 9.1 collective-permute-start.22
  141.0 5.5 shard_map.230.refs_2_
  152.5 8.9 collective-permute-start.27
  176.7 8.7 shard_map.231.refs_2_
  211.0 9.2 %shard_map.232.refs_2_ = f32[256,6144]{1,0:T(8,128)} custom-call(bf16[256,512]{1,0:T(8,128)(2,1)S(1)} %get-tuple-element.1775.left_ref, bf16[4,4,64,2048]{3,2,1,0:T(8,128)(2,1)} %bitcast.36.refs_0_.refs_4_, bf16[4,4,64,2048]{3,2,1,0:T(8,128)(2,1)} %collective-permute-done.32.refs_1_.refs_5_, f32[256,6144]{1,0:T(8,128)} %shard_map.231.refs_2_), custom_call_target="tpu_custom_call" | custom-call | flops 1610612736 | bytes 18874368 | tf_op jit(solution)/shard_map/pallas_call | solution.py:329
  220.3 16.2 %collective-permute-done.30 = bf16[256,2048]{1,0:T(8,128)(2,1)S(1)} collective-permute-done((bf16[256,2048]{1,0:T(8,128)(2,1)}, bf16[256,2048]{1,0:T(8,128)(2,1)S(1)}, u32[]{:S(2)}, u32[]{:S(2)}) %collective-permute-start.30) | collective-permute-done | bytes 1048608 | tf_op jit(solution)/shard_map/ppermute | solution.py:171
  248.9 9.2 %shard_map.233.raw_ref = f32[256,6144]{1,0:T(8,128)} custom-call(bf16[256,512]{1,0:T(8,128)(2,1)S(1)} %get-tuple-element.1778.left_ref, bf16[4,4,64,2048]{3,2,1,0:T(8,128)(2,1)} %bitcast.39.refs_0_.refs_6_, bf16[4,4,64,2048]{3,2,1,0:T(8,128)(2,1)} %collective-permute-done.33.refs_1_.refs_7_, f32[256,6144]{1,0:T(8,128)} %shard_map.232.refs_2_), custom_call_target="tpu_custom_call" | custom-call | flops 1610612736 | bytes 18874368 | tf_op jit(solution)/shard_map/pallas_call | solution.py:329
  258.2 15.8 %shard_map.234 = (bf16[256,2048]{1,0:T(8,128)(2,1)S(1)}, bf16[256,2048]{1,0:T(8,128)(2,1)S(1)}, bf16[256,2048]{1,0:T(8,128)(2,1)S(1)}, bf16[256,2048]{1,0:T(8,12...) custom-call(f32[256,6144]{1,0:T(8,128)} %shard_map.233.raw_ref, ...), custom_call_target="tpu_custom_call" | custom-call | flops 536870912 | bytes 14680064 | tf_op jit(solution)/shard_map/pallas_call | solution.py:427
  309.4 9.4 %collective-permute-done.42 = bf16[128,2048]{1,0:T(8,128)(2,1)S(1)} collective-permute-done((bf16[128,2048]{1,0:T(8,128)(2,1)S(1)}, bf16[128,2048]{1,0:T(8,128)(2,1)S(1)}, u32[]{:S(2)}, u32[]{:S(2)}) %collective-permute-start.42) | collective-permute-done | bytes 524320 | tf_op jit(solution)/shard_map/ppermute | solution.py:171
  339.9 7.3 collective-permute-done.47
  394.3 5.6 collective-permute-done.55
  415.2 5.5 multiply_convert_fusion
  420.7 17.0 %shard_map.236 = (bf16[512,2176]{1,0:T(8,128)(2,1)}, bf16[512,2048]{1,0:T(8,128)(2,1)}, bf16[512,1024]{1,0:T(8,128)(2,1)S(1)}, bf16[512,1024]{1,0:T(8,128)(2,1)}) custom-call(s32[1]{0:T(128)} %bitcast.53.own_ref, bf16[512,2048]{1,0:T(8,128)(2,1)} %pad_maximum_fusion.7.cot_ref, f32[512,1]{1,0:T(8,128)S(1)} %copy.50.gate_ref, ...), custom_call_target="tpu_custom_call" | custom-call | flops 1 | bytes 1 | tf_op jit(solution)/shard_map/pallas_call | solution.py:576
  445.5 17.0 %shard_map.237 = (bf16[512,2176]{1,0:T(8,128)(2,1)}, bf16[512,2048]{1,0:T(8,128)(2,1)}, bf16[512,1024]{1,0:T(8,128)(2,1)S(1)}, bf16[512,1024]{1,0:T(8,128)(2,1)}) custom-call(s32[1]{0:T(128)} %bitcast.53.own_ref, bf16[512,2048]{1,0:T(8,128)(2,1)} %pad_maximum_fusion.8.cot_ref, f32[512,1]{1,0:T(8,128)S(1)} %copy.51.gate_ref, ...), custom_call_target="tpu_custom_call" | custom-call | flops 1 | bytes 1 | tf_op jit(solution)/shard_map/pallas_call | solution.py:576
  470.2 17.2 %shard_map.238 = (bf16[512,2176]{1,0:T(8,128)(2,1)}, bf16[512,2048]{1,0:T(8,128)(2,1)}, bf16[512,1024]{1,0:T(8,128)(2,1)S(1)}, bf16[512,1024]{1,0:T(8,128)(2,1)}) custom-call(s32[1]{0:T(128)} %bitcast.53.own_ref, bf16[512,2048]{1,0:T(8,128)(2,1)} %pad_maximum_fusion.9.cot_ref, f32[512,1]{1,0:T(8,128)S(1)} %copy.52.gate_ref, ...), custom_call_target="tpu_custom_call" | custom-call | flops 1 | bytes 1 | tf_op jit(solution)/shard_map/pallas_call | solution.py:576
  502.1 17.0 %shard_map.239 = (bf16[512,2176]{1,0:T(8,128)(2,1)}, bf16[512,2048]{1,0:T(8,128)(2,1)}, bf16[512,1024]{1,0:T(8,128)(2,1)S(1)}, bf16[512,1024]{1,0:T(8,128)(2,1)}) custom-call(s32[1]{0:T(128)} %bitcast.53.own_ref, bf16[512,2048]{1,0:T(8,128)(2,1)} %pad_maximum_fusion.10.cot_ref, f32[512,1]{1,0:T(8,128)S(1)} %copy.53.gate_ref, ...), custom_call_target="tpu_custom_call" | custom-call | flops 1 | bytes 1 | tf_op jit(solution)/shard_map/pallas_call | solution.py:576
  539.6 15.1 %shard_map.240 = f32[1024,2048]{1,0:T(8,128)} custom-call(bf16[512,1024]{1,0:T(8,128)(2,1)S(1)} %copy-done.23, bf16[512,1024]{1,0:T(8,128)(2,1)} %copy-done.116, bf16[512,1024]{1,0:T(8,128)(2,1)} %copy-done.117, bf16[512,1024]{1,0:T(8,128)(2,1)} %get-tuple-element.1378.refs_3_, bf16[512,2048]{1,0:T(8,128)(2,1)} %get-tuple-element.1379.refs_4_, ...), custom_call_target="tpu_custom_call" | custom-call | flops 1 | bytes 1 | tf_op jit(solution)/shard_map/pallas_call | solution.py:613
  571.1 7.1 collective-permute-done.77
  600.9 14.1 %collective-permute-start.82 = (bf16[256,2048]{1,0:T(8,128)(2,1)S(1)}, bf16[256,2048]{1,0:T(8,128)(2,1)}, u32[]{:S(2)}, u32[]{:S(2)}) collective-permute-start(bf16[256,2048]{1,0:T(8,128)(2,1)S(1)} %fusion.288.left_ref), channel_id=1, source_target_pairs={{0,16},{16,0},{1,17},{17,1},{2,18},{18,2},{3,19},{19,3},{4,20},{20... | collective-permute-start | bytes 3145736 | tf_op jit(solution)/shard_map/ppermute | solution.py:184
  619.2 22.8 %shard_map.242 = (bf16[256,2048]{1,0:T(8,128)(2,1)S(1)}, bf16[256,2048]{1,0:T(8,128)(2,1)S(1)}, bf16[256,2048]{1,0:T(8,128)(2,1)S(1)}, f32[8,2048]{1,0:T(8,128)S(1)}) custom-call(bf16[256,2048]{1,0:T(8,128)(2,1)S(1)} %fusion.24.grad_ref, bf16[256,2048]{1,0:T(8,128)(2,1)S(1)} %get-tuple-element.1453.query_ref, ...), custom_call_target="tpu_custom_call" | custom-call | flops 1073741824 | bytes 15728640 | tf_op jit(solution)/shard_map/pallas_call | solution.py:506
  669.1 12.0 %shard_map.243 = f32[256,2048]{1,0:T(8,128)S(1)} custom-call(bf16[256,6144]{1,0:T(8,128)(2,1)S(1)} %pad_maximum_fusion.1.left_ref, bf16[4,4,64,2048]{3,2,1,0:T(8,128)(2,1)S(1)} %bitcast.225, bf16[4,4,64,2048]{3,2,1,0:T(8,128)(2,1)S(1)} %copy-done.6, bf16[4,4,64,2048]{3,2,1,0:T(8,128)(2,1)} %bitcast.230, bf16[4,4,64,2048]{3,2,1,0:T(8,128)(2,1)} %copy-done.7, ...), custom_call_target="tpu_custom_call" | custom-call | flops 6442450944 | bytes 27262976 | tf_op jit(solution)/shard_map/pallas_call | solution.py:367
  733.4 18.5 %collective-permute-done.92 = bf16[768,1024]{1,0:T(8,128)(2,1)} collective-permute-done((bf16[768,1024]{1,0:T(8,128)(2,1)}, bf16[768,1024]{1,0:T(8,128)(2,1)}, u32[]{:S(2)}, u32[]{:S(2)}) %collective-permute-start.92) | collective-permute-done | bytes 1572896 | tf_op jit(solution)/shard_map/ppermute | solution.py:171
  771.9 13.5 %shard_map.244 = f32[2048,1024]{1,0:T(8,128)} custom-call(bf16[512,2048]{1,0:T(8,128)(2,1)} %copy-done.32, bf16[512,2048]{1,0:T(8,128)(2,1)} %copy-done.33, bf16[512,2048]{1,0:T(8,128)(2,1)} %copy-done.34, bf16[512,2048]{1,0:T(8,128)(2,1)} %copy-done.35, bf16[512,1024]{1,0:T(8,128)(2,1)S(1)} %copy-done.21, bf16[512,1024]{1,0:T(8,128)(2,1)} %copy-done.19, ...), custom_call_target="tpu_custom_call" | custom-call | flops 1 | bytes 1 | tf_op jit(solution)/shard_map/pallas_call | solution.py:613
  790.9 9.3 %collective-permute-done.97 = bf16[768,1024]{1,0:T(8,128)(2,1)S(1)} collective-permute-done((bf16[768,1024]{1,0:T(8,128)(2,1)}, bf16[768,1024]{1,0:T(8,128)(2,1)S(1)}, u32[]{:S(2)}, u32[]{:S(2)}) %collective-permute-start.97) | collective-permute-done | bytes 1572896 | tf_op jit(solution)/shard_map/ppermute | solution.py:171
  821.6 13.7 %shard_map.245 = f32[2048,1024]{1,0:T(8,128)} custom-call(bf16[512,2048]{1,0:T(8,128)(2,1)} %copy-done.32, bf16[512,2048]{1,0:T(8,128)(2,1)} %copy-done.33, bf16[512,2048]{1,0:T(8,128)(2,1)} %copy-done.34, bf16[512,2048]{1,0:T(8,128)(2,1)} %copy-done.35, bf16[512,1024]{1,0:T(8,128)(2,1)S(1)} %copy-done.18, bf16[512,1024]{1,0:T(8,128)(2,1)} %get-tuple-element.1587.refs_5_, ...), custom_call_target="tpu_custom_call" | custom-call | flops 1 | bytes 1 | tf_op jit(solution)/shard_map/pallas_call | solution.py:613
  837.3 10.6 %collective-permute-done.101 = bf16[768,1024]{1,0:T(8,128)(2,1)} collective-permute-done((bf16[768,1024]{1,0:T(8,128)(2,1)}, bf16[768,1024]{1,0:T(8,128)(2,1)}, u32[]{:S(2)}, u32[]{:S(2)}) %collective-permute-start.101) | collective-permute-done | bytes 1572896 | tf_op jit(solution)/shard_map/ppermute | solution.py:171
  873.6 17.1 %collective-permute-done.109 = bf16[66,2048]{1,0:T(8,128)(2,1)S(1)} collective-permute-done((bf16[66,2048]{1,0:T(8,128)(2,1)S(1)}, bf16[66,2048]{1,0:T(8,128)(2,1)S(1)}, u32[]{:S(2)}, u32[]{:S(2)}) %collective-permute-start.109) | collective-permute-done | bytes 270368 | tf_op jit(solution)/shard_map/ppermute | solution.py:180
  898.4 10.4 %collective-permute-start.114 = (f32[32,64]{1,0:T(8,128)S(1)}, f32[32,64]{1,0:T(8,128)S(1)}, u32[]{:S(2)}, u32[]{:S(2)}) collective-permute-start(f32[32,64]{1,0:T(8,128)S(1)} %split.32), channel_id=1, source_target_pairs={{0,16},{16,0},{1,17},{17,1},{2,18},{18,2},{3,19},{19,3},{4,20},{20... | collective-permute-start | bytes 24584 | tf_op jit(solution)/shard_map/ppermute | solution.py:184
  (907 shorter events, 528.6 us)
Async XLA Ops:
  44.7 32.0 %collective-permute-start.10 = (bf16[6,64,2048]{2,1,0:T(8,128)(2,1)}, bf16[6,64,2048]{2,1,0:T(8,128)(2,1)}, u32[]{:S(2)}, u32[]{:S(2)}) collective-permute-start(bf16[6,64,2048]{2,1,0:T(8,128)(2,1)} %get-tuple-element.852), channel_id=1, source_target_pairs={{0,1},{1,0},{2,3},{3,2},{4,5},{5,4},{6,7},{7,6},{8,9},{9,8},{10,11... | collective-permute-start | bytes 4718600 | tf_op jit(solution)/shard_map/ppermute | solution.py:171
  45.9 31.1 %collective-permute-start.11 = (bf16[6,64,2048]{2,1,0:T(8,128)(2,1)}, bf16[6,64,2048]{2,1,0:T(8,128)(2,1)}, u32[]{:S(2)}, u32[]{:S(2)}) collective-permute-start(bf16[6,64,2048]{2,1,0:T(8,128)(2,1)} %get-tuple-element.853), channel_id=1, source_target_pairs={{0,2},{1,3},{2,0},{3,1},{4,6},{5,7},{6,4},{7,5},{8,10},{9,11},{10,... | collective-permute-start | bytes 4718600 | tf_op jit(solution)/shard_map/ppermute | solution.py:171
  200.9 35.6 %collective-permute-start.30 = (bf16[256,2048]{1,0:T(8,128)(2,1)}, bf16[256,2048]{1,0:T(8,128)(2,1)S(1)}, u32[]{:S(2)}, u32[]{:S(2)}) collective-permute-start(bf16[256,2048]{1,0:T(8,128)(2,1)} %pad_maximum_fusion.28), channel_id=1, source_target_pairs={{0,3},{1,2},{2,1},{3,0},{4,7},{5,6},{6,5},{7,4},{8,11},{9,10},{10,... | collective-permute-start | bytes 3145736 | tf_op jit(solution)/shard_map/ppermute | solution.py:171
  201.8 34.7 %collective-permute-start.31 = (bf16[256,2048]{1,0:T(8,128)(2,1)S(1)}, bf16[256,2048]{1,0:T(8,128)(2,1)S(1)}, u32[]{:S(2)}, u32[]{:S(2)}) collective-permute-start(bf16[256,2048]{1,0:T(8,128)(2,1)S(1)} %copy-done.120), channel_id=1, source_target_pairs={{4,0},{5,1},{6,2},{7,3},{8,12},{9,13},{10,14},{11,15},{20,16},{21,... | collective-permute-start | bytes 3145736 | tf_op jit(solution)/shard_map/ppermute | solution.py:180
  244.3 44.1 %collective-permute-start.34 = (bf16[256,2048]{1,0:T(8,128)(2,1)}, bf16[256,2048]{1,0:T(8,128)(2,1)S(1)}, u32[]{:S(2)}, u32[]{:S(2)}) collective-permute-start(bf16[256,2048]{1,0:T(8,128)(2,1)} %pad_maximum_fusion.30), channel_id=1, source_target_pairs={{0,1},{1,0},{2,3},{3,2},{4,5},{5,4},{6,7},{7,6},{8,9},{9,8},{10,11... | collective-permute-start | bytes 3145736 | tf_op jit(solution)/shard_map/ppermute | solution.py:171
  244.6 43.8 %collective-permute-start.35 = (bf16[256,2048]{1,0:T(8,128)(2,1)S(1)}, bf16[256,2048]{1,0:T(8,128)(2,1)S(1)}, u32[]{:S(2)}, u32[]{:S(2)}) collective-permute-start(bf16[256,2048]{1,0:T(8,128)(2,1)S(1)} %copy-done.132), channel_id=1, source_target_pairs={{0,2},{1,3},{2,0},{3,1},{4,6},{5,7},{6,4},{7,5},{8,10},{9,11},{10,... | collective-permute-start | bytes 3145736 | tf_op jit(solution)/shard_map/ppermute | solution.py:171
  246.2 46.0 %collective-permute-start.36 = (bf16[256,2048]{1,0:T(8,128)(2,1)}, bf16[256,2048]{1,0:T(8,128)(2,1)S(1)}, u32[]{:S(2)}, u32[]{:S(2)}) collective-permute-start(bf16[256,2048]{1,0:T(8,128)(2,1)} %pad_maximum_fusion.32), channel_id=1, source_target_pairs={{0,3},{1,2},{2,1},{3,0},{4,7},{5,6},{6,5},{7,4},{8,11},{9,10},{10,... | collective-permute-start | bytes 3145736 | tf_op jit(solution)/shard_map/ppermute | solution.py:171
  247.0 41.4 %collective-permute-start.37 = (bf16[256,1024]{1,0:T(8,128)(2,1)}, bf16[256,1024]{1,0:T(8,128)(2,1)S(1)}, u32[]{:S(2)}, u32[]{:S(2)}) collective-permute-start(bf16[256,1024]{1,0:T(8,128)(2,1)} %get-tuple-element.997), channel_id=1, source_target_pairs={{0,16},{16,0},{1,17},{17,1},{2,18},{18,2},{3,19},{19,3},{4,20},{20... | collective-permute-start | bytes 1572872 | tf_op jit(solution)/shard_map/ppermute | solution.py:184
  404.8 32.9 %collective-permute-start.56 = (bf16[128,2048]{1,0:T(8,128)(2,1)}, bf16[128,2048]{1,0:T(8,128)(2,1)}, u32[]{:S(2)}, u32[]{:S(2)}) collective-permute-start(bf16[128,2048]{1,0:T(8,128)(2,1)} %get-tuple-element.1128), channel_id=1, source_target_pairs={{0,1},{1,0},{2,3},{3,2},{4,5},{5,4},{6,7},{7,6},{8,9},{9,8},{10,11... | collective-permute-start | bytes 1572872 | tf_op jit(solution)/shard_map/ppermute | solution.py:171
  406.0 31.7 %collective-permute-start.57 = (bf16[128,2048]{1,0:T(8,128)(2,1)}, bf16[128,2048]{1,0:T(8,128)(2,1)}, u32[]{:S(2)}, u32[]{:S(2)}) collective-permute-start(bf16[128,2048]{1,0:T(8,128)(2,1)} %get-tuple-element.1129), channel_id=1, source_target_pairs={{0,2},{1,3},{2,0},{3,1},{4,6},{5,7},{6,4},{7,5},{8,10},{9,11},{10,... | collective-permute-start | bytes 1572872 | tf_op jit(solution)/shard_map/ppermute | solution.py:171
  406.0 31.7 %collective-permute-start.58 = (bf16[128,2048]{1,0:T(8,128)(2,1)}, bf16[128,2048]{1,0:T(8,128)(2,1)}, u32[]{:S(2)}, u32[]{:S(2)}) collective-permute-start(bf16[128,2048]{1,0:T(8,128)(2,1)} %get-tuple-element.1130), channel_id=1, source_target_pairs={{0,3},{1,2},{2,1},{3,0},{4,7},{5,6},{6,5},{7,4},{8,11},{9,10},{10,... | collective-permute-start | bytes 1572872 | tf_op jit(solution)/shard_map/ppermute | solution.py:171
  600.9 47.6 %collective-permute-start.82 = (bf16[256,2048]{1,0:T(8,128)(2,1)S(1)}, bf16[256,2048]{1,0:T(8,128)(2,1)}, u32[]{:S(2)}, u32[]{:S(2)}) collective-permute-start(bf16[256,2048]{1,0:T(8,128)(2,1)S(1)} %fusion.288.left_ref), channel_id=1, source_target_pairs={{0,16},{16,0},{1,17},{17,1},{2,18},{18,2},{3,19},{19,3},{4,20},{20... | collective-permute-start | bytes 3145736 | tf_op jit(solution)/shard_map/ppermute | solution.py:184
  615.0 39.2 %collective-permute-start.83 = (bf16[128,2048]{1,0:T(8,128)(2,1)}, bf16[128,2048]{1,0:T(8,128)(2,1)}, u32[]{:S(2)}, u32[]{:S(2)}) collective-permute-start(bf16[128,2048]{1,0:T(8,128)(2,1)} %get-tuple-element.1467), channel_id=1, source_target_pairs={{0,1},{1,0},{2,3},{3,2},{4,5},{5,4},{6,7},{7,6},{8,9},{9,8},{10,11... | collective-permute-start | bytes 1572872 | tf_op jit(solution)/shard_map/ppermute | solution.py:171
  615.2 39.0 %collective-permute-start.84 = (bf16[128,2048]{1,0:T(8,128)(2,1)}, bf16[128,2048]{1,0:T(8,128)(2,1)}, u32[]{:S(2)}, u32[]{:S(2)}) collective-permute-start(bf16[128,2048]{1,0:T(8,128)(2,1)} %get-tuple-element.1468), channel_id=1, source_target_pairs={{0,2},{1,3},{2,0},{3,1},{4,6},{5,7},{6,4},{7,5},{8,10},{9,11},{10,... | collective-permute-start | bytes 1572872 | tf_op jit(solution)/shard_map/ppermute | solution.py:171
  615.6 38.6 %collective-permute-start.85 = (bf16[128,2048]{1,0:T(8,128)(2,1)}, bf16[128,2048]{1,0:T(8,128)(2,1)}, u32[]{:S(2)}, u32[]{:S(2)}) collective-permute-start(bf16[128,2048]{1,0:T(8,128)(2,1)} %get-tuple-element.1469), channel_id=1, source_target_pairs={{0,3},{1,2},{2,1},{3,0},{4,7},{5,6},{6,5},{7,4},{8,11},{9,10},{10,... | collective-permute-start | bytes 1572872 | tf_op jit(solution)/shard_map/ppermute | solution.py:171
  617.7 36.5 %collective-permute-start.86 = (bf16[256,2048]{1,0:T(8,128)(2,1)S(1)}, bf16[256,2048]{1,0:T(8,128)(2,1)}, u32[]{:S(2)}, u32[]{:S(2)}) collective-permute-start(bf16[256,2048]{1,0:T(8,128)(2,1)S(1)} %convert_element_type.691), channel_id=1, source_target_pairs={{0,4},{1,5},{2,6},{3,7},{12,8},{13,9},{14,10},{15,11},{16,20},{17,... | collective-permute-start | bytes 3145736 | tf_op jit(solution)/shard_map/ppermute | solution.py:180
  657.3 37.4 %collective-permute-start.91 = (bf16[3,256,2048]{2,1,0:T(8,128)(2,1)S(1)}, bf16[3,256,2048]{2,1,0:T(8,128)(2,1)}, u32[]{:S(2)}, u32[]{:S(2)}) collective-permute-start(bf16[3,256,2048]{2,1,0:T(8,128)(2,1)S(1)} %pad_maximum_fusion), channel_id=1, source_target_pairs={{0,16},{16,0},{1,17},{17,1},{2,18},{18,2},{3,19},{19,3},{4,20},{20... | collective-permute-start | bytes 9437192 | tf_op jit(solution)/shard_map/ppermute | solution.py:184
  661.7 42.1 %collective-permute-start.89 = (bf16[256,2048]{1,0:T(8,128)(2,1)}, bf16[256,2048]{1,0:T(8,128)(2,1)}, u32[]{:S(2)}, u32[]{:S(2)}) collective-permute-start(bf16[256,2048]{1,0:T(8,128)(2,1)} %add_convert_fusion.6), channel_id=1, source_target_pairs={{4,8},{5,9},{6,10},{7,11},{8,4},{9,5},{10,6},{11,7},{20,24},{21,25... | collective-permute-start | bytes 3145736 | tf_op jit(solution)/shard_map/ppermute | solution.py:180
  664.0 39.8 %collective-permute-start.90 = (bf16[256,2048]{1,0:T(8,128)(2,1)S(1)}, bf16[256,2048]{1,0:T(8,128)(2,1)}, u32[]{:S(2)}, u32[]{:S(2)}) collective-permute-start(bf16[256,2048]{1,0:T(8,128)(2,1)S(1)} %convert_element_type.698), channel_id=1, source_target_pairs={{0,4},{1,5},{2,6},{3,7},{12,8},{13,9},{14,10},{15,11},{16,20},{17,... | collective-permute-start | bytes 3145736 | tf_op jit(solution)/shard_map/ppermute | solution.py:180
  716.4 35.5 %collective-permute-start.92 = (bf16[768,1024]{1,0:T(8,128)(2,1)}, bf16[768,1024]{1,0:T(8,128)(2,1)}, u32[]{:S(2)}, u32[]{:S(2)}) collective-permute-start(bf16[768,1024]{1,0:T(8,128)(2,1)} %pad_maximum_fusion.21), channel_id=1, source_target_pairs={{0,1},{1,0},{2,3},{3,2},{4,5},{5,4},{6,7},{7,6},{8,9},{9,8},{10,11... | collective-permute-start | bytes 4718600 | tf_op jit(solution)/shard_map/ppermute | solution.py:171
  716.6 35.4 %collective-permute-start.93 = (bf16[768,1024]{1,0:T(8,128)(2,1)}, bf16[768,1024]{1,0:T(8,128)(2,1)}, u32[]{:S(2)}, u32[]{:S(2)}) collective-permute-start(bf16[768,1024]{1,0:T(8,128)(2,1)} %pad_maximum_fusion.22), channel_id=1, source_target_pairs={{0,2},{1,3},{2,0},{3,1},{4,6},{5,7},{6,4},{7,5},{8,10},{9,11},{10,... | collective-permute-start | bytes 4718600 | tf_op jit(solution)/shard_map/ppermute | solution.py:171
  720.7 31.3 %collective-permute-start.94 = (bf16[256,2048]{1,0:T(8,128)(2,1)}, bf16[256,2048]{1,0:T(8,128)(2,1)S(1)}, u32[]{:S(2)}, u32[]{:S(2)}) collective-permute-start(bf16[256,2048]{1,0:T(8,128)(2,1)} %add_convert_fusion.5), channel_id=1, source_target_pairs={{0,4},{1,5},{2,6},{3,7},{4,0},{5,1},{6,2},{7,3},{8,12},{9,13},{10,... | collective-permute-start | bytes 3145736 | tf_op jit(solution)/shard_map/ppermute | solution.py:180
  765.0 35.8 %collective-permute-start.96 = (bf16[800,1024]{1,0:T(8,128)(2,1)}, bf16[800,1024]{1,0:T(8,128)(2,1)}, u32[]{:S(2)}, u32[]{:S(2)}) collective-permute-start(bf16[800,1024]{1,0:T(8,128)(2,1)} %pad_maximum_fusion.19), channel_id=1, source_target_pairs={{0,1},{1,0},{2,3},{3,2},{4,5},{5,4},{6,7},{7,6},{8,9},{9,8},{10,11... | collective-permute-start | bytes 4915208 | tf_op jit(solution)/shard_map/ppermute | solution.py:171
  766.1 34.0 %collective-permute-start.97 = (bf16[768,1024]{1,0:T(8,128)(2,1)}, bf16[768,1024]{1,0:T(8,128)(2,1)S(1)}, u32[]{:S(2)}, u32[]{:S(2)}) collective-permute-start(bf16[768,1024]{1,0:T(8,128)(2,1)} %pad_maximum_fusion.23), channel_id=1, source_target_pairs={{0,2},{1,3},{2,0},{3,1},{4,6},{5,7},{6,4},{7,5},{8,10},{9,11},{10,... | collective-permute-start | bytes 4718600 | tf_op jit(solution)/shard_map/ppermute | solution.py:171
  766.4 34.4 %collective-permute-start.98 = (bf16[64,2048]{1,0:T(8,128)(2,1)}, bf16[64,2048]{1,0:T(8,128)(2,1)S(1)}, u32[]{:S(2)}, u32[]{:S(2)}) collective-permute-start(bf16[64,2048]{1,0:T(8,128)(2,1)} %get-tuple-element.1564), channel_id=1, source_target_pairs={{0,4},{1,5},{2,6},{3,7},{4,8},{5,9},{6,10},{7,11},{8,12},{9,13},{1... | collective-permute-start | bytes 786440 | tf_op jit(solution)/shard_map/ppermute | solution.py:180
  767.1 33.8 %collective-permute-start.99 = (bf16[64,2048]{1,0:T(8,128)(2,1)}, bf16[64,2048]{1,0:T(8,128)(2,1)S(1)}, u32[]{:S(2)}, u32[]{:S(2)}) collective-permute-start(bf16[64,2048]{1,0:T(8,128)(2,1)} %get-tuple-element.1565), channel_id=1, source_target_pairs={{0,8},{1,9},{2,10},{3,11},{4,12},{5,13},{6,14},{7,15},{8,0},{9,1},... | collective-permute-start | bytes 786440 | tf_op jit(solution)/shard_map/ppermute | solution.py:180
  814.5 34.1 %collective-permute-start.102 = (bf16[784,1024]{1,0:T(8,128)(2,1)S(1)}, bf16[784,1024]{1,0:T(8,128)(2,1)S(1)}, u32[]{:S(2)}, u32[]{:S(2)}) collective-permute-start(bf16[784,1024]{1,0:T(8,128)(2,1)S(1)} %pad_maximum_fusion.20), channel_id=1, source_target_pairs={{0,2},{1,3},{2,0},{3,1},{4,6},{5,7},{6,4},{7,5},{8,10},{9,11},{10,... | collective-permute-start | bytes 4816904 | tf_op jit(solution)/shard_map/ppermute | solution.py:171
  814.5 33.4 %collective-permute-start.101 = (bf16[768,1024]{1,0:T(8,128)(2,1)}, bf16[768,1024]{1,0:T(8,128)(2,1)}, u32[]{:S(2)}, u32[]{:S(2)}) collective-permute-start(bf16[768,1024]{1,0:T(8,128)(2,1)} %pad_maximum_fusion.24), channel_id=1, source_target_pairs={{0,1},{1,0},{2,3},{3,2},{4,5},{5,4},{6,7},{7,6},{8,9},{9,8},{10,11... | collective-permute-start | bytes 4718600 | tf_op jit(solution)/shard_map/ppermute | solution.py:171
  816.2 32.4 %collective-permute-start.103 = (bf16[64,2048]{1,0:T(8,128)(2,1)}, bf16[64,2048]{1,0:T(8,128)(2,1)S(1)}, u32[]{:S(2)}, u32[]{:S(2)}) collective-permute-start(bf16[64,2048]{1,0:T(8,128)(2,1)} %get-tuple-element.1593), channel_id=1, source_target_pairs={{0,4},{1,5},{2,6},{3,7},{4,8},{5,9},{6,10},{7,11},{8,12},{9,13},{1... | collective-permute-start | bytes 786440 | tf_op jit(solution)/shard_map/ppermute | solution.py:180
  816.8 31.8 %collective-permute-start.104 = (bf16[64,2048]{1,0:T(8,128)(2,1)}, bf16[64,2048]{1,0:T(8,128)(2,1)S(1)}, u32[]{:S(2)}, u32[]{:S(2)}) collective-permute-start(bf16[64,2048]{1,0:T(8,128)(2,1)} %get-tuple-element.1594), channel_id=1, source_target_pairs={{0,8},{1,9},{2,10},{3,11},{4,12},{5,13},{6,14},{7,15},{8,0},{9,1},... | collective-permute-start | bytes 786440 | tf_op jit(solution)/shard_map/ppermute | solution.py:180
  860.8 35.1 %collective-permute-start.106 = (bf16[256,1024]{1,0:T(8,128)(2,1)S(1)}, bf16[256,1024]{1,0:T(8,128)(2,1)S(1)}, u32[]{:S(2)}, u32[]{:S(2)}) collective-permute-start(bf16[256,1024]{1,0:T(8,128)(2,1)S(1)} %copy-done.138), channel_id=1, source_target_pairs={{0,1},{1,0},{2,3},{3,2},{4,5},{5,4},{6,7},{7,6},{8,9},{9,8},{10,11... | collective-permute-start | bytes 1572872 | tf_op jit(solution)/shard_map/ppermute | solution.py:171
  862.0 34.0 %collective-permute-start.107 = (bf16[256,1024]{1,0:T(8,128)(2,1)}, bf16[256,1024]{1,0:T(8,128)(2,1)S(1)}, u32[]{:S(2)}, u32[]{:S(2)}) collective-permute-start(bf16[256,1024]{1,0:T(8,128)(2,1)} %get-tuple-element.1606), channel_id=1, source_target_pairs={{0,2},{1,3},{2,0},{3,1},{4,6},{5,7},{6,4},{7,5},{8,10},{9,11},{10,... | collective-permute-start | bytes 1572872 | tf_op jit(solution)/shard_map/ppermute | solution.py:171
  (271 other events, 3713.6 us)

commit v3 on v2

--- a/solution.py
+++ b/solution.py
@@ -194,7 +194,7 @@
         x = (self.x - step % self.nx) % self.nx
         core = (self.core - core) % self.cores
         source = (core * self.count + self.at(zed, y, x)) * shard + inside
-        return (order[:, None] == source[None, :]).astype(jnp.bfloat16)
+        return (order[:, None] == source[None, :]).astype(jnp.bfloat16), source[None, :]
 
     def queue_of(self, k):
         table = jnp.asarray(self.queue, jnp.int32)[self.z]
@@ -264,16 +264,8 @@
             contract_rows(by_y[:, :far], right[:, half:]),
         ]
 
-    def scatter_sums(self, terms):
-        wire, full = jnp.bfloat16, jnp.float32
-        from_x, from_y, near_x, near_y = terms
-        line = near_x.shape[0] // 2
-        return [
-            (near_x[line:] + from_x[line:].astype(full)).astype(wire),
-            (near_y[line:] + from_y[line:].astype(full)).astype(wire),
-            near_x[:line] + from_x[:line].astype(full),
-            near_y[:line] + from_y[:line].astype(full),
-        ]
+    def rows_first(self, width):
+        return width // self.cores // self.nx
 
     def line_parts(self, terms):
         full = jnp.float32
@@ -306,6 +298,42 @@
 
 
 COLUMNS = 1024
+BESIDE = pl.CostEstimate(flops=1, bytes_accessed=1, transcendentals=0)
+
+
+def fold(came, near, far, more):
+    rows, width = near[0].shape
+    line = rows // 2
+    ahead = rows if far else 0
+    extra = [m.shape[0] if m is not None else 0 for m in more]
+    low, full = jnp.bfloat16, jnp.float32
+
+    def body(*refs):
+        came_refs, near_refs, refs = refs[:2], refs[2:4], refs[4:]
+        far_refs, refs = refs[: len(far)], refs[len(far) :]
+        more_refs, (out_x, out_y, keep_x, keep_y) = list(refs[:-4]), refs[-4:]
+        sums = [
+            n[...] + c[:rows, :].astype(full) for n, c in zip(near_refs, came_refs, strict=True)
+        ]
+        keep_x[...], keep_y[...] = sums[0][:line], sums[1][:line]
+        out_x[ahead : ahead + line, :] = sums[1][line:].astype(low)
+        out_y[ahead : ahead + line, :] = sums[0][line:].astype(low)
+        for out, far_ref in zip((out_x, out_y), far_refs, strict=False):
+            out[:ahead, :] = far_ref[...]
+        for out, count in zip((out_x, out_y), extra, strict=True):
+            if count:
+                out[ahead + line :, :] = more_refs.pop(0)[...]
+
+    outs = [ahead + line + extra[0], ahead + line + extra[1], line, line]
+    return pl.pallas_call(
+        body,
+        out_shape=[
+            jax.ShapeDtypeStruct((count, width), dtype)
+            for count, dtype in zip(outs, (low, low, full, full), strict=True)
+        ],
+        compiler_params=pltpu.CompilerParams(vmem_limit_bytes=40 << 20),
+        cost_estimate=BESIDE,
+    )(*came, *near, *far, *[m for m in more if m is not None])
 
 
 def times_gathered(left, pieces, start, stop, so_far=None):
@@ -335,18 +363,14 @@
         out_specs=out_spec,
         out_shape=jax.ShapeDtypeStruct((left.shape[0], depth), jnp.float32),
         compiler_params=pltpu.CompilerParams(vmem_limit_bytes=40 << 20),
-        cost_estimate=pl.CostEstimate(
-            flops=2 * left.shape[0] * left.shape[1] * depth,
-            bytes_accessed=2 * left.shape[1] * depth + 8 * left.shape[0] * depth,
-            transcendentals=0,
-        ),
+        cost_estimate=BESIDE,
     )(left, *pieces, *([] if so_far is None else [so_far]))
 
 
 def times_transposed(left, pieces, start, stop):
     plane, _, shard, width = pieces[0].shape
     rows, tiles = plane * shard, width // COLUMNS
-    out_shape = (left.shape[0], rows * len(pieces))
+    out_shape = (left.shape[1], rows * len(pieces))
 
     def body(left_ref, *refs):
         *piece_refs, out_ref = refs
@@ -357,7 +381,7 @@
 
         for i, piece_ref in enumerate(piece_refs):
             out_ref[:, i * rows : (i + 1) * rows] += lax.dot_general(
-                left_ref[...],
+                left_ref[0],
                 piece_ref[...].reshape(rows, COLUMNS),
                 (((1,), (1,)), ((), ())),
                 preferred_element_type=jnp.float32,
@@ -367,17 +391,16 @@
     return pl.pallas_call(
         body,
         grid=(stop - start, tiles),
-        in_specs=[pl.BlockSpec((left.shape[0], COLUMNS), lambda w, j: (0, w * tiles + j))]
+        in_specs=[pl.BlockSpec((1, left.shape[1], COLUMNS), lambda w, j: (left.shape[0] - 1 - w, 0, j))]
         + [piece_spec] * len(pieces),
         out_specs=pl.BlockSpec(out_shape, lambda w, j: (0, 0)),
         out_shape=jax.ShapeDtypeStruct(out_shape, jnp.float32),
         compiler_params=pltpu.CompilerParams(vmem_limit_bytes=40 << 20),
-        cost_estimate=pl.CostEstimate(
-            flops=2 * left.size * out_shape[1],
-            bytes_accessed=2 * left.shape[1] * out_shape[1] + 4 * left.shape[0] * out_shape[1],
-            transcendentals=0,
-        ),
+        cost_estimate=BESIDE,
     )(left, *pieces)
+
+
+GROUP = 8
 
 
 def attention(projected, gains, tables, doc_ids, heads):
@@ -387,9 +410,9 @@
 
     def body(raw_ref, gain_ref, cos_ref, sin_ref, row_ref, col_ref,
              query_ref, key_ref, value_ref, out_ref, prob_ref, inv_ref, seen_ref):
-        head = pl.program_id(0)
-
-        @pl.when(head == 0)
+        first = pl.program_id(0) * GROUP
+
+        @pl.when(first == 0)
         def _():
             for i in (0, 1):
                 raw = raw_ref[:, i * width : (i + 1) * width]
@@ -400,49 +423,48 @@
             seen = (row_ref[...] == col_ref[...]) & (at >= to)
             seen_ref[...] = jnp.where(seen, 1.0, 0.0)
 
-        here = pl.multiple_of(head * HD, HD)
-
-        def turned(i):
+        def turned(i, head):
             raw = raw_ref[:, pl.ds(pl.multiple_of(i * width + head * HD, HD), HD)]
-            value = raw * inv_ref[:, i : i + 1] * gain_ref[i + 1 : i + 2, pl.ds(here, HD)]
+            gain = gain_ref[i + 1 : i + 2, pl.ds(pl.multiple_of(head * HD, HD), HD)]
+            value = raw * inv_ref[:, i : i + 1] * gain
             return (value * cos_ref[...] + pltpu.roll(value, HD // 2, 1) * sin_ref[...]).astype(low)
 
-        query, key = turned(0), turned(1)
-        value = raw_ref[:, pl.ds(pl.multiple_of(2 * width + head * HD, HD), HD)].astype(low)
-        scores = lax.dot_general(
-            query, key, (((1,), (1,)), ((), ())), preferred_element_type=full
-        ) * scale
-        scores = jnp.where(seen_ref[...] > 0.0, scores, MASKED)
-        expo = jnp.exp(scores - jnp.max(scores, axis=-1, keepdims=True))
-        probs = expo / jnp.sum(expo, axis=-1, keepdims=True)
-        prob_ref[0] = probs
-        out_ref[...] = jnp.dot(probs.astype(low), value, preferred_element_type=full).astype(low)
-        query_ref[...], key_ref[...], value_ref[...] = query, key, value
+        for g in range(GROUP):
+            at = slice(g * HD, (g + 1) * HD)
+            query, key = turned(0, first + g), turned(1, first + g)
+            value_at = pl.multiple_of(2 * width + (first + g) * HD, HD)
+            value = raw_ref[:, pl.ds(value_at, HD)].astype(low)
+            scores = lax.dot_general(
+                query, key, (((1,), (1,)), ((), ())), preferred_element_type=full
+            ) * scale
+            scores = jnp.where(seen_ref[...] > 0.0, scores, MASKED)
+            expo = jnp.exp(scores - jnp.max(scores, axis=-1, keepdims=True))
+            probs = expo / jnp.sum(expo, axis=-1, keepdims=True)
+            prob_ref[g] = probs
+            out = jnp.dot(probs.astype(low), value, preferred_element_type=full)
+            out_ref[:, at] = out.astype(low)
+            query_ref[:, at], key_ref[:, at], value_ref[:, at] = query, key, value
 
     def whole(shape):
         return pl.BlockSpec(shape, lambda h: (0,) * len(shape))
 
-    part = pl.BlockSpec((length, HD), lambda h: (0, h))
+    part = pl.BlockSpec((length, GROUP * HD), lambda h: (0, h))
     flat = jax.ShapeDtypeStruct((length, width), low)
     return pl.pallas_call(
         body,
-        grid=(heads,),
+        grid=(heads // GROUP,),
         in_specs=[
             whole(projected.shape), whole(gains.shape), whole((length, HD)), whole((length, HD)),
             whole((length, 1)), whole((1, length)),
         ],
         out_specs=[part, part, part, part,
-                   pl.BlockSpec((1, length, length), lambda h: (h, 0, 0)), whole((length, LANES))],
+                   pl.BlockSpec((GROUP, length, length), lambda h: (h, 0, 0)), whole((length, LANES))],
         out_shape=[flat, flat, flat, flat,
                    jax.ShapeDtypeStruct((heads, length, length), full),
                    jax.ShapeDtypeStruct((length, LANES), full)],
         scratch_shapes=[pltpu.VMEM((length, length), full)],
         compiler_params=pltpu.CompilerParams(vmem_limit_bytes=40 << 20),
-        cost_estimate=pl.CostEstimate(
-            flops=4 * heads * length * length * HD,
-            bytes_accessed=4 * projected.size + 8 * length * width + 4 * heads * length * length,
-            transcendentals=heads * length * length,
-        ),
+        cost_estimate=BESIDE,
     )(projected, gains, *tables, doc_ids.reshape(length, 1), doc_ids.reshape(1, length))
 
 
@@ -452,41 +474,44 @@
     scale = HD ** (-0.5)
 
     def body(grad_ref, query_ref, key_ref, value_ref, prob_ref, raw_ref, inv_ref, gain_ref,
-             cos_ref, sin_ref, dq_ref, dk_ref, dv_ref, dgain_ref, turned_ref, inner_ref):
-        head = pl.program_id(0)
-        here = pl.multiple_of(head * HD, HD)
-        grad, probs = grad_ref[...], prob_ref[0]
-        grad_probs = lax.dot_general(
-            grad, value_ref[...], (((1,), (1,)), ((), ())), preferred_element_type=full
-        )
-        dv_ref[...] = lax.dot_general(
-            probs.astype(low), grad, (((0,), (0,)), ((), ())), preferred_element_type=full
-        ).astype(low)
-        inner = jnp.sum(probs * grad_probs, axis=-1, keepdims=True)
-        grad_scores = (probs * (grad_probs - inner)).astype(low)
-        rotated = (
-            jnp.dot(grad_scores, key_ref[...], preferred_element_type=full) * scale,
-            lax.dot_general(
-                grad_scores, query_ref[...], (((0,), (0,)), ((), ())), preferred_element_type=full
-            ) * scale,
-        )
-
-        @pl.when(head == 0)
+             cos_ref, sin_ref, out_ref, dgain_ref, turned_ref, inner_ref):
+        first = pl.program_id(0) * GROUP
+
+        @pl.when(first == 0)
         def _():
             inner_ref[...] = jnp.zeros_like(inner_ref)
 
-        for i in (0, 1):
-            back = rotated[i] * cos_ref[...] - pltpu.roll(rotated[i], HD // 2, 1) * sin_ref[...]
-            at = pl.ds(pl.multiple_of(i * width + head * HD, HD), HD)
-            turned_ref[:, at] = back
-            normed = raw_ref[:, at] * inv_ref[:, i : i + 1]
-            dgain_ref[i : i + 1, pl.ds(here, HD)] = jnp.sum(back * normed, axis=0, keepdims=True)
-            weighed = back * gain_ref[i + 1 : i + 2, pl.ds(here, HD)]
-            inner_ref[:, i : i + 1] += jnp.sum(weighed * normed, axis=-1, keepdims=True)
-
-        @pl.when(head == heads - 1)
+        for g in range(GROUP):
+            head, part = first + g, slice(g * HD, (g + 1) * HD)
+            here = pl.multiple_of(head * HD, HD)
+            grad, probs = grad_ref[:, part], prob_ref[g]
+            grad_probs = lax.dot_general(
+                grad, value_ref[:, part], (((1,), (1,)), ((), ())), preferred_element_type=full
+            )
+            out_ref[0, :, pl.ds(here, HD)] = lax.dot_general(
+                probs.astype(low), grad, (((0,), (0,)), ((), ())), preferred_element_type=full
+            ).astype(low)
+            inner = jnp.sum(probs * grad_probs, axis=-1, keepdims=True)
+            grad_scores = (probs * (grad_probs - inner)).astype(low)
+            rotated = (
+                jnp.dot(grad_scores, key_ref[:, part], preferred_element_type=full) * scale,
+                lax.dot_general(
+                    grad_scores, query_ref[:, part], (((0,), (0,)), ((), ())),
+                    preferred_element_type=full,
+                ) * scale,
+            )
+            for i in (0, 1):
+                back = rotated[i] * cos_ref[...] - pltpu.roll(rotated[i], HD // 2, 1) * sin_ref[...]
+                at = pl.ds(pl.multiple_of(i * width + head * HD, HD), HD)
+                turned_ref[:, at] = back
+                normed = raw_ref[:, at] * inv_ref[:, i : i + 1]
+                dgain_ref[i : i + 1, pl.ds(here, HD)] = jnp.sum(back * normed, axis=0, keepdims=True)
+                weighed = back * gain_ref[i + 1 : i + 2, pl.ds(here, HD)]
+                inner_ref[:, i : i + 1] += jnp.sum(weighed * normed, axis=-1, keepdims=True)
+
+        @pl.when(first == heads - GROUP)
         def _():
-            for i, out_ref in ((0, dq_ref), (1, dk_ref)):
+            for i in (0, 1):
                 inverse = inv_ref[:, i : i + 1]
                 inner = inner_ref[:, i : i + 1] * (1.0 / width)
 
@@ -496,46 +521,43 @@
                     there = pl.ds(pl.multiple_of(j * HD, HD), HD)
                     weighed = turned_ref[:, at] * gain_ref[i + 1 : i + 2, there]
                     normed = raw_ref[:, at] * inverse
-                    out_ref[:, there] = (inverse * (weighed - normed * inner)).astype(low)
+                    out_ref[2 - i, :, there] = (inverse * (weighed - normed * inner)).astype(low)
 
     def whole(shape):
         return pl.BlockSpec(shape, lambda h: (0,) * len(shape))
 
-    part = pl.BlockSpec((length, HD), lambda h: (0, h))
-    flat = jax.ShapeDtypeStruct((length, width), low)
+    part = pl.BlockSpec((length, GROUP * HD), lambda h: (0, h))
     return pl.pallas_call(
         body,
-        grid=(heads,),
+        grid=(heads // GROUP,),
         in_specs=[
             part, part, part, part,
-            pl.BlockSpec((1, length, length), lambda h: (h, 0, 0)),
+            pl.BlockSpec((GROUP, length, length), lambda h: (h, 0, 0)),
             whole((length, 2 * width)), whole(inverses.shape), whole(gains.shape),
             whole((length, HD)), whole((length, HD)),
         ],
-        out_specs=[whole((length, width)), whole((length, width)), part, whole((8, width))],
-        out_shape=[flat, flat, flat, jax.ShapeDtypeStruct((8, width), full)],
+        out_specs=[whole((3, length, width)), whole((8, width))],
+        out_shape=[
+            jax.ShapeDtypeStruct((3, length, width), low), jax.ShapeDtypeStruct((8, width), full)
+        ],
         scratch_shapes=[pltpu.VMEM((length, 2 * width), full), pltpu.VMEM((length, LANES), full)],
         compiler_params=pltpu.CompilerParams(vmem_limit_bytes=40 << 20),
-        cost_estimate=pl.CostEstimate(
-            flops=8 * heads * length * length * HD,
-            bytes_accessed=8 * length * width + 14 * length * width + 4 * heads * length * length,
-            transcendentals=0,
-        ),
+        cost_estimate=BESIDE,
     )(grad_out, query, key, value, probs, projected, inverses, gains, *tables)
 
 
-BESIDE = pl.CostEstimate(flops=1, bytes_accessed=1, transcendentals=0)
-
-
-def expert_back(cot, gate, result, pre_gate, pre_up, gate_w, up_w, down_w, own):
+def expert_back(pieces, cot, gate, result, pre_gate, pre_up, gate_w, up_w, down_w, own):
     total, width = cot.shape
     rows = min(512, total)
+    pieces = pieces if rows == total else 1
     hidden = pre_gate.shape[1]
     low, full = jnp.bfloat16, jnp.float32
     tile = min(512, hidden)
 
     def body(own_ref, cot_ref, gate_ref, result_ref, a_ref, b_ref, gate_w_ref, up_w_ref, down_w_ref,
-             back_ref, grad_y_ref, grad_a_ref, grad_b_ref, sum_ref):
+             *refs):
+        back_refs, (grad_y_ref, grad_a_ref, grad_b_ref, sum_ref) = refs[:pieces], refs[pieces:]
+        each = rows // pieces
         step = pl.program_id(1)
 
         @pl.when(step == 0)
@@ -547,7 +569,8 @@
             lanes = lax.broadcasted_iota(jnp.int32, (rows, LANES), 1)
             tail = jnp.where(lanes == own_ref[0], high, 0.0)
             tail = jnp.where(lanes == own_ref[0] + LANES // 2, grad_g - high, tail)
-            back_ref[:, width:] = tail.astype(low)
+            for p, back_ref in enumerate(back_refs):
+                back_ref[:, width:] = tail[p * each : (p + 1) * each].astype(low)
             sum_ref[...] = jnp.zeros_like(sum_ref)
 
         grad_act = lax.dot_general(
@@ -566,14 +589,15 @@
 
         @pl.when(step == hidden // tile - 1)
         def _():
-            back_ref[:, :width] = sum_ref[...].astype(low)
+            for p, back_ref in enumerate(back_refs):
+                back_ref[:, :width] = sum_ref[p * each : (p + 1) * each, :].astype(low)
 
     def whole(columns):
         return pl.BlockSpec((rows, columns), lambda r, f: (r, 0))
 
     inner = pl.BlockSpec((rows, tile), lambda r, f: (r, f))
     into = pl.BlockSpec((width, tile), lambda r, f: (0, f))
-    return pl.pallas_call(
+    outs = pl.pallas_call(
         body,
         grid=(total // rows, hidden // tile),
         in_specs=[
@@ -581,9 +605,10 @@
             whole(width), whole(1), whole(width), inner, inner, into, into,
             pl.BlockSpec((tile, width), lambda r, f: (f, 0)),
         ],
-        out_specs=[whole(width + LANES), whole(width), inner, inner],
-        out_shape=[
-            jax.ShapeDtypeStruct((total, width + LANES), low),
+        out_specs=[pl.BlockSpec((rows // pieces, width + LANES), lambda r, f: (r, 0))] * pieces
+        + [whole(width), inner, inner],
+        out_shape=[jax.ShapeDtypeStruct((total // pieces, width + LANES), low)] * pieces
+        + [
             jax.ShapeDtypeStruct(cot.shape, low),
             jax.ShapeDtypeStruct(pre_gate.shape, low),
             jax.ShapeDtypeStruct(pre_gate.shape, low),
@@ -592,6 +617,7 @@
         compiler_params=pltpu.CompilerParams(vmem_limit_bytes=52 << 20),
         cost_estimate=BESIDE,
     )(own.reshape(1), cot, gate, result, pre_gate, pre_up, gate_w, up_w, down_w)
+    return (outs[:pieces], *outs[pieces:])
 
 
 def rows_product(lefts, rights):
@@ -620,6 +646,73 @@
         compiler_params=pltpu.CompilerParams(vmem_limit_bytes=52 << 20),
         cost_estimate=BESIDE,
     )(*lefts, *rights)
+
+
+def input_gradient(grad, sources, tokens, inverse, gain, residual):
+    length, width = grad.shape
+    tile = 512
+    low, full = jnp.bfloat16, jnp.float32
+
+    def body(grad_ref, source_ref, token_ref, inverse_ref, gain_ref, residual_ref,
+             out_ref, dgain_ref, split_ref, placed_ref, inner_ref):
+        step = pl.program_id(0)
+
+        @pl.when(step == 0)
+        def _():
+            high = grad_ref[...].astype(low)
+            split_ref[:length, :] = high
+            split_ref[length:, :] = (grad_ref[...] - high.astype(full)).astype(low)
+            inner_ref[...] = jnp.zeros_like(inner_ref)
+
+        at = pl.ds(pl.multiple_of(step * tile, tile), tile)
+        column = step * tile + lax.broadcasted_iota(jnp.int32, (tile, width), 0)
+        arrival = jnp.where(column == source_ref[...], 1.0, 0.0).astype(low)
+        placed = lax.dot_general(
+            split_ref[...], arrival, (((1,), (1,)), ((), ())), preferred_element_type=full
+        )
+        placed = placed[:length] + placed[length:]
+        placed_ref[:, at] = placed
+        normed = token_ref[:, at].astype(full) * inverse_ref[...]
+        dgain_ref[:, at] = jnp.broadcast_to(
+            jnp.sum(placed * normed, axis=0, keepdims=True), (dgain_ref.shape[0], tile)
+        )
+        weighed = placed * gain_ref[:, at]
+        inner_ref[:, :1] += jnp.sum(weighed * normed, axis=-1, keepdims=True)
+
+        @pl.when(step == width // tile - 1)
+        def _():
+            inner = inner_ref[:, :1] * (1.0 / width)
+            inverse = inverse_ref[...]
+
+            @pl.loop(0, width // tile)
+            def _(j):
+                at = pl.ds(pl.multiple_of(j * tile, tile), tile)
+                normed = token_ref[:, at].astype(full) * inverse
+                back = inverse * (placed_ref[:, at] * gain_ref[:, at] - normed * inner)
+                out_ref[:, at] = (residual_ref[:, at] + back).astype(low)
+
+    def whole(shape):
+        return pl.BlockSpec(shape, lambda j: (0,) * len(shape))
+
+    return pl.pallas_call(
+        body,
+        grid=(width // tile,),
+        in_specs=[
+            whole(grad.shape), whole(sources.shape), whole(tokens.shape),
+            whole(inverse.shape), whole(gain.shape), whole(residual.shape),
+        ],
+        out_specs=[whole(tokens.shape), whole((8, width))],
+        out_shape=[
+            jax.ShapeDtypeStruct(tokens.shape, low), jax.ShapeDtypeStruct((8, width), full)
+        ],
+        scratch_shapes=[
+            pltpu.VMEM((2 * length, width), low),
+            pltpu.VMEM((length, width), full),
+            pltpu.VMEM((length, LANES), full),
+        ],
+        compiler_params=pltpu.CompilerParams(vmem_limit_bytes=40 << 20),
+        cost_estimate=BESIDE,
+    )(grad, sources, tokens, inverse, gain, residual)
 
 
 def rope_tables(length):
@@ -668,7 +761,7 @@
     slots = jnp.where(named.T & (slots < capacity), slots, -1.0).astype(bfloat)
 
     order = range(here.nz)
-    arrival = here.arrival(width)
+    arrival, sources = here.arrival(width)
     extra = norm_gains.shape[0] + w_router.shape[1]
     smalls = jnp.concatenate(
         [norm_gains.T, w_router, jnp.zeros((shard, -extra % LANES), jnp.float32)], axis=1
@@ -779,8 +872,9 @@
             smalls = jnp.stack(smalls, axis=1)
             smalls = [smalls] + [here.other_core(smalls, s) for s in range(1, here.cores)]
             smalls = jnp.stack(smalls, axis=1).reshape(width, -1)
+            smalls = product(arrival, smalls).astype(bfloat)
+            smalls, sources = tie(smalls, sources)
         if k == 3:
-            smalls = product(arrival, smalls).astype(bfloat)
             gains_f = smalls[:, : norm_gains.shape[0]].T.astype(jnp.float32)
             wr = smalls[:, norm_gains.shape[0] : extra]
             normed_in_f, normed_one, inverse_one = norm_rows(inputs, gains_f[0])
@@ -853,7 +947,10 @@
 
     def expert_backward(kept, cot):
         gate, pre_gate, pre_up, _, result, _ = kept
-        return expert_back(cot, gate, result, pre_gate, pre_up, gate_w, up_w, down_w, here.me)
+        back, *kept = expert_back(
+            plane, cot, gate, result, pre_gate, pre_up, gate_w, up_w, down_w, here.me
+        )
+        return [back if len(back) == plane else parted(back[0]), *kept]
 
     rows_next = rows_of(spreads[0], normed_mid)
     out_columns = here.core_columns(attended)
@@ -880,11 +977,16 @@
             rows, targets = tie(rows, targets)
         if k == here.nz // 2:
             out_columns = here.to_cores(out_columns)
+        if k == here.nz - 1:
+            out_columns = targeted(out_columns)
+        for j in order[here.nz - k - (k == here.nz - 1) : here.nz - k + 1] if k > 0 else []:
+            rows_cot[j] = joined(rows_cot[j])
+            rows, rows_cot[j] = tie(rows, rows_cot[j])
         moving, rows, forward, out_columns = tie(moving, rows, forward, out_columns)
         rows_in.append(rows)
         line.land(moving)
 
-    targets_out = targeted(out_columns)
+    targets_out = out_columns
     half = here.nz // 2
     back_y = [None] * here.nz
     backward = [None] * here.nz
@@ -896,7 +998,7 @@
             rows_in[-1] = joined(rows_in[-1])
             forward.append(expert_forward(rows_in[-1]))
         elif k is not None:
-            backward[k] = expert_backward(forward[k], joined(rows_cot[k]))
+            backward[k] = expert_backward(forward[k], rows_cot[k])
 
     rows_next = parted(forward[0][5])
     rows_next, forward, rows_in, rows_cot, out_columns = tie(
@@ -910,7 +1012,7 @@
     collect, parts = Collect(here), [None] * here.nz
     moving, sending, back = [], [], None
     for k in reversed(order):
-        rows_next = parted(backward[k][0])
+        rows_next = backward[k][0]
         if k + 2 < here.nz:
             collect.land(moving)
             sending = collect.add(k + 2, parts[k + 2])
@@ -934,17 +1036,19 @@
     collect.land(moving)
     sending = collect.add(1, parts[1])
     rows_next = parted(forward[late[0]][5])
-    rows_next, sending, back = tie(rows_next, sending, back)
+    rows_next, sending, back, back_y = tie(rows_next, sending, back, back_y)
     rows = here.deal_back(rows_next)
     moving = collect.send(sending)
     parts[0] = contract_rows(spreads[0], joined(back))
+    part_y = contract_rows(spreads[0], joined(back_y[0]))
     rows_next = [parted(forward[k][5]) for k in late[1:]]
-    moving, rows, parts, rows_next = tie(moving, rows, parts, rows_next)
+    moving, rows, parts, rows_next, part_y = tie(moving, rows, parts, rows_next, part_y)
     collect.land(moving)
     collect.add(0, parts[0])
     returned = collect.total
     back_y[late[0]] = rows
     parts_y = [None] * here.nz
+    parts_y[0] = part_y
     if rows_next:
         back_y[late[1]] = here.deal_back(rows_next[0])
 
@@ -967,7 +1071,7 @@
     grad_res_two, grad_gain_mid = norm_back(grad_mid, gains_f[3], normed_two, inverse_two)
     grad_residual = cotangent.astype(jnp.float32) + grad_res_two
     grad_attn = grad_residual.astype(bfloat)
-    grad_attended = times_transposed(grad_attn, pieces, 3, 4).astype(bfloat)
+    grad_attended = times_transposed(grad_attn[None], pieces, 3, 4).astype(bfloat)
     grad_attended = contract_cols(grad_attended, arrival).astype(bfloat)
     collect_y, adds_y = Collect(here), list(reversed(order))
     grad_attended, grad_attn, back_y, parts_y = tie(grad_attended, grad_attn, back_y, parts_y)
@@ -979,25 +1083,15 @@
         back_y[late[2]] = here.deal_back(rows_next[1])
     moving = collect_y.send(sending_y)
     out_tokens = here.all_tokens(grad_attn)
-    grad_query, grad_key, grad_values, grad_gain_heads = attention_back(
+    grads, grad_gain_heads = attention_back(
         grad_attended, query_rot, key_rot, values, probs, projected, inverses, gains_f, tables, heads
     )
     far = here.scatter_far(*targets_out, out_tokens)
-    grads = jnp.stack([grad_values, grad_key, grad_query])
-    for k in [0, *late[1:2]]:
+    for k in late[1:2]:
         add_up_y(k)
     grads, far, back_y, parts_y, moving, out_tokens = tie(
         grads, far, back_y, parts_y, moving, out_tokens
     )
-
-    def leave(far, sums, more_x, more_y):
-        if not here.square:
-            return list(far)
-        by_x, by_y = list(far[:1]), list(far[1:])
-        if sums:
-            by_x.append(sums[1])
-            by_y.append(sums[0])
-        return [jnp.concatenate(by_x + more_x, axis=0), jnp.concatenate(by_y + more_y, axis=0)]
 
     def arrive(outs):
         if not here.square:
@@ -1006,41 +1100,31 @@
 
     jobs = 4
     lefts, rights = [targets_out, targets, targets, targets], [out_tokens]
-    firsts, lasts, shares = [], [], []
+    lasts, shares, others, grad_in_norm = [], [], [], None
     near, near_last, ins, small, smalls, expert_grads = [], [], [], [None], [], []
     for i in range(jobs + 2):
-        if here.square and i > 0:
-            by_x, by_y = ins
-            if i <= jobs:
-                rows = near[0].shape[0]
-                firsts.append([by_x[:rows], by_y[:rows], *near])
-                by_x, by_y = by_x[rows:], by_y[rows:]
+        outs, parts, more = [], [], [None, None]
+        if here.square:
+            ahead = here.rows_first(width) if i <= jobs else 0
             if i > 1:
-                rows = near_last[0].shape[0]
-                lasts.append([by_y[:rows], by_x[:rows], *near_last])
-                by_x, by_y = by_x[rows:], by_y[rows:]
-        elif 0 < i <= jobs:
-            lasts.append(ins)
-        sums, parts, more_x, more_y, outs = [], [], [], [], []
-        if here.square:
-            sums = here.scatter_sums(firsts[i - 1]) if 0 < i <= jobs else []
-            near_last = sums[2:]
+                line = ahead + near_last[0].shape[0] if i > 1 else 0
+                lasts.append([ins[1][ahead:line], ins[0][ahead:line], *near_last])
             columns = small[0].shape[1] // 2 if small[0] is not None else 0
-            if i == 2:
-                more_x = [small[0][:, columns:].astype(bfloat).reshape(-1, width // 2)]
+            if i in (3, 4):
+                came = ins[i == 4][line:].reshape(small[0].shape)
+                small = [small[0] + came.astype(jnp.float32)]
+            if i in (2, 3):
+                more[i == 3] = small[0][:, columns:].astype(bfloat).reshape(-1, width // 2)
                 small = [small[0][:, :columns]]
-            elif i == 3:
-                small = [small[0] + by_x.reshape(small[0].shape).astype(jnp.float32)]
-                more_y = [small[0][:, columns:].astype(bfloat).reshape(-1, width // 2)]
-                small = [small[0][:, :columns]]
-            elif i == 4:
-                small = [small[0] + by_y.reshape(small[0].shape).astype(jnp.float32)]
-            if i < jobs:
-                outs = leave(far, sums, more_x, more_y)
-            elif i == jobs:
-                outs = [sums[1], sums[0]]
-        elif i < jobs:
-            outs = leave(far, [], [], [])
+            if i == 0:
+                outs = far
+            elif i <= jobs:
+                *outs, keep_x, keep_y = fold(ins, near, far if i < jobs else [], more)
+                near_last = [keep_x, keep_y]
+        else:
+            if 0 < i <= jobs:
+                lasts.append(ins)
+            outs = far if i < jobs else []
         at = i - 2 if here.square else i - 1
         if 0 <= at < jobs:
             parts = here.line_parts(lasts[at])
@@ -1055,8 +1139,10 @@
         if adds_y:
             collect_y.land(moving)
             sending_y = collect_y.add(adds_y[0], parts_y[adds_y.pop(0)])
-        outs, parts, sending_y, near_last, small, rights, smalls, grads, back_y, rows_in = tie(
-            outs, parts, sending_y, near_last, small, rights, smalls, grads, back_y, rows_in
+        (
+            outs, parts, sending_y, near_last, small, rights, smalls, grads, back_y, rows_in, grad_in_norm
+        ) = tie(
+            outs, parts, sending_y, near_last, small, rights, smalls, grads, back_y, rows_in, grad_in_norm
         )
         ins = arrive(outs) if outs else []
         if parts:
@@ -1068,26 +1154,21 @@
             near = here.scatter_near(*lefts[i], rights[i])
         if i == 0:
             others = [here.other_core(grads, step) for step in range(1, here.cores)]
-            rights += [jnp.concatenate([v[j] for v in [grads, *others]], axis=0) for j in range(3)]
+        if i + 1 < jobs:
+            rights.append(jnp.concatenate([v[i] for v in [grads, *others]], axis=0))
         if i + 1 < jobs:
             far = here.scatter_far(*lefts[i + 1], rights[i + 1])
         if i == 0:
-            grad_in_norm = times_transposed(
-                jnp.concatenate([grads[2], grads[1], grads[0]], axis=1), pieces, 0, 3
+            grads, others = tie(grads, others)
+            grad_in_norm = times_transposed(grads, pieces, 0, 3)
+        if i == 1:
+            grad_tokens, grad_gain_in = input_gradient(
+                grad_in_norm, sources, tokens, inverse_one, gains_f[:1], grad_residual
             )
-            high = grad_in_norm.astype(bfloat)
-            low = (grad_in_norm - high.astype(jnp.float32)).astype(bfloat)
-            high, low, ins = tie(high, low, ins)
-        if i == 1:
-            grad_in_norm = contract_cols(high, arrival) + contract_cols(low, arrival)
-            grad_res_one, grad_gain_in = norm_back(
-                grad_in_norm, gains_f[0], normed_one, inverse_one
-            )
-            grad_tokens = (grad_residual + grad_res_one).astype(bfloat)
             small_rows = 4 + experts
             smalls = jnp.concatenate(
                 [
-                    grad_gain_in[None],
+                    grad_gain_in[:1],
                     grad_gain_heads[:2],
                     grad_gain_mid[None],
                     grad_router.T,
@@ -1105,8 +1186,11 @@
             grad = rows_product(rows_in, [kept[i] for kept in backward])
             expert_grads.append(grad)
             ins, expert_grads = tie(ins, expert_grads)
-        ins, parts, moving, far, near, rights, smalls, parts_y = tie(
-            ins, parts, moving, far, near, rights, smalls, parts_y
+        if i == 3:
+            mixed = (residual + collect_y.total).astype(bfloat)
+            mixed, ins = tie(mixed, ins)
+        ins, parts, moving, far, near, rights, smalls, parts_y, grad_in_norm, others = tie(
+            ins, parts, moving, far, near, rights, smalls, parts_y, grad_in_norm, others
         )
         if parts:
             share = sum(part.astype(jnp.float32) for part in parts)
@@ -1120,7 +1204,6 @@
         smalls = lax.dynamic_slice(
             smalls, (0, (here.core * here.count + here.me) * shard), (smalls.shape[0], shard)
         )
-    mixed = (residual + collect_y.total).astype(bfloat)
     grad_wo, grad_wv, grad_wk, grad_wq = shares
     grad_gate_w, grad_up_w = expert_grads
     return (

time: 932 us -> 892 us (0.957)
  waiting for transfers between devices: 201 us -> 174 us
  other arithmetic: 101 us -> 80 us
  Pallas kernels: 204 us -> 215 us
    ppermute x65, waiting for transfers between devices: 147 us -> 111 us  [shift_plane(): return lax.ppermute(value, 'expert', pairs)]
    add x9 -> x1, other arithmetic: 18 us -> 0.02 us  [on_device(): small = [small[0] + came.astype(jnp.float32)]]
    unnamed x408 -> x446, local copies, waits for them, and re-layouts: 38.1 us -> 49.2 us
    pallas_call x2 -> x7, Pallas kernels: 38.5 us -> 49.5 us  [the longest x1 19.1 us: attention_back(): pl.pallas_call(body, grid=(heads // GROUP,), in_specs=[part, part, part,...]
    another operation x8 -> x4, local copies, waits for them, and re-layouts: 14 us -> 4.12 us  [parted(): return list(rows.reshape(plane, capacity, -1))]
    ppermute x10, starting transfers between devices: 58.8 us -> 49.1 us  [other_core(): return lax.ppermute(value, 'dp', pairs)]
  transfers between devices with their start and end apart: 115 -> 115, of which waited for: 41 -> 40; matrix products, arithmetic and copies ran while one was open for 21% -> 21% of each run, Pallas kernels for 22% -> 23%
where the time goes in v3:
time: 892 us; the launch traced here: 881 us
  Pallas kernels  215 us (24%)
  starting transfers between devices  188 us (21%)
  waiting for transfers between devices  174 us (20%)
  matrix products  130 us (15%)
  local copies, waits for them, and re-layouts  89.7 us (10%)
  other arithmetic  80 us (9%)
    ppermute x65, waiting for transfers between devices, shift_plane(): return lax.ppermute(value, 'expert', pairs)  111 us
    ppermute x40, starting transfers between devices, along_line(): return lax.ppermute(value, 'expert', pairs)  79 us
    dot_general x34, matrix products, product(): return jnp.dot(left, right, preferred_element_type=jnp.float32)  76.2 us
    pallas_call x4, Pallas kernels, expert_back(): pl.pallas_call(body, grid=(total // rows, hidden // tile), in_specs=[pl.B...  68.1 us
    ppermute x40, waiting for transfers between devices, along_line(): return lax.ppermute(value, 'expert', pairs)  62.9 us
    ppermute x65, starting transfers between devices, shift_plane(): return lax.ppermute(value, 'expert', pairs)  60.1 us
    unnamed x446, local copies, waits for them, and re-layouts  49.2 us
    ppermute x10, starting transfers between devices, other_core(): return lax.ppermute(value, 'dp', pairs)  49.1 us
  transfers between devices with their start and end apart: 115, of which 40 were waited for; matrix products, arithmetic and copies ran while one was open for 21% of the time, Pallas kernels for 23%

profile of v3, /device:TPU:9, one launch (start us, length us, event | category | flops | bytes accessed | tf_op | source)
XLA Modules:
  0.0 881.0 jit_solution(1089046194842459215)
XLA Ops:
  20.1 11.5 %collective-permute-done.3 = bf16[4,64,2048]{2,1,0:T(8,128)(2,1)S(1)} collective-permute-done((bf16[4,64,2048]{2,1,0:T(8,128)(2,1)S(1)}, bf16[4,64,2048]{2,1,0:T(8,128)(2,1)S(1)}, u32[]{:S(2)}, u32[]{:S(2)}) %collective-permute-start.3) | collective-permute-done | bytes 1048608 | tf_op jit(solution)/shard_map/ppermute | solution.py:171
  60.5 7.5 collective-permute-done.12
  84.3 7.2 collective-permute-start.17
  100.1 9.9 %collective-permute-done.14 = bf16[6,64,2048]{2,1,0:T(8,128)(2,1)S(1)} collective-permute-done((bf16[6,64,2048]{2,1,0:T(8,128)(2,1)S(1)}, bf16[6,64,2048]{2,1,0:T(8,128)(2,1)S(1)}, u32[]{:S(2)}, u32[]{:S(2)}) %collective-permute-start.14) | collective-permute-done | bytes 1572896 | tf_op jit(solution)/shard_map/ppermute | solution.py:171
  119.6 8.5 collective-permute-start.22
  137.0 5.7 shard_map.230.refs_2_
  150.3 8.7 collective-permute-start.27
  174.2 8.7 shard_map.231.refs_2_
  206.6 9.5 %shard_map.232.refs_2_ = f32[256,6144]{1,0:T(8,128)} custom-call(bf16[256,512]{1,0:T(8,128)(2,1)S(1)} %get-tuple-element.1827.left_ref, bf16[4,4,64,2048]{3,2,1,0:T(8,128)(2,1)} %bitcast.36.refs_0_.refs_4_, bf16[4,4,64,2048]{3,2,1,0:T(8,128)(2,1)} %collective-permute-done.32.refs_1_.refs_5_, f32[256,6144]{1,0:T(8,128)} %shard_map.231.refs_2_), custom_call_target="tpu_custom_call" | custom-call | flops 1 | bytes 1 | tf_op jit(solution)/shard_map/pallas_call | solution.py:357
  216.2 17.7 %collective-permute-done.30 = bf16[256,2048]{1,0:T(8,128)(2,1)S(1)} collective-permute-done((bf16[256,2048]{1,0:T(8,128)(2,1)}, bf16[256,2048]{1,0:T(8,128)(2,1)S(1)}, u32[]{:S(2)}, u32[]{:S(2)}) %collective-permute-start.30) | collective-permute-done | bytes 1048608 | tf_op jit(solution)/shard_map/ppermute | solution.py:171
  248.2 9.2 %shard_map.233.raw_ref = f32[256,6144]{1,0:T(8,128)} custom-call(bf16[256,512]{1,0:T(8,128)(2,1)S(1)} %get-tuple-element.1830.left_ref, bf16[4,4,64,2048]{3,2,1,0:T(8,128)(2,1)} %bitcast.39.refs_0_.refs_6_, bf16[4,4,64,2048]{3,2,1,0:T(8,128)(2,1)} %collective-permute-done.33.refs_1_.refs_7_, f32[256,6144]{1,0:T(8,128)} %shard_map.232.refs_2_), custom_call_target="tpu_custom_call" | custom-call | flops 1 | bytes 1 | tf_op jit(solution)/shard_map/pallas_call | solution.py:357
  257.5 12.8 %shard_map.234 = (bf16[256,2048]{1,0:T(8,128)(2,1)S(1)}, bf16[256,2048]{1,0:T(8,128)(2,1)S(1)}, bf16[256,2048]{1,0:T(8,128)(2,1)S(1)}, bf16[256,2048]{1,0:T(8,12...) custom-call(f32[256,6144]{1,0:T(8,128)} %shard_map.233.raw_ref, ...), custom_call_target="tpu_custom_call" | custom-call | flops 1 | bytes 1 | tf_op jit(solution)/shard_map/pallas_call | solution.py:453
  278.7 5.0 shard_map.235
  307.7 7.9 collective-permute-done.42
  337.2 7.7 collective-permute-done.47
  396.9 5.8 collective-permute-done.55
  414.4 6.8 multiply_convert_fusion
  421.2 17.0 %shard_map.236 = (bf16[128,2176]{1,0:T(8,128)(2,1)S(1)}, bf16[128,2176]{1,0:T(8,128)(2,1)}, bf16[128,2176]{1,0:T(8,128)(2,1)}, bf16[128,2176]{1,0:T(8,128)(2,1)}...) custom-call(s32[1]{0:T(128)} %bitcast.53.own_ref, ...), custom_call_target="tpu_custom_call" | custom-call | flops 1 | bytes 1 | tf_op jit(solution)/shard_map/pallas_call | solution.py:600
  442.0 16.9 %shard_map.237 = (bf16[128,2176]{1,0:T(8,128)(2,1)S(1)}, bf16[128,2176]{1,0:T(8,128)(2,1)}, bf16[128,2176]{1,0:T(8,128)(2,1)}, bf16[128,2176]{1,0:T(8,128)(2,1)}...) custom-call(s32[1]{0:T(128)} %bitcast.53.own_ref, ...), custom_call_target="tpu_custom_call" | custom-call | flops 1 | bytes 1 | tf_op jit(solution)/shard_map/pallas_call | solution.py:600
  462.6 17.2 %shard_map.238 = (bf16[128,2176]{1,0:T(8,128)(2,1)S(1)}, bf16[128,2176]{1,0:T(8,128)(2,1)}, bf16[128,2176]{1,0:T(8,128)(2,1)}, bf16[128,2176]{1,0:T(8,128)(2,1)}...) custom-call(s32[1]{0:T(128)} %bitcast.53.own_ref, ...), custom_call_target="tpu_custom_call" | custom-call | flops 1 | bytes 1 | tf_op jit(solution)/shard_map/pallas_call | solution.py:600
  488.2 17.0 %shard_map.239 = (bf16[128,2176]{1,0:T(8,128)(2,1)S(1)}, bf16[128,2176]{1,0:T(8,128)(2,1)}, bf16[128,2176]{1,0:T(8,128)(2,1)}, bf16[128,2176]{1,0:T(8,128)(2,1)}...) custom-call(s32[1]{0:T(128)} %bitcast.53.own_ref, ...), custom_call_target="tpu_custom_call" | custom-call | flops 1 | bytes 1 | tf_op jit(solution)/shard_map/pallas_call | solution.py:600
  521.4 15.5 %shard_map.240 = f32[1024,2048]{1,0:T(8,128)} custom-call(bf16[512,1024]{1,0:T(8,128)(2,1)S(1)} %get-tuple-element.1457.refs_0_, bf16[512,1024]{1,0:T(8,128)(2,1)} %copy-done.143, bf16[512,1024]{1,0:T(8,128)(2,1)} %copy-done.144, bf16[512,1024]{1,0:T(8,128)(2,1)} %get-tuple-element.1460.refs_3_, bf16[512,2048]{1,0:T(8,128)(2,1)} %get-tuple-element.1461.refs_4_, ...), custom_call_target="tpu_custom_call" | custom-call | flops 1 | bytes 1 | tf_op jit(solution)/shard_map/pallas_call | solution.py:639
  588.8 14.9 %collective-permute-start.82 = (bf16[256,2048]{1,0:T(8,128)(2,1)S(1)}, bf16[256,2048]{1,0:T(8,128)(2,1)S(1)}, u32[]{:S(2)}, u32[]{:S(2)}) collective-permute-start(bf16[256,2048]{1,0:T(8,128)(2,1)S(1)} %get-tuple-element.1542), channel_id=1, source_target_pairs={{0,16},{16,0},{1,17},{17,1},{2,18},{18,2},{3,19},{19,3},{4,20},{20... | collective-permute-start | bytes 3145736 | tf_op jit(solution)/shard_map/ppermute | solution.py:184
  607.7 19.1 %shard_map.242 = (bf16[3,256,2048]{2,1,0:T(8,128)(2,1)}, f32[8,2048]{1,0:T(8,128)S(1)}) custom-call(bf16[256,2048]{1,0:T(8,128)(2,1)S(1)} %fusion.15.grad_ref, bf16[256,2048]{1,0:T(8,128)(2,1)S(1)} %copy-done.27, bf16[256,2048]{1,0:T(8,128)(2,1)S(1)} %copy-done.29, bf16[256,2048]{1,0:T(8,128)(2,1)S(1)} %copy-done.31, f32[16,256,256]{2,1,0:T(8,128)S(1)} %copy-done.13, ...), custom_call_target="tpu_custom_call" | custom-call | flops 1 | bytes 1 | tf_op jit(solution)/shard_map/pallas_call | solution.py:530
  657.4 12.0 %shard_map.243.grad_ref = f32[256,2048]{1,0:T(8,128)S(1)} custom-call(bf16[3,256,2048]{2,1,0:T(8,128)(2,1)} %get-tuple-element.1652.left_ref, bf16[4,4,64,2048]{3,2,1,0:T(8,128)(2,1)S(1)} %bitcast.221, bf16[4,4,64,2048]{3,2,1,0:T(8,128)(2,1)S(1)} %copy-done.8, bf16[4,4,64,2048]{3,2,1,0:T(8,128)(2,1)} %bitcast.226, bf16[4,4,64,2048]{3,2,1,0:T(8,128)(2,1)} %copy-done.9, ...), custom_call_target="tpu_custom_call" | custom-call | flops 1 | bytes 1 | tf_op jit(solution)/shard_map/pallas_call | solution.py:391
  695.5 7.7 shard_map.245
  713.9 5.0 collective-permute-done.92.refs_0_
  740.3 13.9 %shard_map.247 = f32[2048,1024]{1,0:T(8,128)} custom-call(bf16[512,2048]{1,0:T(8,128)(2,1)} %copy-done.60, bf16[512,2048]{1,0:T(8,128)(2,1)} %copy-done.61, bf16[512,2048]{1,0:T(8,128)(2,1)} %copy-done.62, bf16[512,2048]{1,0:T(8,128)(2,1)} %copy-done.63, bf16[512,1024]{1,0:T(8,128)(2,1)S(1)} %copy-done.33, bf16[512,1024]{1,0:T(8,128)(2,1)} %get-tuple-element.1643.refs_5_, ...), custom_call_target="tpu_custom_call" | custom-call | flops 1 | bytes 1 | tf_op jit(solution)/shard_map/pallas_call | solution.py:639
  787.5 13.5 %shard_map.249 = f32[2048,1024]{1,0:T(8,128)} custom-call(bf16[512,2048]{1,0:T(8,128)(2,1)} %copy-done.60, bf16[512,2048]{1,0:T(8,128)(2,1)} %copy-done.61, bf16[512,2048]{1,0:T(8,128)(2,1)} %copy-done.62, bf16[512,2048]{1,0:T(8,128)(2,1)} %copy-done.63, bf16[512,1024]{1,0:T(8,128)(2,1)S(1)} %copy-done.32, bf16[512,1024]{1,0:T(8,128)(2,1)} %get-tuple-element.1677.refs_5_, ...), custom_call_target="tpu_custom_call" | custom-call | flops 1 | bytes 1 | tf_op jit(solution)/shard_map/pallas_call | solution.py:639
  831.2 15.8 %collective-permute-done.109 = bf16[66,2048]{1,0:T(8,128)(2,1)S(1)} collective-permute-done((bf16[66,2048]{1,0:T(8,128)(2,1)S(1)}, bf16[66,2048]{1,0:T(8,128)(2,1)S(1)}, u32[]{:S(2)}, u32[]{:S(2)}) %collective-permute-start.109) | collective-permute-done | bytes 270368 | tf_op jit(solution)/shard_map/ppermute | solution.py:180
  847.0 7.2 collective-permute-done.110
  863.5 15.0 %collective-permute-done.112 = bf16[64,2048]{1,0:T(8,128)(2,1)S(1)} collective-permute-done((bf16[64,2048]{1,0:T(8,128)(2,1)S(1)}, bf16[64,2048]{1,0:T(8,128)(2,1)S(1)}, u32[]{:S(2)}, u32[]{:S(2)}) %collective-permute-start.112) | collective-permute-done | bytes 262176 | tf_op jit(solution)/shard_map/ppermute | solution.py:180
  (940 shorter events, 518.3 us)
Async XLA Ops:
  44.7 32.0 %collective-permute-start.10 = (bf16[6,64,2048]{2,1,0:T(8,128)(2,1)}, bf16[6,64,2048]{2,1,0:T(8,128)(2,1)}, u32[]{:S(2)}, u32[]{:S(2)}) collective-permute-start(bf16[6,64,2048]{2,1,0:T(8,128)(2,1)} %get-tuple-element.901), channel_id=1, source_target_pairs={{0,1},{1,0},{2,3},{3,2},{4,5},{5,4},{6,7},{7,6},{8,9},{9,8},{10,11... | collective-permute-start | bytes 4718600 | tf_op jit(solution)/shard_map/ppermute | solution.py:171
  45.9 31.1 %collective-permute-start.11 = (bf16[6,64,2048]{2,1,0:T(8,128)(2,1)}, bf16[6,64,2048]{2,1,0:T(8,128)(2,1)}, u32[]{:S(2)}, u32[]{:S(2)}) collective-permute-start(bf16[6,64,2048]{2,1,0:T(8,128)(2,1)} %get-tuple-element.902), channel_id=1, source_target_pairs={{0,2},{1,3},{2,0},{3,1},{4,6},{5,7},{6,4},{7,5},{8,10},{9,11},{10,... | collective-permute-start | bytes 4718600 | tf_op jit(solution)/shard_map/ppermute | solution.py:171
  82.2 29.4 %collective-permute-start.15 = (bf16[6,64,2048]{2,1,0:T(8,128)(2,1)S(1)}, bf16[6,64,2048]{2,1,0:T(8,128)(2,1)S(1)}, u32[]{:S(2)}, u32[]{:S(2)}) collective-permute-start(bf16[6,64,2048]{2,1,0:T(8,128)(2,1)S(1)} %get-tuple-element.928), channel_id=1, source_target_pairs={{0,2},{1,3},{2,0},{3,1},{4,6},{5,7},{6,4},{7,5},{8,10},{9,11},{10,... | collective-permute-start | bytes 4718600 | tf_op jit(solution)/shard_map/ppermute | solution.py:171
  198.5 35.4 %collective-permute-start.30 = (bf16[256,2048]{1,0:T(8,128)(2,1)}, bf16[256,2048]{1,0:T(8,128)(2,1)S(1)}, u32[]{:S(2)}, u32[]{:S(2)}) collective-permute-start(bf16[256,2048]{1,0:T(8,128)(2,1)} %pad_maximum_fusion.20), channel_id=1, source_target_pairs={{0,3},{1,2},{2,1},{3,0},{4,7},{5,6},{6,5},{7,4},{8,11},{9,10},{10,... | collective-permute-start | bytes 3145736 | tf_op jit(solution)/shard_map/ppermute | solution.py:171
  199.5 34.4 %collective-permute-start.31 = (bf16[256,2048]{1,0:T(8,128)(2,1)}, bf16[256,2048]{1,0:T(8,128)(2,1)S(1)}, u32[]{:S(2)}, u32[]{:S(2)}) collective-permute-start(bf16[256,2048]{1,0:T(8,128)(2,1)} %copy-done.145), channel_id=1, source_target_pairs={{4,0},{5,1},{6,2},{7,3},{8,12},{9,13},{10,14},{11,15},{20,16},{21,... | collective-permute-start | bytes 3145736 | tf_op jit(solution)/shard_map/ppermute | solution.py:180
  241.1 45.2 %collective-permute-start.34 = (bf16[256,2048]{1,0:T(8,128)(2,1)}, bf16[256,2048]{1,0:T(8,128)(2,1)S(1)}, u32[]{:S(2)}, u32[]{:S(2)}) collective-permute-start(bf16[256,2048]{1,0:T(8,128)(2,1)} %pad_maximum_fusion.22), channel_id=1, source_target_pairs={{0,1},{1,0},{2,3},{3,2},{4,5},{5,4},{6,7},{7,6},{8,9},{9,8},{10,11... | collective-permute-start | bytes 3145736 | tf_op jit(solution)/shard_map/ppermute | solution.py:171
  242.0 44.3 %collective-permute-start.35 = (bf16[256,2048]{1,0:T(8,128)(2,1)S(1)}, bf16[256,2048]{1,0:T(8,128)(2,1)S(1)}, u32[]{:S(2)}, u32[]{:S(2)}) collective-permute-start(bf16[256,2048]{1,0:T(8,128)(2,1)S(1)} %copy-done.149), channel_id=1, source_target_pairs={{0,2},{1,3},{2,0},{3,1},{4,6},{5,7},{6,4},{7,5},{8,10},{9,11},{10,... | collective-permute-start | bytes 3145736 | tf_op jit(solution)/shard_map/ppermute | solution.py:171
  243.1 46.3 %collective-permute-start.36 = (bf16[256,2048]{1,0:T(8,128)(2,1)S(1)}, bf16[256,2048]{1,0:T(8,128)(2,1)}, u32[]{:S(2)}, u32[]{:S(2)}) collective-permute-start(bf16[256,2048]{1,0:T(8,128)(2,1)S(1)} %copy-done.150), channel_id=1, source_target_pairs={{0,3},{1,2},{2,1},{3,0},{4,7},{5,6},{6,5},{7,4},{8,11},{9,10},{10,... | collective-permute-start | bytes 3145736 | tf_op jit(solution)/shard_map/ppermute | solution.py:171
  243.9 42.4 %collective-permute-start.37 = (bf16[256,1024]{1,0:T(8,128)(2,1)}, bf16[256,1024]{1,0:T(8,128)(2,1)S(1)}, u32[]{:S(2)}, u32[]{:S(2)}) collective-permute-start(bf16[256,1024]{1,0:T(8,128)(2,1)} %get-tuple-element.1047), channel_id=1, source_target_pairs={{0,16},{16,0},{1,17},{17,1},{2,18},{18,2},{3,19},{19,3},{4,20},{20... | collective-permute-start | bytes 1572872 | tf_op jit(solution)/shard_map/ppermute | solution.py:184
  315.7 29.3 %collective-permute-start.43 = (bf16[256,2048]{1,0:T(8,128)(2,1)S(1)}, bf16[256,2048]{1,0:T(8,128)(2,1)S(1)}, u32[]{:S(2)}, u32[]{:S(2)}) collective-permute-start(bf16[256,2048]{1,0:T(8,128)(2,1)S(1)} %collective-permute-done.39), channel_id=1, source_target_pairs={{4,0},{5,1},{6,2},{7,3},{8,12},{9,13},{10,14},{11,15},{20,16},{21,... | collective-permute-start | bytes 3145736 | tf_op jit(solution)/shard_map/ppermute | solution.py:180
  407.3 31.8 %collective-permute-start.56 = (bf16[128,2048]{1,0:T(8,128)(2,1)}, bf16[128,2048]{1,0:T(8,128)(2,1)}, u32[]{:S(2)}, u32[]{:S(2)}) collective-permute-start(bf16[128,2048]{1,0:T(8,128)(2,1)} %get-tuple-element.1198), channel_id=1, source_target_pairs={{0,1},{1,0},{2,3},{3,2},{4,5},{5,4},{6,7},{7,6},{8,9},{9,8},{10,11... | collective-permute-start | bytes 1572872 | tf_op jit(solution)/shard_map/ppermute | solution.py:171
  408.3 30.8 %collective-permute-start.57 = (bf16[128,2048]{1,0:T(8,128)(2,1)}, bf16[128,2048]{1,0:T(8,128)(2,1)}, u32[]{:S(2)}, u32[]{:S(2)}) collective-permute-start(bf16[128,2048]{1,0:T(8,128)(2,1)} %get-tuple-element.1199), channel_id=1, source_target_pairs={{0,2},{1,3},{2,0},{3,1},{4,6},{5,7},{6,4},{7,5},{8,10},{9,11},{10,... | collective-permute-start | bytes 1572872 | tf_op jit(solution)/shard_map/ppermute | solution.py:171
  408.3 30.8 %collective-permute-start.58 = (bf16[128,2048]{1,0:T(8,128)(2,1)}, bf16[128,2048]{1,0:T(8,128)(2,1)}, u32[]{:S(2)}, u32[]{:S(2)}) collective-permute-start(bf16[128,2048]{1,0:T(8,128)(2,1)} %get-tuple-element.1200), channel_id=1, source_target_pairs={{0,3},{1,2},{2,1},{3,0},{4,7},{5,6},{6,5},{7,4},{8,11},{9,10},{10,... | collective-permute-start | bytes 1572872 | tf_op jit(solution)/shard_map/ppermute | solution.py:171
  588.8 40.1 %collective-permute-start.82 = (bf16[256,2048]{1,0:T(8,128)(2,1)S(1)}, bf16[256,2048]{1,0:T(8,128)(2,1)S(1)}, u32[]{:S(2)}, u32[]{:S(2)}) collective-permute-start(bf16[256,2048]{1,0:T(8,128)(2,1)S(1)} %get-tuple-element.1542), channel_id=1, source_target_pairs={{0,16},{16,0},{1,17},{17,1},{2,18},{18,2},{3,19},{19,3},{4,20},{20... | collective-permute-start | bytes 3145736 | tf_op jit(solution)/shard_map/ppermute | solution.py:184
  603.7 30.8 %collective-permute-start.83 = (bf16[128,2048]{1,0:T(8,128)(2,1)}, bf16[128,2048]{1,0:T(8,128)(2,1)}, u32[]{:S(2)}, u32[]{:S(2)}) collective-permute-start(bf16[128,2048]{1,0:T(8,128)(2,1)} %get-tuple-element.1544), channel_id=1, source_target_pairs={{0,1},{1,0},{2,3},{3,2},{4,5},{5,4},{6,7},{7,6},{8,9},{9,8},{10,11... | collective-permute-start | bytes 1572872 | tf_op jit(solution)/shard_map/ppermute | solution.py:171
  605.1 29.4 %collective-permute-start.84 = (bf16[128,2048]{1,0:T(8,128)(2,1)}, bf16[128,2048]{1,0:T(8,128)(2,1)}, u32[]{:S(2)}, u32[]{:S(2)}) collective-permute-start(bf16[128,2048]{1,0:T(8,128)(2,1)} %get-tuple-element.1545), channel_id=1, source_target_pairs={{0,2},{1,3},{2,0},{3,1},{4,6},{5,7},{6,4},{7,5},{8,10},{9,11},{10,... | collective-permute-start | bytes 1572872 | tf_op jit(solution)/shard_map/ppermute | solution.py:171
  605.1 29.4 %collective-permute-start.85 = (bf16[128,2048]{1,0:T(8,128)(2,1)}, bf16[128,2048]{1,0:T(8,128)(2,1)}, u32[]{:S(2)}, u32[]{:S(2)}) collective-permute-start(bf16[128,2048]{1,0:T(8,128)(2,1)} %get-tuple-element.1546), channel_id=1, source_target_pairs={{0,3},{1,2},{2,1},{3,0},{4,7},{5,6},{6,5},{7,4},{8,11},{9,10},{10,... | collective-permute-start | bytes 1572872 | tf_op jit(solution)/shard_map/ppermute | solution.py:171
  640.7 33.1 %collective-permute-start.87 = (bf16[512,1024]{1,0:T(8,128)(2,1)}, bf16[512,1024]{1,0:T(8,128)(2,1)S(1)}, u32[]{:S(2)}, u32[]{:S(2)}) collective-permute-start(bf16[512,1024]{1,0:T(8,128)(2,1)} %convolution_convert_fusion.20), channel_id=1, source_target_pairs={{0,1},{1,0},{2,3},{3,2},{4,5},{5,4},{6,7},{7,6},{8,9},{9,8},{10,11... | collective-permute-start | bytes 3145736 | tf_op jit(solution)/shard_map/ppermute | solution.py:171
  642.2 31.6 %collective-permute-start.88 = (bf16[512,1024]{1,0:T(8,128)(2,1)}, bf16[512,1024]{1,0:T(8,128)(2,1)S(1)}, u32[]{:S(2)}, u32[]{:S(2)}) collective-permute-start(bf16[512,1024]{1,0:T(8,128)(2,1)} %convolution_convert_fusion.19), channel_id=1, source_target_pairs={{0,2},{1,3},{2,0},{3,1},{4,6},{5,7},{6,4},{7,5},{8,10},{9,11},{10,... | collective-permute-start | bytes 3145736 | tf_op jit(solution)/shard_map/ppermute | solution.py:171
  642.2 31.7 %collective-permute-start.89 = (bf16[256,2048]{1,0:T(8,128)(2,1)}, bf16[256,2048]{1,0:T(8,128)(2,1)}, u32[]{:S(2)}, u32[]{:S(2)}) collective-permute-start(bf16[256,2048]{1,0:T(8,128)(2,1)} %add_convert_fusion.6), channel_id=1, source_target_pairs={{4,8},{5,9},{6,10},{7,11},{8,4},{9,5},{10,6},{11,7},{20,24},{21,25... | collective-permute-start | bytes 3145736 | tf_op jit(solution)/shard_map/ppermute | solution.py:180
  683.2 35.7 %collective-permute-start.92 = (bf16[768,1024]{1,0:T(8,128)(2,1)}, bf16[768,1024]{1,0:T(8,128)(2,1)}, u32[]{:S(2)}, u32[]{:S(2)}) collective-permute-start(bf16[768,1024]{1,0:T(8,128)(2,1)} %get-tuple-element.1605), channel_id=1, source_target_pairs={{0,1},{1,0},{2,3},{3,2},{4,5},{5,4},{6,7},{7,6},{8,9},{9,8},{10,11... | collective-permute-start | bytes 4718600 | tf_op jit(solution)/shard_map/ppermute | solution.py:171
  683.4 35.5 %collective-permute-start.93 = (bf16[768,1024]{1,0:T(8,128)(2,1)}, bf16[768,1024]{1,0:T(8,128)(2,1)}, u32[]{:S(2)}, u32[]{:S(2)}) collective-permute-start(bf16[768,1024]{1,0:T(8,128)(2,1)} %get-tuple-element.1606), channel_id=1, source_target_pairs={{0,2},{1,3},{2,0},{3,1},{4,6},{5,7},{6,4},{7,5},{8,10},{9,11},{10,... | collective-permute-start | bytes 4718600 | tf_op jit(solution)/shard_map/ppermute | solution.py:171
  684.7 34.2 %collective-permute-start.94 = (bf16[256,2048]{1,0:T(8,128)(2,1)}, bf16[256,2048]{1,0:T(8,128)(2,1)}, u32[]{:S(2)}, u32[]{:S(2)}) collective-permute-start(bf16[256,2048]{1,0:T(8,128)(2,1)} %add_convert_fusion.5), channel_id=1, source_target_pairs={{0,4},{1,5},{2,6},{3,7},{4,0},{5,1},{6,2},{7,3},{8,12},{9,13},{10,... | collective-permute-start | bytes 3145736 | tf_op jit(solution)/shard_map/ppermute | solution.py:180
  687.9 31.0 %collective-permute-start.95 = (bf16[256,2048]{1,0:T(8,128)(2,1)}, bf16[256,2048]{1,0:T(8,128)(2,1)}, u32[]{:S(2)}, u32[]{:S(2)}) collective-permute-start(bf16[256,2048]{1,0:T(8,128)(2,1)} %add_convert_fusion.4), channel_id=1, source_target_pairs={{4,8},{5,9},{6,10},{7,11},{8,4},{9,5},{10,6},{11,7},{20,24},{21,25... | collective-permute-start | bytes 3145736 | tf_op jit(solution)/shard_map/ppermute | solution.py:180
  729.4 35.6 %collective-permute-start.96 = (bf16[800,1024]{1,0:T(8,128)(2,1)S(1)}, bf16[800,1024]{1,0:T(8,128)(2,1)S(1)}, u32[]{:S(2)}, u32[]{:S(2)}) collective-permute-start(bf16[800,1024]{1,0:T(8,128)(2,1)S(1)} %get-tuple-element.1636), channel_id=1, source_target_pairs={{0,1},{1,0},{2,3},{3,2},{4,5},{5,4},{6,7},{7,6},{8,9},{9,8},{10,11... | collective-permute-start | bytes 4915208 | tf_op jit(solution)/shard_map/ppermute | solution.py:171
  730.5 34.1 %collective-permute-start.97 = (bf16[768,1024]{1,0:T(8,128)(2,1)}, bf16[768,1024]{1,0:T(8,128)(2,1)S(1)}, u32[]{:S(2)}, u32[]{:S(2)}) collective-permute-start(bf16[768,1024]{1,0:T(8,128)(2,1)} %get-tuple-element.1637), channel_id=1, source_target_pairs={{0,2},{1,3},{2,0},{3,1},{4,6},{5,7},{6,4},{7,5},{8,10},{9,11},{10,... | collective-permute-start | bytes 4718600 | tf_op jit(solution)/shard_map/ppermute | solution.py:171
  731.7 33.4 %collective-permute-start.98 = (bf16[64,2048]{1,0:T(8,128)(2,1)}, bf16[64,2048]{1,0:T(8,128)(2,1)S(1)}, u32[]{:S(2)}, u32[]{:S(2)}) collective-permute-start(bf16[64,2048]{1,0:T(8,128)(2,1)} %get-tuple-element.1649), channel_id=1, source_target_pairs={{0,4},{1,5},{2,6},{3,7},{4,8},{5,9},{6,10},{7,11},{8,12},{9,13},{1... | collective-permute-start | bytes 786440 | tf_op jit(solution)/shard_map/ppermute | solution.py:180
  731.8 33.3 %collective-permute-start.99 = (bf16[64,2048]{1,0:T(8,128)(2,1)}, bf16[64,2048]{1,0:T(8,128)(2,1)}, u32[]{:S(2)}, u32[]{:S(2)}) collective-permute-start(bf16[64,2048]{1,0:T(8,128)(2,1)} %get-tuple-element.1650), channel_id=1, source_target_pairs={{0,8},{1,9},{2,10},{3,11},{4,12},{5,13},{6,14},{7,15},{8,0},{9,1},... | collective-permute-start | bytes 786440 | tf_op jit(solution)/shard_map/ppermute | solution.py:180
  776.8 33.6 %collective-permute-start.102 = (bf16[784,1024]{1,0:T(8,128)(2,1)S(1)}, bf16[784,1024]{1,0:T(8,128)(2,1)S(1)}, u32[]{:S(2)}, u32[]{:S(2)}) collective-permute-start(bf16[784,1024]{1,0:T(8,128)(2,1)S(1)} %get-tuple-element.1670), channel_id=1, source_target_pairs={{0,2},{1,3},{2,0},{3,1},{4,6},{5,7},{6,4},{7,5},{8,10},{9,11},{10,... | collective-permute-start | bytes 4816904 | tf_op jit(solution)/shard_map/ppermute | solution.py:171
  777.7 32.6 %collective-permute-start.101 = (bf16[768,1024]{1,0:T(8,128)(2,1)}, bf16[768,1024]{1,0:T(8,128)(2,1)S(1)}, u32[]{:S(2)}, u32[]{:S(2)}) collective-permute-start(bf16[768,1024]{1,0:T(8,128)(2,1)} %get-tuple-element.1669), channel_id=1, source_target_pairs={{0,1},{1,0},{2,3},{3,2},{4,5},{5,4},{6,7},{7,6},{8,9},{9,8},{10,11... | collective-permute-start | bytes 4718600 | tf_op jit(solution)/shard_map/ppermute | solution.py:171
  820.9 33.4 %collective-permute-start.106 = (bf16[256,1024]{1,0:T(8,128)(2,1)S(1)}, bf16[256,1024]{1,0:T(8,128)(2,1)S(1)}, u32[]{:S(2)}, u32[]{:S(2)}) collective-permute-start(bf16[256,1024]{1,0:T(8,128)(2,1)S(1)} %get-tuple-element.1703), channel_id=1, source_target_pairs={{0,1},{1,0},{2,3},{3,2},{4,5},{5,4},{6,7},{7,6},{8,9},{9,8},{10,11... | collective-permute-start | bytes 1572872 | tf_op jit(solution)/shard_map/ppermute | solution.py:171
  822.1 32.1 %collective-permute-start.107 = (bf16[256,1024]{1,0:T(8,128)(2,1)S(1)}, bf16[256,1024]{1,0:T(8,128)(2,1)S(1)}, u32[]{:S(2)}, u32[]{:S(2)}) collective-permute-start(bf16[256,1024]{1,0:T(8,128)(2,1)S(1)} %get-tuple-element.1704), channel_id=1, source_target_pairs={{0,2},{1,3},{2,0},{3,1},{4,6},{5,7},{6,4},{7,5},{8,10},{9,11},{10,... | collective-permute-start | bytes 1572872 | tf_op jit(solution)/shard_map/ppermute | solution.py:171
  (292 other events, 3650.8 us)

commit v4 on v3

--- a/solution.py
+++ b/solution.py
@@ -268,14 +268,7 @@
         return width // self.cores // self.nx
 
     def line_parts(self, terms):
-        full = jnp.float32
-        if not self.square:
-            total = sum(t.astype(full) for t in terms)
-        else:
-            from_y, from_x, near_x, near_y = terms
-            total = jnp.concatenate(
-                [near_x + from_y.astype(full), near_y + from_x.astype(full)], axis=1
-            )
+        total = sum(t.astype(jnp.float32) for t in terms)
         shard = total.shape[0] // self.nz
         parts = [total[k * shard : (k + 1) * shard] for k in range(self.nz)]
         return parts[:1] + [part.astype(jnp.bfloat16) for part in parts[1:]]
@@ -334,6 +327,37 @@
         compiler_params=pltpu.CompilerParams(vmem_limit_bytes=40 << 20),
         cost_estimate=BESIDE,
     )(*came, *near, *far, *[m for m in more if m is not None])
+
+
+def line_fold(came, at, keep, count, more):
+    line, width = keep[0].shape
+    each = line // count
+    full = jnp.float32
+
+    def body(came_x, came_y, keep_x, keep_y, *refs):
+        for p, out in enumerate(refs[-count:]):
+            rows = slice(p * each, (p + 1) * each)
+            out[:each, :width] = (keep_x[rows, :] + came_y[rows, :].astype(full)).astype(out.dtype)
+            out[:each, width:] = (keep_y[rows, :] + came_x[rows, :].astype(full)).astype(out.dtype)
+            if more:
+                out[each:, :] = refs[p][...]
+
+    def whole(shape):
+        return pl.BlockSpec(shape, lambda i: (0, 0))
+
+    shape = (each + (more[0].shape[0] if more else 0), 2 * width)
+    return pl.pallas_call(
+        body,
+        grid=(1,),
+        in_specs=[pl.BlockSpec((line, width), lambda i: (at // line, 0))] * 2
+        + [whole(value.shape) for value in (*keep, *more)],
+        out_specs=[whole(shape)] * count,
+        out_shape=[
+            jax.ShapeDtypeStruct(shape, full if p == 0 else jnp.bfloat16) for p in range(count)
+        ],
+        compiler_params=pltpu.CompilerParams(vmem_limit_bytes=40 << 20),
+        cost_estimate=BESIDE,
+    )(*came, *keep, *more)
 
 
 def times_gathered(left, pieces, start, stop, so_far=None):
@@ -546,31 +570,23 @@
     )(grad_out, query, key, value, probs, projected, inverses, gains, *tables)
 
 
-def expert_back(pieces, cot, gate, result, pre_gate, pre_up, gate_w, up_w, down_w, own):
-    total, width = cot.shape
+def expert_back(pieces, grad_y, tail, pre_gate, pre_up, gate_w, up_w, down_w):
+    total, width = grad_y.shape
     rows = min(512, total)
     pieces = pieces if rows == total else 1
     hidden = pre_gate.shape[1]
     low, full = jnp.bfloat16, jnp.float32
     tile = min(512, hidden)
 
-    def body(own_ref, cot_ref, gate_ref, result_ref, a_ref, b_ref, gate_w_ref, up_w_ref, down_w_ref,
-             *refs):
-        back_refs, (grad_y_ref, grad_a_ref, grad_b_ref, sum_ref) = refs[:pieces], refs[pieces:]
+    def body(grad_y_ref, tail_ref, a_ref, b_ref, gate_w_ref, up_w_ref, down_w_ref, *refs):
+        back_refs, (grad_a_ref, grad_b_ref, sum_ref) = refs[:pieces], refs[pieces:]
         each = rows // pieces
         step = pl.program_id(1)
 
         @pl.when(step == 0)
         def _():
-            cot_f = cot_ref[...].astype(full)
-            grad_y_ref[...] = (gate_ref[...] * cot_f).astype(low)
-            grad_g = jnp.sum(cot_f * result_ref[...].astype(full), axis=-1, keepdims=True)
-            high = grad_g.astype(low).astype(full)
-            lanes = lax.broadcasted_iota(jnp.int32, (rows, LANES), 1)
-            tail = jnp.where(lanes == own_ref[0], high, 0.0)
-            tail = jnp.where(lanes == own_ref[0] + LANES // 2, grad_g - high, tail)
             for p, back_ref in enumerate(back_refs):
-                back_ref[:, width:] = tail[p * each : (p + 1) * each].astype(low)
+                back_ref[:, width:] = tail_ref[p * each : (p + 1) * each, :]
             sum_ref[...] = jnp.zeros_like(sum_ref)
 
         grad_act = lax.dot_general(
@@ -601,22 +617,17 @@
         body,
         grid=(total // rows, hidden // tile),
         in_specs=[
-            pl.BlockSpec(memory_space=pltpu.SMEM),
-            whole(width), whole(1), whole(width), inner, inner, into, into,
+            whole(width), whole(LANES), inner, inner, into, into,
             pl.BlockSpec((tile, width), lambda r, f: (f, 0)),
         ],
         out_specs=[pl.BlockSpec((rows // pieces, width + LANES), lambda r, f: (r, 0))] * pieces
-        + [whole(width), inner, inner],
+        + [inner, inner],
         out_shape=[jax.ShapeDtypeStruct((total // pieces, width + LANES), low)] * pieces
-        + [
-            jax.ShapeDtypeStruct(cot.shape, low),
-            jax.ShapeDtypeStruct(pre_gate.shape, low),
-            jax.ShapeDtypeStruct(pre_gate.shape, low),
-        ],
+        + [jax.ShapeDtypeStruct(pre_gate.shape, low)] * 2,
         scratch_shapes=[pltpu.VMEM((rows, width), full)],
         compiler_params=pltpu.CompilerParams(vmem_limit_bytes=52 << 20),
         cost_estimate=BESIDE,
-    )(own.reshape(1), cot, gate, result, pre_gate, pre_up, gate_w, up_w, down_w)
+    )(grad_y, tail, pre_gate, pre_up, gate_w, up_w, down_w)
     return (outs[:pieces], *outs[pieces:])
 
 
@@ -868,7 +879,7 @@
             pieces.append(share(chunks[k - 3]))
         if k > 1:
             chunks.append(chunk_of(k - 2))
-        if k == 2:
+        if k == 1:
             smalls = jnp.stack(smalls, axis=1)
             smalls = [smalls] + [here.other_core(smalls, s) for s in range(1, here.cores)]
             smalls = jnp.stack(smalls, axis=1).reshape(width, -1)
@@ -882,9 +893,6 @@
             in_order = product(normed_in, arrival).astype(bfloat)
         if k > 2:
             projected = project(k - 3)
-        if k == 1:
-            both_w = jnp.concatenate([gate_w, up_w], axis=1)
-            spreads, both_w = tie(spreads, both_w)
         if k >= here.nz - 1 and k - here.nz + 1 < here.nz:
             at = k - here.nz + 1
             cot_rows[at] = rows_of(spreads[at], cot_line.queue[at])
@@ -934,23 +942,31 @@
 
     own_label = labels[None, :] == here.me
 
-    def expert_forward(arrived):
+    def expert_forward(arrived, cot):
         route_here = jax.nn.softmax(product(arrived, wr), axis=-1)
         gate = jnp.sum(jnp.where(own_label, route_here, 0.0), axis=-1)
         gate = gate.astype(bfloat).astype(jnp.float32)[:, None]
         pre_gate = product(arrived, gate_w)
         pre_up = product(arrived, up_w)
         activated = (jax.nn.silu(pre_gate) * pre_up).astype(bfloat)
-        result = product(activated, down_w).astype(bfloat)
-        gated = (gate * result.astype(jnp.float32)).astype(bfloat)
-        return (gate, pre_gate, pre_up, activated, result, gated)
-
-    def expert_backward(kept, cot):
-        gate, pre_gate, pre_up, _, result, _ = kept
-        back, *kept = expert_back(
-            plane, cot, gate, result, pre_gate, pre_up, gate_w, up_w, down_w, here.me
+        result = product(activated, down_w).astype(bfloat).astype(jnp.float32)
+        gated = (gate * result).astype(bfloat)
+        cot = cot.astype(jnp.float32)
+        grad_y = (gate * cot).astype(bfloat)
+        grad_g = jnp.sum(cot * result, axis=-1, keepdims=True)
+        high = grad_g.astype(bfloat)
+        low = (grad_g - high.astype(jnp.float32)).astype(bfloat)
+        lanes = jnp.arange(LANES, dtype=jnp.int32)[None, :]
+        tail = jnp.where(lanes == here.me, high, jnp.zeros((), bfloat))
+        tail = jnp.where(lanes == here.me + LANES // 2, low, tail)
+        return (pre_gate, pre_up, activated, gated, grad_y, tail)
+
+    def expert_backward(kept):
+        pre_gate, pre_up, _, _, grad_y, tail = kept
+        back, grad_a, grad_b = expert_back(
+            plane, grad_y, tail, pre_gate, pre_up, gate_w, up_w, down_w
         )
-        return [back if len(back) == plane else parted(back[0]), *kept]
+        return [back if len(back) == plane else parted(back[0]), grad_y, grad_a, grad_b]
 
     rows_next = rows_of(spreads[0], normed_mid)
     out_columns = here.core_columns(attended)
@@ -971,7 +987,7 @@
         rows = here.along_plane(rows_next)
         if k > 0:
             rows_in[-1] = joined(rows_in[-1])
-            forward.append(expert_forward(rows_in[-1]))
+            forward.append(expert_forward(rows_in[-1], joined(rows_cot[k - 1])))
         if k == 0:
             targets = targeted(in_columns)
             rows, targets = tie(rows, targets)
@@ -979,9 +995,8 @@
             out_columns = here.to_cores(out_columns)
         if k == here.nz - 1:
             out_columns = targeted(out_columns)
-        for j in order[here.nz - k - (k == here.nz - 1) : here.nz - k + 1] if k > 0 else []:
-            rows_cot[j] = joined(rows_cot[j])
-            rows, rows_cot[j] = tie(rows, rows_cot[j])
+            rows_cot[k] = joined(rows_cot[k])
+            rows, rows_cot[k] = tie(rows, rows_cot[k])
         moving, rows, forward, out_columns = tie(moving, rows, forward, out_columns)
         rows_in.append(rows)
         line.land(moving)
@@ -996,11 +1011,11 @@
         k = todo.pop(0) if todo else None
         if k == "forward":
             rows_in[-1] = joined(rows_in[-1])
-            forward.append(expert_forward(rows_in[-1]))
+            forward.append(expert_forward(rows_in[-1], rows_cot[-1]))
         elif k is not None:
-            backward[k] = expert_backward(forward[k], rows_cot[k])
-
-    rows_next = parted(forward[0][5])
+            backward[k] = expert_backward(forward[k])
+
+    rows_next = parted(forward[0][3])
     rows_next, forward, rows_in, rows_cot, out_columns = tie(
         rows_next, forward, rows_in, rows_cot, out_columns
     )
@@ -1016,32 +1031,32 @@
         if k + 2 < here.nz:
             collect.land(moving)
             sending = collect.add(k + 2, parts[k + 2])
-        rows_next, sending, forward, backward, back = tie(
-            rows_next, sending, forward, backward, back
-        )
+        rows_next, sending, forward, backward = tie(rows_next, sending, forward, backward)
         rows = here.deal_back(rows_next)
         moving = collect.send(sending)
         if k > 0:
             work()
         else:
             grad_down = rows_product(
-                [kept[3] for kept in forward], [kept[1] for kept in backward]
+                [kept[2] for kept in forward], [kept[1] for kept in backward]
             )
             rows, grad_down = tie(rows, grad_down)
         if back is not None:
             parts[k + 1] = contract_rows(spreads[k + 1], joined(back))
-        moving, rows, forward, backward, parts = tie(moving, rows, forward, backward, parts)
+        moving, rows[:-1], forward, backward, parts = tie(
+            moving, rows[:-1], forward, backward, parts
+        )
         back = rows
     late = list(order[:0:-1])
     collect.land(moving)
     sending = collect.add(1, parts[1])
-    rows_next = parted(forward[late[0]][5])
-    rows_next, sending, back, back_y = tie(rows_next, sending, back, back_y)
+    rows_next = parted(forward[late[0]][3])
+    rows_next, sending, back_y = tie(rows_next, sending, back_y)
     rows = here.deal_back(rows_next)
     moving = collect.send(sending)
     parts[0] = contract_rows(spreads[0], joined(back))
     part_y = contract_rows(spreads[0], joined(back_y[0]))
-    rows_next = [parted(forward[k][5]) for k in late[1:]]
+    rows_next = [parted(forward[k][3]) for k in late[1:]]
     moving, rows, parts, rows_next, part_y = tie(moving, rows, parts, rows_next, part_y)
     collect.land(moving)
     collect.add(0, parts[0])
@@ -1100,7 +1115,7 @@
 
     jobs = 4
     lefts, rights = [targets_out, targets, targets, targets], [out_tokens]
-    lasts, shares, others, grad_in_norm = [], [], [], None
+    shares, others, grad_in_norm = [], [], None
     near, near_last, ins, small, smalls, expert_grads = [], [], [], [None], [], []
     for i in range(jobs + 2):
         outs, parts, more = [], [], [None, None]
@@ -1108,7 +1123,6 @@
             ahead = here.rows_first(width) if i <= jobs else 0
             if i > 1:
                 line = ahead + near_last[0].shape[0] if i > 1 else 0
-                lasts.append([ins[1][ahead:line], ins[0][ahead:line], *near_last])
             columns = small[0].shape[1] // 2 if small[0] is not None else 0
             if i in (3, 4):
                 came = ins[i == 4][line:].reshape(small[0].shape)
@@ -1116,25 +1130,23 @@
             if i in (2, 3):
                 more[i == 3] = small[0][:, columns:].astype(bfloat).reshape(-1, width // 2)
                 small = [small[0][:, :columns]]
+            if i > 1:
+                pieces_small = []
+                if i == 4:
+                    pieces_small = [
+                        piece.reshape(-1, width).astype(jnp.float32 if p == 0 else bfloat)
+                        for p, piece in enumerate(jnp.split(small[0], here.nz, axis=1))
+                    ]
+                parts = list(line_fold(ins, ahead, near_last, here.nz, pieces_small))
             if i == 0:
                 outs = far
             elif i <= jobs:
                 *outs, keep_x, keep_y = fold(ins, near, far if i < jobs else [], more)
                 near_last = [keep_x, keep_y]
         else:
-            if 0 < i <= jobs:
-                lasts.append(ins)
             outs = far if i < jobs else []
-        at = i - 2 if here.square else i - 1
-        if 0 <= at < jobs:
-            parts = here.line_parts(lasts[at])
-            if here.square and i == 4:
-                parts = [
-                    jnp.concatenate([part, piece.reshape(-1, width).astype(part.dtype)], axis=0)
-                    for part, piece in zip(
-                        parts, jnp.split(small[0], here.nz, axis=1), strict=True
-                    )
-                ]
+        if not here.square and 0 < i <= jobs:
+            parts = here.line_parts(ins)
         sending_y = []
         if adds_y:
             collect_y.land(moving)

time: 892 us -> 882 us (0.989)
  other arithmetic: 80 us -> 67.1 us
  waiting for transfers between devices: 174 us -> 184 us
  local copies, waits for them, and re-layouts: 89.7 us -> 99.4 us
  Pallas kernels: 215 us -> 206 us
  starting transfers between devices: 188 us -> 179 us
    unnamed x446 -> x456, local copies, waits for them, and re-layouts: 49.2 us -> 62.4 us
    pallas_call x4 -> x8, Pallas kernels: 68.1 us -> 60.7 us  [the longest x4 58.7 us: expert_back(): pl.pallas_call(body, grid=(total // rows, hidden // tile), in_specs=[whol...]
  transfers between devices with their start and end apart: 115 -> 115, of which waited for: 40 -> 44; matrix products, arithmetic and copies ran while one was open for 21% -> 21% of each run, Pallas kernels for 23% -> 22%
where the time goes in v4:
time: 882 us; the launch traced here: 873 us
  Pallas kernels  206 us (23%)
  waiting for transfers between devices  184 us (21%)
  starting transfers between devices  179 us (20%)
  matrix products  134 us (15%)
  local copies, waits for them, and re-layouts  99.4 us (11%)
  other arithmetic  67.1 us (8%)
    ppermute x65, waiting for transfers between devices, shift_plane(): return lax.ppermute(value, 'expert', pairs)  112 us
    dot_general x34, matrix products, product(): return jnp.dot(left, right, preferred_element_type=jnp.float32)  82.4 us
    ppermute x40, starting transfers between devices, along_line(): return lax.ppermute(value, 'expert', pairs)  73.6 us
    ppermute x40, waiting for transfers between devices, along_line(): return lax.ppermute(value, 'expert', pairs)  69.2 us
    unnamed x456, local copies, waits for them, and re-layouts  62.4 us
    ppermute x65, starting transfers between devices, shift_plane(): return lax.ppermute(value, 'expert', pairs)  59.7 us
    pallas_call x4, Pallas kernels, expert_back(): pl.pallas_call(body, grid=(total // rows, hidden // tile), in_specs=[whol...  58.7 us
    dot_general x26, matrix products, contract_rows(): lax.dot_general(left, right, (((0,), (0,)), ((), ())), preferred_element_...  46 us
  transfers between devices with their start and end apart: 115, of which 44 were waited for; matrix products, arithmetic and copies ran while one was open for 21% of the time, Pallas kernels for 22%

profile of v4, /device:TPU:9, one launch (start us, length us, event | category | flops | bytes accessed | tf_op | source)
XLA Modules:
  0.0 872.5 jit_solution(1509975431907538972)
XLA Ops:
  19.7 13.2 %collective-permute-done.3 = bf16[4,64,2048]{2,1,0:T(8,128)(2,1)} collective-permute-done((bf16[4,64,2048]{2,1,0:T(8,128)(2,1)S(1)}, bf16[4,64,2048]{2,1,0:T(8,128)(2,1)}, u32[]{:S(2)}, u32[]{:S(2)}) %collective-permute-start.3) | collective-permute-done | bytes 1048608 | tf_op jit(solution)/shard_map/ppermute | solution.py:171
  60.2 6.6 collective-permute-start.14
  91.2 7.6 collective-permute-done.17
  98.9 14.6 %collective-permute-done.15 = bf16[6,64,2048]{2,1,0:T(8,128)(2,1)S(1)} collective-permute-done((bf16[6,64,2048]{2,1,0:T(8,128)(2,1)S(1)}, bf16[6,64,2048]{2,1,0:T(8,128)(2,1)S(1)}, u32[]{:S(2)}, u32[]{:S(2)}) %collective-permute-start.15) | collective-permute-done | bytes 1572896 | tf_op jit(solution)/shard_map/ppermute | solution.py:171
  124.3 7.7 collective-permute-start.22
  140.9 5.7 shard_map.230.refs_2_
  153.7 8.5 collective-permute-start.27
  177.5 8.7 %shard_map.231.refs_2_ = f32[256,6144]{1,0:T(8,128)} custom-call(bf16[256,512]{1,0:T(8,128)(2,1)S(1)} %get-tuple-element.1764.left_ref, bf16[4,4,64,2048]{3,2,1,0:T(8,128)(2,1)S(1)} %bitcast.218, bf16[4,4,64,2048]{3,2,1,0:T(8,128)(2,1)S(1)} %collective-permute-done.27.refs_1_.refs_3_, f32[256,6144]{1,0:T(8,128)} %shard_map.230.refs_2_), custom_call_target="tpu_custom_call" | custom-call | flops 1 | bytes 1 | tf_op jit(solution)/shard_map/pallas_call | solution.py:381
  210.5 9.5 %shard_map.232.refs_2_ = f32[256,6144]{1,0:T(8,128)} custom-call(bf16[256,512]{1,0:T(8,128)(2,1)S(1)} %get-tuple-element.1763.left_ref, bf16[4,4,64,2048]{3,2,1,0:T(8,128)(2,1)} %bitcast.36.refs_0_.refs_4_, bf16[4,4,64,2048]{3,2,1,0:T(8,128)(2,1)} %collective-permute-done.32.refs_1_.refs_5_, f32[256,6144]{1,0:T(8,128)} %shard_map.231.refs_2_), custom_call_target="tpu_custom_call" | custom-call | flops 1 | bytes 1 | tf_op jit(solution)/shard_map/pallas_call | solution.py:381
  220.1 14.5 %collective-permute-done.30 = bf16[256,2048]{1,0:T(8,128)(2,1)S(1)} collective-permute-done((bf16[256,2048]{1,0:T(8,128)(2,1)}, bf16[256,2048]{1,0:T(8,128)(2,1)S(1)}, u32[]{:S(2)}, u32[]{:S(2)}) %collective-permute-start.30) | collective-permute-done | bytes 1048608 | tf_op jit(solution)/shard_map/ppermute | solution.py:171
  248.9 9.2 %shard_map.233.raw_ref = f32[256,6144]{1,0:T(8,128)} custom-call(bf16[256,512]{1,0:T(8,128)(2,1)S(1)} %get-tuple-element.1766.left_ref, bf16[4,4,64,2048]{3,2,1,0:T(8,128)(2,1)} %bitcast.39.refs_0_.refs_6_, bf16[4,4,64,2048]{3,2,1,0:T(8,128)(2,1)} %collective-permute-done.33.refs_1_.refs_7_, f32[256,6144]{1,0:T(8,128)} %shard_map.232.refs_2_), custom_call_target="tpu_custom_call" | custom-call | flops 1 | bytes 1 | tf_op jit(solution)/shard_map/pallas_call | solution.py:381
  258.1 12.8 %shard_map.234 = (bf16[256,2048]{1,0:T(8,128)(2,1)S(1)}, bf16[256,2048]{1,0:T(8,128)(2,1)S(1)}, bf16[256,2048]{1,0:T(8,128)(2,1)S(1)}, bf16[256,2048]{1,0:T(8,12...) custom-call(f32[256,6144]{1,0:T(8,128)} %shard_map.233.raw_ref, ...), custom_call_target="tpu_custom_call" | custom-call | flops 1 | bytes 1 | tf_op jit(solution)/shard_map/pallas_call | solution.py:477
  304.4 12.2 %collective-permute-done.42 = bf16[128,2048]{1,0:T(8,128)(2,1)S(1)} collective-permute-done((bf16[128,2048]{1,0:T(8,128)(2,1)S(1)}, bf16[128,2048]{1,0:T(8,128)(2,1)S(1)}, u32[]{:S(2)}, u32[]{:S(2)}) %collective-permute-start.42) | collective-permute-done | bytes 524320 | tf_op jit(solution)/shard_map/ppermute | solution.py:171
  355.3 5.6 collective-permute-start.52
  365.0 5.8 fusion.13
  386.6 5.9 fusion.16
  414.2 14.7 %shard_map.236 = (bf16[128,2176]{1,0:T(8,128)(2,1)S(1)}, bf16[128,2176]{1,0:T(8,128)(2,1)S(1)}, bf16[128,2176]{1,0:T(8,128)(2,1)S(1)}, bf16[128,2176]{1,0:T(8,12...) custom-call(bf16[512,2048]{1,0:T(8,128)(2,1)} %get-tuple-element.1381.grad_y_ref.refs_7_, ...), custom_call_target="tpu_custom_call" | custom-call | flops 1 | bytes 1 | tf_op jit(solution)/shard_map/pallas_call | solution.py:616
  432.6 14.5 %shard_map.237 = (bf16[128,2176]{1,0:T(8,128)(2,1)S(1)}, bf16[128,2176]{1,0:T(8,128)(2,1)S(1)}, bf16[128,2176]{1,0:T(8,128)(2,1)S(1)}, bf16[128,2176]{1,0:T(8,12...) custom-call(bf16[512,2048]{1,0:T(8,128)(2,1)} %get-tuple-element.1380.grad_y_ref.refs_6_, ...), custom_call_target="tpu_custom_call" | custom-call | flops 1 | bytes 1 | tf_op jit(solution)/shard_map/pallas_call | solution.py:616
  447.7 14.4 %shard_map.238 = (bf16[128,2176]{1,0:T(8,128)(2,1)S(1)}, bf16[128,2176]{1,0:T(8,128)(2,1)S(1)}, bf16[128,2176]{1,0:T(8,128)(2,1)S(1)}, bf16[128,2176]{1,0:T(8,12...) custom-call(bf16[512,2048]{1,0:T(8,128)(2,1)} %get-tuple-element.1379.grad_y_ref.refs_5_, ...), custom_call_target="tpu_custom_call" | custom-call | flops 1 | bytes 1 | tf_op jit(solution)/shard_map/pallas_call | solution.py:616
  471.4 15.1 %shard_map.239 = (bf16[128,2176]{1,0:T(8,128)(2,1)S(1)}, bf16[128,2176]{1,0:T(8,128)(2,1)}, bf16[128,2176]{1,0:T(8,128)(2,1)}, bf16[128,2176]{1,0:T(8,128)(2,1)}...) custom-call(bf16[512,2048]{1,0:T(8,128)(2,1)} %get-tuple-element.1378.grad_y_ref.refs_4_, ...), custom_call_target="tpu_custom_call" | custom-call | flops 1 | bytes 1 | tf_op jit(solution)/shard_map/pallas_call | solution.py:616
  506.1 15.2 %shard_map.240 = f32[1024,2048]{1,0:T(8,128)} custom-call(bf16[512,1024]{1,0:T(8,128)(2,1)S(1)} %get-tuple-element.1374.refs_0_, bf16[512,1024]{1,0:T(8,128)(2,1)} %copy-done.146, bf16[512,1024]{1,0:T(8,128)(2,1)} %copy-done.147, bf16[512,1024]{1,0:T(8,128)(2,1)} %copy-done.148, bf16[512,2048]{1,0:T(8,128)(2,1)} %get-tuple-element.1378.grad_y_ref.refs_4_, ...), custom_call_target="tpu_custom_call" | custom-call | flops 1 | bytes 1 | tf_op jit(solution)/shard_map/pallas_call | solution.py:650
  572.9 11.0 %collective-permute-start.82 = (bf16[256,2048]{1,0:T(8,128)(2,1)S(1)}, bf16[256,2048]{1,0:T(8,128)(2,1)S(1)}, u32[]{:S(2)}, u32[]{:S(2)}) collective-permute-start(bf16[256,2048]{1,0:T(8,128)(2,1)S(1)} %get-tuple-element.1454), channel_id=1, source_target_pairs={{0,16},{16,0},{1,17},{17,1},{2,18},{18,2},{3,19},{19,3},{4,20},{20... | collective-permute-start | bytes 3145736 | tf_op jit(solution)/shard_map/ppermute | solution.py:184
  588.4 19.0 %shard_map.242 = (bf16[3,256,2048]{2,1,0:T(8,128)(2,1)}, f32[8,2048]{1,0:T(8,128)S(1)}) custom-call(bf16[256,2048]{1,0:T(8,128)(2,1)S(1)} %fusion.27.grad_ref, bf16[256,2048]{1,0:T(8,128)(2,1)S(1)} %copy-done.30, bf16[256,2048]{1,0:T(8,128)(2,1)S(1)} %copy-done.32, bf16[256,2048]{1,0:T(8,128)(2,1)S(1)} %copy-done.34, f32[16,256,256]{2,1,0:T(8,128)S(1)} %copy-done.24, ...), custom_call_target="tpu_custom_call" | custom-call | flops 1 | bytes 1 | tf_op jit(solution)/shard_map/pallas_call | solution.py:554
  638.2 11.8 %shard_map.243.grad_ref = f32[256,2048]{1,0:T(8,128)S(1)} custom-call(bf16[3,256,2048]{2,1,0:T(8,128)(2,1)} %get-tuple-element.1568.left_ref, bf16[4,4,64,2048]{3,2,1,0:T(8,128)(2,1)S(1)} %bitcast.216, bf16[4,4,64,2048]{3,2,1,0:T(8,128)(2,1)S(1)} %copy-done.8, bf16[4,4,64,2048]{3,2,1,0:T(8,128)(2,1)} %bitcast.221, bf16[4,4,64,2048]{3,2,1,0:T(8,128)(2,1)} %copy-done.9, ...), custom_call_target="tpu_custom_call" | custom-call | flops 1 | bytes 1 | tf_op jit(solution)/shard_map/pallas_call | solution.py:415
  676.4 7.7 shard_map.245
  694.3 14.3 %collective-permute-done.92.refs_0_.came_x = bf16[768,1024]{1,0:T(8,128)(2,1)} collective-permute-done((bf16[768,1024]{1,0:T(8,128)(2,1)}, bf16[768,1024]{1,0:T(8,128)(2,1)}, u32[]{:S(2)}, u32[]{:S(2)}) %collective-permute-start.92) | collective-permute-done | bytes 1572896 | tf_op jit(solution)/shard_map/ppermute | solution.py:171
  723.2 13.9 %shard_map.248 = f32[2048,1024]{1,0:T(8,128)} custom-call(bf16[512,2048]{1,0:T(8,128)(2,1)} %copy-done.75, bf16[512,2048]{1,0:T(8,128)(2,1)} %copy-done.76, bf16[512,2048]{1,0:T(8,128)(2,1)} %copy-done.77, bf16[512,2048]{1,0:T(8,128)(2,1)} %copy-done.78, bf16[512,1024]{1,0:T(8,128)(2,1)S(1)} %copy-done.36, bf16[512,1024]{1,0:T(8,128)(2,1)} %get-tuple-element.1559.refs_5_, ...), custom_call_target="tpu_custom_call" | custom-call | flops 1 | bytes 1 | tf_op jit(solution)/shard_map/pallas_call | solution.py:650
  746.9 6.2 collective-permute-done.97.refs_1_.came_y
  775.7 13.5 %shard_map.251 = f32[2048,1024]{1,0:T(8,128)} custom-call(bf16[512,2048]{1,0:T(8,128)(2,1)} %copy-done.75, bf16[512,2048]{1,0:T(8,128)(2,1)} %copy-done.76, bf16[512,2048]{1,0:T(8,128)(2,1)} %copy-done.77, bf16[512,2048]{1,0:T(8,128)(2,1)} %copy-done.78, bf16[512,1024]{1,0:T(8,128)(2,1)S(1)} %copy-done.35, bf16[512,1024]{1,0:T(8,128)(2,1)} %get-tuple-element.1597.refs_5_, ...), custom_call_target="tpu_custom_call" | custom-call | flops 1 | bytes 1 | tf_op jit(solution)/shard_map/pallas_call | solution.py:650
  793.4 5.7 collective-permute-done.101.refs_0_.came_x
  822.2 14.9 %collective-permute-done.109 = bf16[66,2048]{1,0:T(8,128)(2,1)S(1)} collective-permute-done((bf16[66,2048]{1,0:T(8,128)(2,1)S(1)}, bf16[66,2048]{1,0:T(8,128)(2,1)S(1)}, u32[]{:S(2)}, u32[]{:S(2)}) %collective-permute-start.109) | collective-permute-done | bytes 270368 | tf_op jit(solution)/shard_map/ppermute | solution.py:180
  853.1 14.9 %collective-permute-done.112 = bf16[64,2048]{1,0:T(8,128)(2,1)S(1)} collective-permute-done((bf16[64,2048]{1,0:T(8,128)(2,1)S(1)}, bf16[64,2048]{1,0:T(8,128)(2,1)S(1)}, u32[]{:S(2)}, u32[]{:S(2)}) %collective-permute-start.112) | collective-permute-done | bytes 262176 | tf_op jit(solution)/shard_map/ppermute | solution.py:180
  (932 shorter events, 513.3 us)
Async XLA Ops:
  46.8 31.6 %collective-permute-start.10 = (bf16[6,64,2048]{2,1,0:T(8,128)(2,1)}, bf16[6,64,2048]{2,1,0:T(8,128)(2,1)}, u32[]{:S(2)}, u32[]{:S(2)}) collective-permute-start(bf16[6,64,2048]{2,1,0:T(8,128)(2,1)} %get-tuple-element.865), channel_id=1, source_target_pairs={{0,1},{1,0},{2,3},{3,2},{4,5},{5,4},{6,7},{7,6},{8,9},{9,8},{10,11... | collective-permute-start | bytes 4718600 | tf_op jit(solution)/shard_map/ppermute | solution.py:171
  48.0 30.4 %collective-permute-start.11 = (bf16[6,64,2048]{2,1,0:T(8,128)(2,1)}, bf16[6,64,2048]{2,1,0:T(8,128)(2,1)}, u32[]{:S(2)}, u32[]{:S(2)}) collective-permute-start(bf16[6,64,2048]{2,1,0:T(8,128)(2,1)} %get-tuple-element.866), channel_id=1, source_target_pairs={{0,2},{1,3},{2,0},{3,1},{4,6},{5,7},{6,4},{7,5},{8,10},{9,11},{10,... | collective-permute-start | bytes 4718600 | tf_op jit(solution)/shard_map/ppermute | solution.py:171
  84.5 28.9 %collective-permute-start.15 = (bf16[6,64,2048]{2,1,0:T(8,128)(2,1)S(1)}, bf16[6,64,2048]{2,1,0:T(8,128)(2,1)S(1)}, u32[]{:S(2)}, u32[]{:S(2)}) collective-permute-start(bf16[6,64,2048]{2,1,0:T(8,128)(2,1)S(1)} %get-tuple-element.885), channel_id=1, source_target_pairs={{0,1},{1,0},{2,3},{3,2},{4,5},{5,4},{6,7},{7,6},{8,9},{9,8},{10,11... | collective-permute-start | bytes 4718600 | tf_op jit(solution)/shard_map/ppermute | solution.py:171
  85.8 29.2 %collective-permute-start.16 = (bf16[6,64,2048]{2,1,0:T(8,128)(2,1)S(1)}, bf16[6,64,2048]{2,1,0:T(8,128)(2,1)S(1)}, u32[]{:S(2)}, u32[]{:S(2)}) collective-permute-start(bf16[6,64,2048]{2,1,0:T(8,128)(2,1)S(1)} %get-tuple-element.886), channel_id=1, source_target_pairs={{0,2},{1,3},{2,0},{3,1},{4,6},{5,7},{6,4},{7,5},{8,10},{9,11},{10,... | collective-permute-start | bytes 4718600 | tf_op jit(solution)/shard_map/ppermute | solution.py:171
  199.1 35.4 %collective-permute-start.30 = (bf16[256,2048]{1,0:T(8,128)(2,1)}, bf16[256,2048]{1,0:T(8,128)(2,1)S(1)}, u32[]{:S(2)}, u32[]{:S(2)}) collective-permute-start(bf16[256,2048]{1,0:T(8,128)(2,1)} %pad_maximum_fusion.16), channel_id=1, source_target_pairs={{0,3},{1,2},{2,1},{3,0},{4,7},{5,6},{6,5},{7,4},{8,11},{9,10},{10,... | collective-permute-start | bytes 3145736 | tf_op jit(solution)/shard_map/ppermute | solution.py:171
  200.8 33.7 %collective-permute-start.31 = (bf16[256,2048]{1,0:T(8,128)(2,1)}, bf16[256,2048]{1,0:T(8,128)(2,1)S(1)}, u32[]{:S(2)}, u32[]{:S(2)}) collective-permute-start(bf16[256,2048]{1,0:T(8,128)(2,1)} %copy-done.149), channel_id=1, source_target_pairs={{4,0},{5,1},{6,2},{7,3},{8,12},{9,13},{10,14},{11,15},{20,16},{21,... | collective-permute-start | bytes 3145736 | tf_op jit(solution)/shard_map/ppermute | solution.py:180
  242.7 44.3 %collective-permute-start.37 = (bf16[256,1024]{1,0:T(8,128)(2,1)}, bf16[256,1024]{1,0:T(8,128)(2,1)S(1)}, u32[]{:S(2)}, u32[]{:S(2)}) collective-permute-start(bf16[256,1024]{1,0:T(8,128)(2,1)} %get-tuple-element.1001), channel_id=1, source_target_pairs={{0,16},{16,0},{1,17},{17,1},{2,18},{18,2},{3,19},{19,3},{4,20},{20... | collective-permute-start | bytes 1572872 | tf_op jit(solution)/shard_map/ppermute | solution.py:184
  242.7 44.2 %collective-permute-start.34 = (bf16[256,2048]{1,0:T(8,128)(2,1)}, bf16[256,2048]{1,0:T(8,128)(2,1)S(1)}, u32[]{:S(2)}, u32[]{:S(2)}) collective-permute-start(bf16[256,2048]{1,0:T(8,128)(2,1)} %pad_maximum_fusion.18), channel_id=1, source_target_pairs={{0,1},{1,0},{2,3},{3,2},{4,5},{5,4},{6,7},{7,6},{8,9},{9,8},{10,11... | collective-permute-start | bytes 3145736 | tf_op jit(solution)/shard_map/ppermute | solution.py:171
  243.3 43.6 %collective-permute-start.35 = (bf16[256,2048]{1,0:T(8,128)(2,1)S(1)}, bf16[256,2048]{1,0:T(8,128)(2,1)}, u32[]{:S(2)}, u32[]{:S(2)}) collective-permute-start(bf16[256,2048]{1,0:T(8,128)(2,1)S(1)} %copy-done.158), channel_id=1, source_target_pairs={{0,2},{1,3},{2,0},{3,1},{4,6},{5,7},{6,4},{7,5},{8,10},{9,11},{10,... | collective-permute-start | bytes 3145736 | tf_op jit(solution)/shard_map/ppermute | solution.py:171
  243.8 45.8 %collective-permute-start.36 = (bf16[256,2048]{1,0:T(8,128)(2,1)S(1)}, bf16[256,2048]{1,0:T(8,128)(2,1)S(1)}, u32[]{:S(2)}, u32[]{:S(2)}) collective-permute-start(bf16[256,2048]{1,0:T(8,128)(2,1)S(1)} %copy-done.157), channel_id=1, source_target_pairs={{0,3},{1,2},{2,1},{3,0},{4,7},{5,6},{6,5},{7,4},{8,11},{9,10},{10,... | collective-permute-start | bytes 3145736 | tf_op jit(solution)/shard_map/ppermute | solution.py:171
  430.5 31.6 %collective-permute-start.63 = (bf16[128,2176]{1,0:T(8,128)(2,1)}, bf16[128,2176]{1,0:T(8,128)(2,1)}, u32[]{:S(2)}, u32[]{:S(2)}) collective-permute-start(bf16[128,2176]{1,0:T(8,128)(2,1)} %get-tuple-element.1283), channel_id=1, source_target_pairs={{0,3},{1,2},{2,1},{3,0},{4,7},{5,6},{6,5},{7,4},{8,11},{9,10},{10,... | collective-permute-start | bytes 1671176 | tf_op jit(solution)/shard_map/ppermute | solution.py:171
  469.5 35.0 %collective-permute-start.73 = (bf16[128,2176]{1,0:T(8,128)(2,1)}, bf16[128,2176]{1,0:T(8,128)(2,1)}, u32[]{:S(2)}, u32[]{:S(2)}) collective-permute-start(bf16[128,2176]{1,0:T(8,128)(2,1)} %get-tuple-element.1399), channel_id=1, source_target_pairs={{0,3},{1,2},{2,1},{3,0},{4,7},{5,6},{6,5},{7,4},{8,11},{9,10},{10,... | collective-permute-start | bytes 1671176 | tf_op jit(solution)/shard_map/ppermute | solution.py:171
  572.9 36.6 %collective-permute-start.82 = (bf16[256,2048]{1,0:T(8,128)(2,1)S(1)}, bf16[256,2048]{1,0:T(8,128)(2,1)S(1)}, u32[]{:S(2)}, u32[]{:S(2)}) collective-permute-start(bf16[256,2048]{1,0:T(8,128)(2,1)S(1)} %get-tuple-element.1454), channel_id=1, source_target_pairs={{0,16},{16,0},{1,17},{17,1},{2,18},{18,2},{3,19},{19,3},{4,20},{20... | collective-permute-start | bytes 3145736 | tf_op jit(solution)/shard_map/ppermute | solution.py:184
  583.9 31.2 %collective-permute-start.83 = (bf16[128,2048]{1,0:T(8,128)(2,1)}, bf16[128,2048]{1,0:T(8,128)(2,1)}, u32[]{:S(2)}, u32[]{:S(2)}) collective-permute-start(bf16[128,2048]{1,0:T(8,128)(2,1)} %get-tuple-element.1456), channel_id=1, source_target_pairs={{0,1},{1,0},{2,3},{3,2},{4,5},{5,4},{6,7},{7,6},{8,9},{9,8},{10,11... | collective-permute-start | bytes 1572872 | tf_op jit(solution)/shard_map/ppermute | solution.py:171
  585.3 29.8 %collective-permute-start.84 = (bf16[128,2048]{1,0:T(8,128)(2,1)}, bf16[128,2048]{1,0:T(8,128)(2,1)}, u32[]{:S(2)}, u32[]{:S(2)}) collective-permute-start(bf16[128,2048]{1,0:T(8,128)(2,1)} %get-tuple-element.1457), channel_id=1, source_target_pairs={{0,2},{1,3},{2,0},{3,1},{4,6},{5,7},{6,4},{7,5},{8,10},{9,11},{10,... | collective-permute-start | bytes 1572872 | tf_op jit(solution)/shard_map/ppermute | solution.py:171
  585.8 29.2 %collective-permute-start.85 = (bf16[128,2048]{1,0:T(8,128)(2,1)}, bf16[128,2048]{1,0:T(8,128)(2,1)}, u32[]{:S(2)}, u32[]{:S(2)}) collective-permute-start(bf16[128,2048]{1,0:T(8,128)(2,1)} %get-tuple-element.1458), channel_id=1, source_target_pairs={{0,3},{1,2},{2,1},{3,0},{4,7},{5,6},{6,5},{7,4},{8,11},{9,10},{10,... | collective-permute-start | bytes 1572872 | tf_op jit(solution)/shard_map/ppermute | solution.py:171
  621.2 33.1 %collective-permute-start.87 = (bf16[512,1024]{1,0:T(8,128)(2,1)}, bf16[512,1024]{1,0:T(8,128)(2,1)S(1)}, u32[]{:S(2)}, u32[]{:S(2)}) collective-permute-start(bf16[512,1024]{1,0:T(8,128)(2,1)} %convolution_convert_fusion.20), channel_id=1, source_target_pairs={{0,1},{1,0},{2,3},{3,2},{4,5},{5,4},{6,7},{7,6},{8,9},{9,8},{10,11... | collective-permute-start | bytes 3145736 | tf_op jit(solution)/shard_map/ppermute | solution.py:171
  622.7 31.7 %collective-permute-start.88 = (bf16[512,1024]{1,0:T(8,128)(2,1)}, bf16[512,1024]{1,0:T(8,128)(2,1)S(1)}, u32[]{:S(2)}, u32[]{:S(2)}) collective-permute-start(bf16[512,1024]{1,0:T(8,128)(2,1)} %convolution_convert_fusion.19), channel_id=1, source_target_pairs={{0,2},{1,3},{2,0},{3,1},{4,6},{5,7},{6,4},{7,5},{8,10},{9,11},{10,... | collective-permute-start | bytes 3145736 | tf_op jit(solution)/shard_map/ppermute | solution.py:171
  623.3 31.1 %collective-permute-start.89 = (bf16[256,2048]{1,0:T(8,128)(2,1)}, bf16[256,2048]{1,0:T(8,128)(2,1)}, u32[]{:S(2)}, u32[]{:S(2)}) collective-permute-start(bf16[256,2048]{1,0:T(8,128)(2,1)} %add_convert_fusion.6), channel_id=1, source_target_pairs={{4,8},{5,9},{6,10},{7,11},{8,4},{9,5},{10,6},{11,7},{20,24},{21,25... | collective-permute-start | bytes 3145736 | tf_op jit(solution)/shard_map/ppermute | solution.py:180
  667.5 41.8 %collective-permute-start.94 = (bf16[256,2048]{1,0:T(8,128)(2,1)}, bf16[256,2048]{1,0:T(8,128)(2,1)}, u32[]{:S(2)}, u32[]{:S(2)}) collective-permute-start(bf16[256,2048]{1,0:T(8,128)(2,1)} %add_convert_fusion.5), channel_id=1, source_target_pairs={{0,4},{1,5},{2,6},{3,7},{4,0},{5,1},{6,2},{7,3},{8,12},{9,13},{10,... | collective-permute-start | bytes 3145736 | tf_op jit(solution)/shard_map/ppermute | solution.py:180
  670.8 38.6 %collective-permute-start.95 = (bf16[256,2048]{1,0:T(8,128)(2,1)}, bf16[256,2048]{1,0:T(8,128)(2,1)}, u32[]{:S(2)}, u32[]{:S(2)}) collective-permute-start(bf16[256,2048]{1,0:T(8,128)(2,1)} %add_convert_fusion.4), channel_id=1, source_target_pairs={{4,8},{5,9},{6,10},{7,11},{8,4},{9,5},{10,6},{11,7},{20,24},{21,25... | collective-permute-start | bytes 3145736 | tf_op jit(solution)/shard_map/ppermute | solution.py:180
  673.6 35.0 %collective-permute-start.92 = (bf16[768,1024]{1,0:T(8,128)(2,1)}, bf16[768,1024]{1,0:T(8,128)(2,1)}, u32[]{:S(2)}, u32[]{:S(2)}) collective-permute-start(bf16[768,1024]{1,0:T(8,128)(2,1)} %get-tuple-element.1517), channel_id=1, source_target_pairs={{0,1},{1,0},{2,3},{3,2},{4,5},{5,4},{6,7},{7,6},{8,9},{9,8},{10,11... | collective-permute-start | bytes 4718600 | tf_op jit(solution)/shard_map/ppermute | solution.py:171
  674.6 34.7 %collective-permute-start.93 = (bf16[768,1024]{1,0:T(8,128)(2,1)}, bf16[768,1024]{1,0:T(8,128)(2,1)}, u32[]{:S(2)}, u32[]{:S(2)}) collective-permute-start(bf16[768,1024]{1,0:T(8,128)(2,1)} %get-tuple-element.1518), channel_id=1, source_target_pairs={{0,2},{1,3},{2,0},{3,1},{4,6},{5,7},{6,4},{7,5},{8,10},{9,11},{10,... | collective-permute-start | bytes 4718600 | tf_op jit(solution)/shard_map/ppermute | solution.py:171
  718.8 35.9 %collective-permute-start.98 = (bf16[64,2048]{1,0:T(8,128)(2,1)S(1)}, bf16[64,2048]{1,0:T(8,128)(2,1)S(1)}, u32[]{:S(2)}, u32[]{:S(2)}) collective-permute-start(bf16[64,2048]{1,0:T(8,128)(2,1)S(1)} %get-tuple-element.1565), channel_id=1, source_target_pairs={{0,4},{1,5},{2,6},{3,7},{4,8},{5,9},{6,10},{7,11},{8,12},{9,13},{1... | collective-permute-start | bytes 786440 | tf_op jit(solution)/shard_map/ppermute | solution.py:180
  719.0 35.7 %collective-permute-start.99 = (bf16[64,2048]{1,0:T(8,128)(2,1)S(1)}, bf16[64,2048]{1,0:T(8,128)(2,1)}, u32[]{:S(2)}, u32[]{:S(2)}) collective-permute-start(bf16[64,2048]{1,0:T(8,128)(2,1)S(1)} %get-tuple-element.1566), channel_id=1, source_target_pairs={{0,8},{1,9},{2,10},{3,11},{4,12},{5,13},{6,14},{7,15},{8,0},{9,1},... | collective-permute-start | bytes 786440 | tf_op jit(solution)/shard_map/ppermute | solution.py:180
  719.9 35.5 %collective-permute-start.100 = (bf16[64,2048]{1,0:T(8,128)(2,1)S(1)}, bf16[64,2048]{1,0:T(8,128)(2,1)}, u32[]{:S(2)}, u32[]{:S(2)}) collective-permute-start(bf16[64,2048]{1,0:T(8,128)(2,1)S(1)} %get-tuple-element.1567), channel_id=1, source_target_pairs={{0,12},{1,13},{2,14},{3,15},{4,0},{5,1},{6,2},{7,3},{8,4},{9,5},{1... | collective-permute-start | bytes 786440 | tf_op jit(solution)/shard_map/ppermute | solution.py:180
  720.5 32.6 %collective-permute-start.97 = (bf16[768,1024]{1,0:T(8,128)(2,1)S(1)}, bf16[768,1024]{1,0:T(8,128)(2,1)S(1)}, u32[]{:S(2)}, u32[]{:S(2)}) collective-permute-start(bf16[768,1024]{1,0:T(8,128)(2,1)S(1)} %get-tuple-element.1553), channel_id=1, source_target_pairs={{0,2},{1,3},{2,0},{3,1},{4,6},{5,7},{6,4},{7,5},{8,10},{9,11},{10,... | collective-permute-start | bytes 4718600 | tf_op jit(solution)/shard_map/ppermute | solution.py:171
  720.7 34.0 %collective-permute-start.96 = (bf16[800,1024]{1,0:T(8,128)(2,1)S(1)}, bf16[800,1024]{1,0:T(8,128)(2,1)S(1)}, u32[]{:S(2)}, u32[]{:S(2)}) collective-permute-start(bf16[800,1024]{1,0:T(8,128)(2,1)S(1)} %get-tuple-element.1552), channel_id=1, source_target_pairs={{0,1},{1,0},{2,3},{3,2},{4,5},{5,4},{6,7},{7,6},{8,9},{9,8},{10,11... | collective-permute-start | bytes 4915208 | tf_op jit(solution)/shard_map/ppermute | solution.py:171
  767.0 33.3 %collective-permute-start.102 = (bf16[784,1024]{1,0:T(8,128)(2,1)S(1)}, bf16[784,1024]{1,0:T(8,128)(2,1)S(1)}, u32[]{:S(2)}, u32[]{:S(2)}) collective-permute-start(bf16[784,1024]{1,0:T(8,128)(2,1)S(1)} %get-tuple-element.1590), channel_id=1, source_target_pairs={{0,2},{1,3},{2,0},{3,1},{4,6},{5,7},{6,4},{7,5},{8,10},{9,11},{10,... | collective-permute-start | bytes 4816904 | tf_op jit(solution)/shard_map/ppermute | solution.py:171
  768.0 31.1 %collective-permute-start.101 = (bf16[768,1024]{1,0:T(8,128)(2,1)S(1)}, bf16[768,1024]{1,0:T(8,128)(2,1)S(1)}, u32[]{:S(2)}, u32[]{:S(2)}) collective-permute-start(bf16[768,1024]{1,0:T(8,128)(2,1)S(1)} %get-tuple-element.1589), channel_id=1, source_target_pairs={{0,1},{1,0},{2,3},{3,2},{4,5},{5,4},{6,7},{7,6},{8,9},{9,8},{10,11... | collective-permute-start | bytes 4718600 | tf_op jit(solution)/shard_map/ppermute | solution.py:171
  810.9 29.7 %collective-permute-start.106 = (bf16[256,1024]{1,0:T(8,128)(2,1)S(1)}, bf16[256,1024]{1,0:T(8,128)(2,1)S(1)}, u32[]{:S(2)}, u32[]{:S(2)}) collective-permute-start(bf16[256,1024]{1,0:T(8,128)(2,1)S(1)} %get-tuple-element.1626), channel_id=1, source_target_pairs={{0,1},{1,0},{2,3},{3,2},{4,5},{5,4},{6,7},{7,6},{8,9},{9,8},{10,11... | collective-permute-start | bytes 1572872 | tf_op jit(solution)/shard_map/ppermute | solution.py:171
  811.4 29.3 %collective-permute-start.107 = (bf16[256,1024]{1,0:T(8,128)(2,1)S(1)}, bf16[256,1024]{1,0:T(8,128)(2,1)S(1)}, u32[]{:S(2)}, u32[]{:S(2)}) collective-permute-start(bf16[256,1024]{1,0:T(8,128)(2,1)S(1)} %get-tuple-element.1627), channel_id=1, source_target_pairs={{0,2},{1,3},{2,0},{3,1},{4,6},{5,7},{6,4},{7,5},{8,10},{9,11},{10,... | collective-permute-start | bytes 1572872 | tf_op jit(solution)/shard_map/ppermute | solution.py:171
  (297 other events, 3814.4 us)

commit v5 on v4

--- a/solution.py
+++ b/solution.py
@@ -1057,7 +1057,9 @@
     parts[0] = contract_rows(spreads[0], joined(back))
     part_y = contract_rows(spreads[0], joined(back_y[0]))
     rows_next = [parted(forward[k][3]) for k in late[1:]]
-    moving, rows, parts, rows_next, part_y = tie(moving, rows, parts, rows_next, part_y)
+    moving, rows[:-1], parts, rows_next, part_y = tie(
+        moving, rows[:-1], parts, rows_next, part_y
+    )
     collect.land(moving)
     collect.add(0, parts[0])
     returned = collect.total

time: 882 us -> 882 us (level)
    unnamed x456 -> x464, local copies, waits for them, and re-layouts: 62.4 us -> 62.1 us
  transfers between devices with their start and end apart: 115 -> 115, of which waited for: 44 -> 41; matrix products, arithmetic and copies ran while one was open for 21% -> 22% of each run, Pallas kernels for 22% -> 22%
where the time goes in v5:
time: 882 us; the launch traced here: 872 us
  Pallas kernels  205 us (23%)
  waiting for transfers between devices  183 us (21%)
  starting transfers between devices  179 us (20%)
  matrix products  134 us (15%)
  local copies, waits for them, and re-layouts  100 us (11%)
  other arithmetic  66.9 us (8%)
    ppermute x65, waiting for transfers between devices, shift_plane(): return lax.ppermute(value, 'expert', pairs)  108 us
    dot_general x34, matrix products, product(): return jnp.dot(left, right, preferred_element_type=jnp.float32)  82.4 us
    ppermute x40, starting transfers between devices, along_line(): return lax.ppermute(value, 'expert', pairs)  73.5 us
    ppermute x40, waiting for transfers between devices, along_line(): return lax.ppermute(value, 'expert', pairs)  71.6 us
    unnamed x464, local copies, waits for them, and re-layouts  62.1 us
    ppermute x65, starting transfers between devices, shift_plane(): return lax.ppermute(value, 'expert', pairs)  60.3 us
    pallas_call x4, Pallas kernels, expert_back(): pl.pallas_call(body, grid=(total // rows, hidden // tile), in_specs=[whol...  58.6 us
    dot_general x26, matrix products, contract_rows(): lax.dot_general(left, right, (((0,), (0,)), ((), ())), preferred_element_...  45.9 us
  transfers between devices with their start and end apart: 115, of which 41 were waited for; matrix products, arithmetic and copies ran while one was open for 22% of the time, Pallas kernels for 22%

profile of v5, /device:TPU:9, one launch (start us, length us, event | category | flops | bytes accessed | tf_op | source)
XLA Modules:
  0.0 871.7 jit_solution(18192635569543061345)
XLA Ops:
  19.7 13.2 %collective-permute-done.3 = bf16[4,64,2048]{2,1,0:T(8,128)(2,1)} collective-permute-done((bf16[4,64,2048]{2,1,0:T(8,128)(2,1)S(1)}, bf16[4,64,2048]{2,1,0:T(8,128)(2,1)}, u32[]{:S(2)}, u32[]{:S(2)}) %collective-permute-start.3) | collective-permute-done | bytes 1048608 | tf_op jit(solution)/shard_map/ppermute | solution.py:171
  60.3 6.6 collective-permute-start.14
  91.3 7.7 collective-permute-done.17
  98.9 14.6 %collective-permute-done.15 = bf16[6,64,2048]{2,1,0:T(8,128)(2,1)S(1)} collective-permute-done((bf16[6,64,2048]{2,1,0:T(8,128)(2,1)S(1)}, bf16[6,64,2048]{2,1,0:T(8,128)(2,1)S(1)}, u32[]{:S(2)}, u32[]{:S(2)}) %collective-permute-start.15) | collective-permute-done | bytes 1572896 | tf_op jit(solution)/shard_map/ppermute | solution.py:171
  124.3 7.7 collective-permute-start.22
  140.8 5.7 shard_map.230.refs_2_
  153.6 8.6 collective-permute-start.27
  177.5 8.7 %shard_map.231.refs_2_ = f32[256,6144]{1,0:T(8,128)} custom-call(bf16[256,512]{1,0:T(8,128)(2,1)S(1)} %get-tuple-element.1762.left_ref, bf16[4,4,64,2048]{3,2,1,0:T(8,128)(2,1)S(1)} %bitcast.218, bf16[4,4,64,2048]{3,2,1,0:T(8,128)(2,1)S(1)} %collective-permute-done.27.refs_1_.refs_3_, f32[256,6144]{1,0:T(8,128)} %shard_map.230.refs_2_), custom_call_target="tpu_custom_call" | custom-call | flops 1 | bytes 1 | tf_op jit(solution)/shard_map/pallas_call | solution.py:381
  210.4 9.5 %shard_map.232.refs_2_ = f32[256,6144]{1,0:T(8,128)} custom-call(bf16[256,512]{1,0:T(8,128)(2,1)S(1)} %get-tuple-element.1761.left_ref, bf16[4,4,64,2048]{3,2,1,0:T(8,128)(2,1)} %bitcast.36.refs_0_.refs_4_, bf16[4,4,64,2048]{3,2,1,0:T(8,128)(2,1)} %collective-permute-done.32.refs_1_.refs_5_, f32[256,6144]{1,0:T(8,128)} %shard_map.231.refs_2_), custom_call_target="tpu_custom_call" | custom-call | flops 1 | bytes 1 | tf_op jit(solution)/shard_map/pallas_call | solution.py:381
  220.0 14.5 %collective-permute-done.30 = bf16[256,2048]{1,0:T(8,128)(2,1)S(1)} collective-permute-done((bf16[256,2048]{1,0:T(8,128)(2,1)}, bf16[256,2048]{1,0:T(8,128)(2,1)S(1)}, u32[]{:S(2)}, u32[]{:S(2)}) %collective-permute-start.30) | collective-permute-done | bytes 1048608 | tf_op jit(solution)/shard_map/ppermute | solution.py:171
  248.7 9.2 %shard_map.233.raw_ref = f32[256,6144]{1,0:T(8,128)} custom-call(bf16[256,512]{1,0:T(8,128)(2,1)S(1)} %get-tuple-element.1764.left_ref, bf16[4,4,64,2048]{3,2,1,0:T(8,128)(2,1)} %bitcast.39.refs_0_.refs_6_, bf16[4,4,64,2048]{3,2,1,0:T(8,128)(2,1)} %collective-permute-done.33.refs_1_.refs_7_, f32[256,6144]{1,0:T(8,128)} %shard_map.232.refs_2_), custom_call_target="tpu_custom_call" | custom-call | flops 1 | bytes 1 | tf_op jit(solution)/shard_map/pallas_call | solution.py:381
  258.0 12.8 %shard_map.234 = (bf16[256,2048]{1,0:T(8,128)(2,1)S(1)}, bf16[256,2048]{1,0:T(8,128)(2,1)S(1)}, bf16[256,2048]{1,0:T(8,128)(2,1)S(1)}, bf16[256,2048]{1,0:T(8,12...) custom-call(f32[256,6144]{1,0:T(8,128)} %shard_map.233.raw_ref, ...), custom_call_target="tpu_custom_call" | custom-call | flops 1 | bytes 1 | tf_op jit(solution)/shard_map/pallas_call | solution.py:477
  304.4 12.2 %collective-permute-done.42 = bf16[128,2048]{1,0:T(8,128)(2,1)S(1)} collective-permute-done((bf16[128,2048]{1,0:T(8,128)(2,1)S(1)}, bf16[128,2048]{1,0:T(8,128)(2,1)S(1)}, u32[]{:S(2)}, u32[]{:S(2)}) %collective-permute-start.42) | collective-permute-done | bytes 524320 | tf_op jit(solution)/shard_map/ppermute | solution.py:171
  355.3 5.6 collective-permute-start.52
  364.9 5.8 fusion.13
  386.5 5.9 fusion.16
  414.2 14.6 %shard_map.236 = (bf16[128,2176]{1,0:T(8,128)(2,1)S(1)}, bf16[128,2176]{1,0:T(8,128)(2,1)S(1)}, bf16[128,2176]{1,0:T(8,128)(2,1)S(1)}, bf16[128,2176]{1,0:T(8,12...) custom-call(bf16[512,2048]{1,0:T(8,128)(2,1)} %get-tuple-element.1380.grad_y_ref.refs_7_, ...), custom_call_target="tpu_custom_call" | custom-call | flops 1 | bytes 1 | tf_op jit(solution)/shard_map/pallas_call | solution.py:616
  432.6 14.5 %shard_map.237 = (bf16[128,2176]{1,0:T(8,128)(2,1)S(1)}, bf16[128,2176]{1,0:T(8,128)(2,1)S(1)}, bf16[128,2176]{1,0:T(8,128)(2,1)S(1)}, bf16[128,2176]{1,0:T(8,12...) custom-call(bf16[512,2048]{1,0:T(8,128)(2,1)} %get-tuple-element.1379.grad_y_ref.refs_6_, ...), custom_call_target="tpu_custom_call" | custom-call | flops 1 | bytes 1 | tf_op jit(solution)/shard_map/pallas_call | solution.py:616
  447.7 14.5 %shard_map.238 = (bf16[128,2176]{1,0:T(8,128)(2,1)S(1)}, bf16[128,2176]{1,0:T(8,128)(2,1)S(1)}, bf16[128,2176]{1,0:T(8,128)(2,1)S(1)}, bf16[128,2176]{1,0:T(8,12...) custom-call(bf16[512,2048]{1,0:T(8,128)(2,1)} %get-tuple-element.1378.grad_y_ref.refs_5_, ...), custom_call_target="tpu_custom_call" | custom-call | flops 1 | bytes 1 | tf_op jit(solution)/shard_map/pallas_call | solution.py:616
  471.5 15.0 %shard_map.239 = (bf16[128,2176]{1,0:T(8,128)(2,1)S(1)}, bf16[128,2176]{1,0:T(8,128)(2,1)}, bf16[128,2176]{1,0:T(8,128)(2,1)}, bf16[128,2176]{1,0:T(8,128)(2,1)}...) custom-call(bf16[512,2048]{1,0:T(8,128)(2,1)} %get-tuple-element.1377.grad_y_ref.refs_4_, ...), custom_call_target="tpu_custom_call" | custom-call | flops 1 | bytes 1 | tf_op jit(solution)/shard_map/pallas_call | solution.py:616
  506.2 15.2 %shard_map.240 = f32[1024,2048]{1,0:T(8,128)} custom-call(bf16[512,1024]{1,0:T(8,128)(2,1)S(1)} %get-tuple-element.1373.refs_0_, bf16[512,1024]{1,0:T(8,128)(2,1)} %copy-done.146, bf16[512,1024]{1,0:T(8,128)(2,1)} %copy-done.147, bf16[512,1024]{1,0:T(8,128)(2,1)} %copy-done.148, bf16[512,2048]{1,0:T(8,128)(2,1)} %get-tuple-element.1377.grad_y_ref.refs_4_, ...), custom_call_target="tpu_custom_call" | custom-call | flops 1 | bytes 1 | tf_op jit(solution)/shard_map/pallas_call | solution.py:650
  544.9 5.7 collective-permute-done.74
  573.9 10.6 %collective-permute-start.82 = (bf16[256,2048]{1,0:T(8,128)(2,1)S(1)}, bf16[256,2048]{1,0:T(8,128)(2,1)S(1)}, u32[]{:S(2)}, u32[]{:S(2)}) collective-permute-start(bf16[256,2048]{1,0:T(8,128)(2,1)S(1)} %get-tuple-element.1452), channel_id=1, source_target_pairs={{0,16},{16,0},{1,17},{17,1},{2,18},{18,2},{3,19},{19,3},{4,20},{20... | collective-permute-start | bytes 3145736 | tf_op jit(solution)/shard_map/ppermute | solution.py:184
  589.0 18.9 %shard_map.242 = (bf16[3,256,2048]{2,1,0:T(8,128)(2,1)}, f32[8,2048]{1,0:T(8,128)S(1)}) custom-call(bf16[256,2048]{1,0:T(8,128)(2,1)S(1)} %fusion.27.grad_ref, bf16[256,2048]{1,0:T(8,128)(2,1)S(1)} %copy-done.30, bf16[256,2048]{1,0:T(8,128)(2,1)S(1)} %copy-done.32, bf16[256,2048]{1,0:T(8,128)(2,1)S(1)} %copy-done.34, f32[16,256,256]{2,1,0:T(8,128)S(1)} %copy-done.24, ...), custom_call_target="tpu_custom_call" | custom-call | flops 1 | bytes 1 | tf_op jit(solution)/shard_map/pallas_call | solution.py:554
  637.9 11.8 %shard_map.243.grad_ref = f32[256,2048]{1,0:T(8,128)S(1)} custom-call(bf16[3,256,2048]{2,1,0:T(8,128)(2,1)} %get-tuple-element.1566.left_ref, bf16[4,4,64,2048]{3,2,1,0:T(8,128)(2,1)S(1)} %bitcast.216, bf16[4,4,64,2048]{3,2,1,0:T(8,128)(2,1)S(1)} %copy-done.8, bf16[4,4,64,2048]{3,2,1,0:T(8,128)(2,1)} %bitcast.221, bf16[4,4,64,2048]{3,2,1,0:T(8,128)(2,1)} %copy-done.9, ...), custom_call_target="tpu_custom_call" | custom-call | flops 1 | bytes 1 | tf_op jit(solution)/shard_map/pallas_call | solution.py:415
  675.8 7.7 shard_map.245
  693.7 14.5 %collective-permute-done.92.refs_0_.came_x = bf16[768,1024]{1,0:T(8,128)(2,1)} collective-permute-done((bf16[768,1024]{1,0:T(8,128)(2,1)}, bf16[768,1024]{1,0:T(8,128)(2,1)}, u32[]{:S(2)}, u32[]{:S(2)}) %collective-permute-start.92) | collective-permute-done | bytes 1572896 | tf_op jit(solution)/shard_map/ppermute | solution.py:171
  722.3 13.9 %shard_map.248 = f32[2048,1024]{1,0:T(8,128)} custom-call(bf16[512,2048]{1,0:T(8,128)(2,1)} %copy-done.75, bf16[512,2048]{1,0:T(8,128)(2,1)} %copy-done.76, bf16[512,2048]{1,0:T(8,128)(2,1)} %copy-done.77, bf16[512,2048]{1,0:T(8,128)(2,1)} %copy-done.78, bf16[512,1024]{1,0:T(8,128)(2,1)S(1)} %copy-done.36, bf16[512,1024]{1,0:T(8,128)(2,1)} %get-tuple-element.1557.refs_5_, ...), custom_call_target="tpu_custom_call" | custom-call | flops 1 | bytes 1 | tf_op jit(solution)/shard_map/pallas_call | solution.py:650
  746.0 6.3 collective-permute-done.97.refs_1_.came_y
  775.4 13.5 %shard_map.251 = f32[2048,1024]{1,0:T(8,128)} custom-call(bf16[512,2048]{1,0:T(8,128)(2,1)} %copy-done.75, bf16[512,2048]{1,0:T(8,128)(2,1)} %copy-done.76, bf16[512,2048]{1,0:T(8,128)(2,1)} %copy-done.77, bf16[512,2048]{1,0:T(8,128)(2,1)} %copy-done.78, bf16[512,1024]{1,0:T(8,128)(2,1)S(1)} %copy-done.35, bf16[512,1024]{1,0:T(8,128)(2,1)} %get-tuple-element.1595.refs_5_, ...), custom_call_target="tpu_custom_call" | custom-call | flops 1 | bytes 1 | tf_op jit(solution)/shard_map/pallas_call | solution.py:650
  821.2 15.1 %collective-permute-done.109 = bf16[66,2048]{1,0:T(8,128)(2,1)S(1)} collective-permute-done((bf16[66,2048]{1,0:T(8,128)(2,1)S(1)}, bf16[66,2048]{1,0:T(8,128)(2,1)S(1)}, u32[]{:S(2)}, u32[]{:S(2)}) %collective-permute-start.109) | collective-permute-done | bytes 270368 | tf_op jit(solution)/shard_map/ppermute | solution.py:180
  852.3 14.9 %collective-permute-done.112 = bf16[64,2048]{1,0:T(8,128)(2,1)S(1)} collective-permute-done((bf16[64,2048]{1,0:T(8,128)(2,1)S(1)}, bf16[64,2048]{1,0:T(8,128)(2,1)S(1)}, u32[]{:S(2)}, u32[]{:S(2)}) %collective-permute-start.112) | collective-permute-done | bytes 262176 | tf_op jit(solution)/shard_map/ppermute | solution.py:180
  (940 shorter events, 512.3 us)
Async XLA Ops:
  46.8 31.6 %collective-permute-start.10 = (bf16[6,64,2048]{2,1,0:T(8,128)(2,1)}, bf16[6,64,2048]{2,1,0:T(8,128)(2,1)}, u32[]{:S(2)}, u32[]{:S(2)}) collective-permute-start(bf16[6,64,2048]{2,1,0:T(8,128)(2,1)} %get-tuple-element.864), channel_id=1, source_target_pairs={{0,1},{1,0},{2,3},{3,2},{4,5},{5,4},{6,7},{7,6},{8,9},{9,8},{10,11... | collective-permute-start | bytes 4718600 | tf_op jit(solution)/shard_map/ppermute | solution.py:171
  48.0 30.4 %collective-permute-start.11 = (bf16[6,64,2048]{2,1,0:T(8,128)(2,1)}, bf16[6,64,2048]{2,1,0:T(8,128)(2,1)}, u32[]{:S(2)}, u32[]{:S(2)}) collective-permute-start(bf16[6,64,2048]{2,1,0:T(8,128)(2,1)} %get-tuple-element.865), channel_id=1, source_target_pairs={{0,2},{1,3},{2,0},{3,1},{4,6},{5,7},{6,4},{7,5},{8,10},{9,11},{10,... | collective-permute-start | bytes 4718600 | tf_op jit(solution)/shard_map/ppermute | solution.py:171
  84.6 28.9 %collective-permute-start.15 = (bf16[6,64,2048]{2,1,0:T(8,128)(2,1)S(1)}, bf16[6,64,2048]{2,1,0:T(8,128)(2,1)S(1)}, u32[]{:S(2)}, u32[]{:S(2)}) collective-permute-start(bf16[6,64,2048]{2,1,0:T(8,128)(2,1)S(1)} %get-tuple-element.884), channel_id=1, source_target_pairs={{0,1},{1,0},{2,3},{3,2},{4,5},{5,4},{6,7},{7,6},{8,9},{9,8},{10,11... | collective-permute-start | bytes 4718600 | tf_op jit(solution)/shard_map/ppermute | solution.py:171
  85.9 29.2 %collective-permute-start.16 = (bf16[6,64,2048]{2,1,0:T(8,128)(2,1)S(1)}, bf16[6,64,2048]{2,1,0:T(8,128)(2,1)S(1)}, u32[]{:S(2)}, u32[]{:S(2)}) collective-permute-start(bf16[6,64,2048]{2,1,0:T(8,128)(2,1)S(1)} %get-tuple-element.885), channel_id=1, source_target_pairs={{0,2},{1,3},{2,0},{3,1},{4,6},{5,7},{6,4},{7,5},{8,10},{9,11},{10,... | collective-permute-start | bytes 4718600 | tf_op jit(solution)/shard_map/ppermute | solution.py:171
  199.0 35.4 %collective-permute-start.30 = (bf16[256,2048]{1,0:T(8,128)(2,1)}, bf16[256,2048]{1,0:T(8,128)(2,1)S(1)}, u32[]{:S(2)}, u32[]{:S(2)}) collective-permute-start(bf16[256,2048]{1,0:T(8,128)(2,1)} %pad_maximum_fusion.16), channel_id=1, source_target_pairs={{0,3},{1,2},{2,1},{3,0},{4,7},{5,6},{6,5},{7,4},{8,11},{9,10},{10,... | collective-permute-start | bytes 3145736 | tf_op jit(solution)/shard_map/ppermute | solution.py:171
  200.7 33.7 %collective-permute-start.31 = (bf16[256,2048]{1,0:T(8,128)(2,1)}, bf16[256,2048]{1,0:T(8,128)(2,1)S(1)}, u32[]{:S(2)}, u32[]{:S(2)}) collective-permute-start(bf16[256,2048]{1,0:T(8,128)(2,1)} %copy-done.149), channel_id=1, source_target_pairs={{4,0},{5,1},{6,2},{7,3},{8,12},{9,13},{10,14},{11,15},{20,16},{21,... | collective-permute-start | bytes 3145736 | tf_op jit(solution)/shard_map/ppermute | solution.py:180
  242.5 44.2 %collective-permute-start.37 = (bf16[256,1024]{1,0:T(8,128)(2,1)}, bf16[256,1024]{1,0:T(8,128)(2,1)S(1)}, u32[]{:S(2)}, u32[]{:S(2)}) collective-permute-start(bf16[256,1024]{1,0:T(8,128)(2,1)} %get-tuple-element.1000), channel_id=1, source_target_pairs={{0,16},{16,0},{1,17},{17,1},{2,18},{18,2},{3,19},{19,3},{4,20},{20... | collective-permute-start | bytes 1572872 | tf_op jit(solution)/shard_map/ppermute | solution.py:184
  242.6 44.2 %collective-permute-start.34 = (bf16[256,2048]{1,0:T(8,128)(2,1)}, bf16[256,2048]{1,0:T(8,128)(2,1)S(1)}, u32[]{:S(2)}, u32[]{:S(2)}) collective-permute-start(bf16[256,2048]{1,0:T(8,128)(2,1)} %pad_maximum_fusion.18), channel_id=1, source_target_pairs={{0,1},{1,0},{2,3},{3,2},{4,5},{5,4},{6,7},{7,6},{8,9},{9,8},{10,11... | collective-permute-start | bytes 3145736 | tf_op jit(solution)/shard_map/ppermute | solution.py:171
  243.2 43.6 %collective-permute-start.35 = (bf16[256,2048]{1,0:T(8,128)(2,1)S(1)}, bf16[256,2048]{1,0:T(8,128)(2,1)}, u32[]{:S(2)}, u32[]{:S(2)}) collective-permute-start(bf16[256,2048]{1,0:T(8,128)(2,1)S(1)} %copy-done.158), channel_id=1, source_target_pairs={{0,2},{1,3},{2,0},{3,1},{4,6},{5,7},{6,4},{7,5},{8,10},{9,11},{10,... | collective-permute-start | bytes 3145736 | tf_op jit(solution)/shard_map/ppermute | solution.py:171
  243.7 45.8 %collective-permute-start.36 = (bf16[256,2048]{1,0:T(8,128)(2,1)S(1)}, bf16[256,2048]{1,0:T(8,128)(2,1)S(1)}, u32[]{:S(2)}, u32[]{:S(2)}) collective-permute-start(bf16[256,2048]{1,0:T(8,128)(2,1)S(1)} %copy-done.157), channel_id=1, source_target_pairs={{0,3},{1,2},{2,1},{3,0},{4,7},{5,6},{6,5},{7,4},{8,11},{9,10},{10,... | collective-permute-start | bytes 3145736 | tf_op jit(solution)/shard_map/ppermute | solution.py:171
  430.4 31.7 %collective-permute-start.63 = (bf16[128,2176]{1,0:T(8,128)(2,1)}, bf16[128,2176]{1,0:T(8,128)(2,1)}, u32[]{:S(2)}, u32[]{:S(2)}) collective-permute-start(bf16[128,2176]{1,0:T(8,128)(2,1)} %get-tuple-element.1282), channel_id=1, source_target_pairs={{0,3},{1,2},{2,1},{3,0},{4,7},{5,6},{6,5},{7,4},{8,11},{9,10},{10,... | collective-permute-start | bytes 1671176 | tf_op jit(solution)/shard_map/ppermute | solution.py:171
  469.5 35.1 %collective-permute-start.73 = (bf16[128,2176]{1,0:T(8,128)(2,1)}, bf16[128,2176]{1,0:T(8,128)(2,1)}, u32[]{:S(2)}, u32[]{:S(2)}) collective-permute-start(bf16[128,2176]{1,0:T(8,128)(2,1)} %get-tuple-element.1398), channel_id=1, source_target_pairs={{0,3},{1,2},{2,1},{3,0},{4,7},{5,6},{6,5},{7,4},{8,11},{9,10},{10,... | collective-permute-start | bytes 1671176 | tf_op jit(solution)/shard_map/ppermute | solution.py:171
  531.3 37.0 %collective-permute-start.81 = (bf16[128,2048]{1,0:T(8,128)(2,1)}, bf16[128,2048]{1,0:T(8,128)(2,1)}, u32[]{:S(2)}, u32[]{:S(2)}) collective-permute-start(bf16[128,2048]{1,0:T(8,128)(2,1)} %get-tuple-element.1432), channel_id=1, source_target_pairs={{0,3},{1,2},{2,1},{3,0},{4,7},{5,6},{6,5},{7,4},{8,11},{9,10},{10,... | collective-permute-start | bytes 1572872 | tf_op jit(solution)/shard_map/ppermute | solution.py:171
  573.9 34.9 %collective-permute-start.82 = (bf16[256,2048]{1,0:T(8,128)(2,1)S(1)}, bf16[256,2048]{1,0:T(8,128)(2,1)S(1)}, u32[]{:S(2)}, u32[]{:S(2)}) collective-permute-start(bf16[256,2048]{1,0:T(8,128)(2,1)S(1)} %get-tuple-element.1452), channel_id=1, source_target_pairs={{0,16},{16,0},{1,17},{17,1},{2,18},{18,2},{3,19},{19,3},{4,20},{20... | collective-permute-start | bytes 3145736 | tf_op jit(solution)/shard_map/ppermute | solution.py:184
  584.5 29.9 %collective-permute-start.83 = (bf16[128,2048]{1,0:T(8,128)(2,1)}, bf16[128,2048]{1,0:T(8,128)(2,1)}, u32[]{:S(2)}, u32[]{:S(2)}) collective-permute-start(bf16[128,2048]{1,0:T(8,128)(2,1)} %get-tuple-element.1454), channel_id=1, source_target_pairs={{0,1},{1,0},{2,3},{3,2},{4,5},{5,4},{6,7},{7,6},{8,9},{9,8},{10,11... | collective-permute-start | bytes 1572872 | tf_op jit(solution)/shard_map/ppermute | solution.py:171
  585.7 28.7 %collective-permute-start.84 = (bf16[128,2048]{1,0:T(8,128)(2,1)}, bf16[128,2048]{1,0:T(8,128)(2,1)}, u32[]{:S(2)}, u32[]{:S(2)}) collective-permute-start(bf16[128,2048]{1,0:T(8,128)(2,1)} %get-tuple-element.1455), channel_id=1, source_target_pairs={{0,2},{1,3},{2,0},{3,1},{4,6},{5,7},{6,4},{7,5},{8,10},{9,11},{10,... | collective-permute-start | bytes 1572872 | tf_op jit(solution)/shard_map/ppermute | solution.py:171
  620.6 33.5 %collective-permute-start.87 = (bf16[512,1024]{1,0:T(8,128)(2,1)}, bf16[512,1024]{1,0:T(8,128)(2,1)S(1)}, u32[]{:S(2)}, u32[]{:S(2)}) collective-permute-start(bf16[512,1024]{1,0:T(8,128)(2,1)} %convolution_convert_fusion.20), channel_id=1, source_target_pairs={{0,1},{1,0},{2,3},{3,2},{4,5},{5,4},{6,7},{7,6},{8,9},{9,8},{10,11... | collective-permute-start | bytes 3145736 | tf_op jit(solution)/shard_map/ppermute | solution.py:171
  621.8 32.3 %collective-permute-start.88 = (bf16[512,1024]{1,0:T(8,128)(2,1)}, bf16[512,1024]{1,0:T(8,128)(2,1)S(1)}, u32[]{:S(2)}, u32[]{:S(2)}) collective-permute-start(bf16[512,1024]{1,0:T(8,128)(2,1)} %convolution_convert_fusion.19), channel_id=1, source_target_pairs={{0,2},{1,3},{2,0},{3,1},{4,6},{5,7},{6,4},{7,5},{8,10},{9,11},{10,... | collective-permute-start | bytes 3145736 | tf_op jit(solution)/shard_map/ppermute | solution.py:171
  623.0 31.1 %collective-permute-start.89 = (bf16[256,2048]{1,0:T(8,128)(2,1)}, bf16[256,2048]{1,0:T(8,128)(2,1)}, u32[]{:S(2)}, u32[]{:S(2)}) collective-permute-start(bf16[256,2048]{1,0:T(8,128)(2,1)} %add_convert_fusion.6), channel_id=1, source_target_pairs={{4,8},{5,9},{6,10},{7,11},{8,4},{9,5},{10,6},{11,7},{20,24},{21,25... | collective-permute-start | bytes 3145736 | tf_op jit(solution)/shard_map/ppermute | solution.py:180
  667.3 41.3 %collective-permute-start.94 = (bf16[256,2048]{1,0:T(8,128)(2,1)}, bf16[256,2048]{1,0:T(8,128)(2,1)}, u32[]{:S(2)}, u32[]{:S(2)}) collective-permute-start(bf16[256,2048]{1,0:T(8,128)(2,1)} %add_convert_fusion.5), channel_id=1, source_target_pairs={{0,4},{1,5},{2,6},{3,7},{4,0},{5,1},{6,2},{7,3},{8,12},{9,13},{10,... | collective-permute-start | bytes 3145736 | tf_op jit(solution)/shard_map/ppermute | solution.py:180
  670.5 38.2 %collective-permute-start.95 = (bf16[256,2048]{1,0:T(8,128)(2,1)}, bf16[256,2048]{1,0:T(8,128)(2,1)}, u32[]{:S(2)}, u32[]{:S(2)}) collective-permute-start(bf16[256,2048]{1,0:T(8,128)(2,1)} %add_convert_fusion.4), channel_id=1, source_target_pairs={{4,8},{5,9},{6,10},{7,11},{8,4},{9,5},{10,6},{11,7},{20,24},{21,25... | collective-permute-start | bytes 3145736 | tf_op jit(solution)/shard_map/ppermute | solution.py:180
  673.3 35.0 %collective-permute-start.92 = (bf16[768,1024]{1,0:T(8,128)(2,1)}, bf16[768,1024]{1,0:T(8,128)(2,1)}, u32[]{:S(2)}, u32[]{:S(2)}) collective-permute-start(bf16[768,1024]{1,0:T(8,128)(2,1)} %get-tuple-element.1515), channel_id=1, source_target_pairs={{0,1},{1,0},{2,3},{3,2},{4,5},{5,4},{6,7},{7,6},{8,9},{9,8},{10,11... | collective-permute-start | bytes 4718600 | tf_op jit(solution)/shard_map/ppermute | solution.py:171
  673.9 34.6 %collective-permute-start.93 = (bf16[768,1024]{1,0:T(8,128)(2,1)}, bf16[768,1024]{1,0:T(8,128)(2,1)}, u32[]{:S(2)}, u32[]{:S(2)}) collective-permute-start(bf16[768,1024]{1,0:T(8,128)(2,1)} %get-tuple-element.1516), channel_id=1, source_target_pairs={{0,2},{1,3},{2,0},{3,1},{4,6},{5,7},{6,4},{7,5},{8,10},{9,11},{10,... | collective-permute-start | bytes 4718600 | tf_op jit(solution)/shard_map/ppermute | solution.py:171
  718.1 35.8 %collective-permute-start.98 = (bf16[64,2048]{1,0:T(8,128)(2,1)S(1)}, bf16[64,2048]{1,0:T(8,128)(2,1)S(1)}, u32[]{:S(2)}, u32[]{:S(2)}) collective-permute-start(bf16[64,2048]{1,0:T(8,128)(2,1)S(1)} %get-tuple-element.1563), channel_id=1, source_target_pairs={{0,4},{1,5},{2,6},{3,7},{4,8},{5,9},{6,10},{7,11},{8,12},{9,13},{1... | collective-permute-start | bytes 786440 | tf_op jit(solution)/shard_map/ppermute | solution.py:180
  718.3 35.5 %collective-permute-start.99 = (bf16[64,2048]{1,0:T(8,128)(2,1)S(1)}, bf16[64,2048]{1,0:T(8,128)(2,1)}, u32[]{:S(2)}, u32[]{:S(2)}) collective-permute-start(bf16[64,2048]{1,0:T(8,128)(2,1)S(1)} %get-tuple-element.1564), channel_id=1, source_target_pairs={{0,8},{1,9},{2,10},{3,11},{4,12},{5,13},{6,14},{7,15},{8,0},{9,1},... | collective-permute-start | bytes 786440 | tf_op jit(solution)/shard_map/ppermute | solution.py:180
  719.2 35.4 %collective-permute-start.100 = (bf16[64,2048]{1,0:T(8,128)(2,1)S(1)}, bf16[64,2048]{1,0:T(8,128)(2,1)}, u32[]{:S(2)}, u32[]{:S(2)}) collective-permute-start(bf16[64,2048]{1,0:T(8,128)(2,1)S(1)} %get-tuple-element.1565), channel_id=1, source_target_pairs={{0,12},{1,13},{2,14},{3,15},{4,0},{5,1},{6,2},{7,3},{8,4},{9,5},{1... | collective-permute-start | bytes 786440 | tf_op jit(solution)/shard_map/ppermute | solution.py:180
  719.8 32.5 %collective-permute-start.97 = (bf16[768,1024]{1,0:T(8,128)(2,1)S(1)}, bf16[768,1024]{1,0:T(8,128)(2,1)S(1)}, u32[]{:S(2)}, u32[]{:S(2)}) collective-permute-start(bf16[768,1024]{1,0:T(8,128)(2,1)S(1)} %get-tuple-element.1551), channel_id=1, source_target_pairs={{0,2},{1,3},{2,0},{3,1},{4,6},{5,7},{6,4},{7,5},{8,10},{9,11},{10,... | collective-permute-start | bytes 4718600 | tf_op jit(solution)/shard_map/ppermute | solution.py:171
  720.1 33.8 %collective-permute-start.96 = (bf16[800,1024]{1,0:T(8,128)(2,1)S(1)}, bf16[800,1024]{1,0:T(8,128)(2,1)S(1)}, u32[]{:S(2)}, u32[]{:S(2)}) collective-permute-start(bf16[800,1024]{1,0:T(8,128)(2,1)S(1)} %get-tuple-element.1550), channel_id=1, source_target_pairs={{0,1},{1,0},{2,3},{3,2},{4,5},{5,4},{6,7},{7,6},{8,9},{9,8},{10,11... | collective-permute-start | bytes 4915208 | tf_op jit(solution)/shard_map/ppermute | solution.py:171
  766.3 33.3 %collective-permute-start.102 = (bf16[784,1024]{1,0:T(8,128)(2,1)S(1)}, bf16[784,1024]{1,0:T(8,128)(2,1)S(1)}, u32[]{:S(2)}, u32[]{:S(2)}) collective-permute-start(bf16[784,1024]{1,0:T(8,128)(2,1)S(1)} %get-tuple-element.1588), channel_id=1, source_target_pairs={{0,2},{1,3},{2,0},{3,1},{4,6},{5,7},{6,4},{7,5},{8,10},{9,11},{10,... | collective-permute-start | bytes 4816904 | tf_op jit(solution)/shard_map/ppermute | solution.py:171
  767.3 31.1 %collective-permute-start.101 = (bf16[768,1024]{1,0:T(8,128)(2,1)S(1)}, bf16[768,1024]{1,0:T(8,128)(2,1)S(1)}, u32[]{:S(2)}, u32[]{:S(2)}) collective-permute-start(bf16[768,1024]{1,0:T(8,128)(2,1)S(1)} %get-tuple-element.1587), channel_id=1, source_target_pairs={{0,1},{1,0},{2,3},{3,2},{4,5},{5,4},{6,7},{7,6},{8,9},{9,8},{10,11... | collective-permute-start | bytes 4718600 | tf_op jit(solution)/shard_map/ppermute | solution.py:171
  810.2 29.6 %collective-permute-start.106 = (bf16[256,1024]{1,0:T(8,128)(2,1)S(1)}, bf16[256,1024]{1,0:T(8,128)(2,1)S(1)}, u32[]{:S(2)}, u32[]{:S(2)}) collective-permute-start(bf16[256,1024]{1,0:T(8,128)(2,1)S(1)} %get-tuple-element.1624), channel_id=1, source_target_pairs={{0,1},{1,0},{2,3},{3,2},{4,5},{5,4},{6,7},{7,6},{8,9},{9,8},{10,11... | collective-permute-start | bytes 1572872 | tf_op jit(solution)/shard_map/ppermute | solution.py:171
  811.2 28.7 %collective-permute-start.107 = (bf16[256,1024]{1,0:T(8,128)(2,1)S(1)}, bf16[256,1024]{1,0:T(8,128)(2,1)S(1)}, u32[]{:S(2)}, u32[]{:S(2)}) collective-permute-start(bf16[256,1024]{1,0:T(8,128)(2,1)S(1)} %get-tuple-element.1625), channel_id=1, source_target_pairs={{0,2},{1,3},{2,0},{3,1},{4,6},{5,7},{6,4},{7,5},{8,10},{9,11},{10,... | collective-permute-start | bytes 1572872 | tf_op jit(solution)/shard_map/ppermute | solution.py:171
  (301 other events, 3841.4 us)
